TPU v7x, 32 devices: a whole 2x2x4 slice. The times are simulated.
32 devices in a mesh: fsdp: 16 (over z, y, core), rep: 2 (over x).
Axes of the slice: x: 2, y: 2, z: 4, core: 2. Of those that a mesh axis runs over, the one named last changes fastest.
Arguments:
- block_input: bfloat16 [64, 128, 768], P(('fsdp', 'rep')), may hold values from -6 to 6
- span_lengths: int32 [64], P(('fsdp', 'rep')), may hold values from 32 to 128, as said below
- mlm_positions: int32 [64, 32], P(('fsdp', 'rep')), may hold values from 0 to 127, as said below
- mlm_labels: int32 [64, 32], P(('fsdp', 'rep')), may hold values from 0 to 30521
- span_pairs: int32 [64], P(('fsdp', 'rep')), may hold values from 0 to 63, as said below
- layer_mats: float32 [7077888], P(('fsdp', 'rep'))
- vectors: float32 [9216], P(('fsdp', 'rep'))
- embedding: float32 [23440896], P(('fsdp', 'rep'))
- mom1_mats: float32 [7077888], P(('fsdp', 'rep')), may hold values from -6 to 6
- mom2_mats: float32 [7077888], P(('fsdp', 'rep')), may hold values from 0.01 to 10
- mom1_vecs: float32 [9216], P(('fsdp', 'rep')), may hold values from -6 to 6
- mom2_vecs: float32 [9216], P(('fsdp', 'rep')), may hold values from 0.01 to 10
- mom1_embed: float32 [23440896], P(('fsdp', 'rep')), may hold values from -6 to 6
- mom2_embed: float32 [23440896], P(('fsdp', 'rep')), may hold values from 0.01 to 10
Outputs:
- grad_input: float32 [64, 128, 768], P(('fsdp', 'rep'))
- grad_mats: float32 [7077888], P(('fsdp', 'rep'))
- grad_vecs: float32 [9216], P(('fsdp', 'rep'))
- grad_embed: float32 [23440896], P(('fsdp', 'rep'))
- step_mats: float32 [7077888], P(('fsdp', 'rep'))
- step_vecs: float32 [9216], P(('fsdp', 'rep'))
- step_embed: float32 [23440896], P(('fsdp', 'rep'))
Inputs may be any that keep to these rules, and one draw needn't show every extreme that they name: `span_lengths`: A sequence's real tokens come first, padding after; some sequence has exactly 128 and some exactly 32 real tokens. `mlm_positions`: every slot's position lies below its sequence's span length; positions may repeat within a sequence; slot j of sequence s is used when j < span_lengths[s] // 4. span_pairs[span_pairs[s]] = s and span_pairs[s] != s for every s.
All inputs are finite; a program needn't handle non-finite values.
Results may differ from a plain program's by a relative error of at most 0.012.
The roundings to bfloat16 on the way count: a program that leaves them out, or rounds other values in their place, can miss the bound.
Values may be sent and summed in bfloat16 or wider, within the bound.
No kernel may reach another device: no remote copies, remote signals or barrier semaphores. Data moves between devices by JAX's collectives and lax.ppermute only.
A program may use at most 512 MiB of HBM per device.

v0:
```python
import math

import jax
import jax.numpy as jnp
from jax import lax
from jax.sharding import PartitionSpec as P

D = 768
FF = 3072
HEAD_DIM = 64
VOCAB = 30522
ADAM_STEP = 10


norm_eps = 1e-12
beta_one = 0.9
beta_two = 0.999
adam_eps = 1e-06
decay_rate = 0.01


def split_mats(flat):
    first = 3 * D * D
    second = first + D * D
    third = second + D * FF
    return (
        flat[:first].reshape(D, 3 * D),
        flat[first:second].reshape(D, D),
        flat[second:third].reshape(D, FF),
        flat[third:].reshape(FF, D),
    )


def split_vecs(flat):
    widths_list = [D, D, D, D, D, FF, D, D, D]
    pieces = []
    offset = 0
    for piece_width in widths_list:
        pieces.append(flat[offset : offset + piece_width].astype(jnp.float32))
        offset = offset + piece_width
    return pieces


def center_scale(resid):
    center = resid - jnp.mean(resid, axis=-1, keepdims=True)
    inverse = lax.rsqrt(jnp.mean(center * center, axis=-1, keepdims=True) + norm_eps)
    return (center * inverse, inverse)


def norm_back(d_normed, normed, inverse):
    return inverse * (
        d_normed
        - jnp.mean(d_normed, axis=-1, keepdims=True)
        - normed * jnp.mean(d_normed * normed, axis=-1, keepdims=True)
    )


def gelu_slope(value):
    return (
        0.5 * (1.0 + lax.erf(value * 0.7071067811865476))
        + value * jnp.exp(-0.5 * value * value) * 0.3989422804014327
    )


def contract_rows(left, right):
    return lax.dot_general(
        left, right, (((0,), (0,)), ((), ())), preferred_element_type=jnp.float32
    )


def contract_cols(left, right):
    return lax.dot_general(
        left, right, (((1,), (1,)), ((), ())), preferred_element_type=jnp.float32
    )


def adam_step(weight, grad, first, second, step_float, decay):
    first_new = beta_one * first + (1.0 - beta_one) * grad
    second_new = beta_two * second + (1.0 - beta_two) * grad * grad
    first_hat = first_new / (1.0 - beta_one**step_float)
    second_hat = second_new / (1.0 - beta_two**step_float)
    return first_hat / (jnp.sqrt(second_hat) + adam_eps) + decay * weight


def embed_reduce(d_logits, picked):
    block = contract_rows(d_logits, picked).reshape(-1)
    return lax.psum_scatter(block, ("fsdp", "rep"), scatter_dimension=0, tiled=True)


def on_device(
    block_input,
    span_lengths,
    mlm_positions,
    mlm_labels,
    span_pairs,
    layer_mats,
    vectors,
    embedding,
    mom1_mats,
    mom2_mats,
    mom1_vecs,
    mom2_vecs,
    mom1_embed,
    mom2_embed,
):
    seq_here, length, width = block_input.shape
    rows_here = seq_here * length
    heads_count = width // HEAD_DIM
    head_scale = HEAD_DIM ** (-0.5)
    mats_low = layer_mats.astype(jnp.bfloat16)
    vecs_low = vectors.astype(jnp.bfloat16)
    embed_low = embedding.astype(jnp.bfloat16)
    mats_all, vecs_all, embed_all = (
        lax.all_gather(mats_low, ("fsdp", "rep"), axis=0, tiled=True),
        lax.all_gather(vecs_low, ("fsdp", "rep"), axis=0, tiled=True),
        lax.all_gather(embed_low, ("fsdp", "rep"), axis=0, tiled=True),
    )
    w_qkv, w_out, w_up, w_down = split_mats(mats_all)
    bias_q, bias_v, bias_out, gain_one, shift_one, bias_up, bias_down, gain_two, shift_two = (
        split_vecs(vecs_all)
    )
    table = embed_all.reshape(VOCAB, width)
    valid = jnp.arange(length)[None, :] < span_lengths[:, None]
    valid_col = valid.reshape(rows_here, 1).astype(jnp.float32)
    tok_rows = (block_input * valid[:, :, None].astype(jnp.bfloat16)).reshape(rows_here, width)
    qkv_bias = jnp.concatenate([bias_q, jnp.zeros((width,), jnp.float32), bias_v])
    projected = (jnp.dot(tok_rows, w_qkv, preferred_element_type=jnp.float32) + qkv_bias).astype(
        jnp.bfloat16
    )
    shaped = projected.reshape(seq_here, length, 3, heads_count, HEAD_DIM)
    queries = shaped[:, :, 0]
    key_rows = shaped[:, :, 1]
    value_rows = shaped[:, :, 2]
    key_valid = valid[:, None, None, :]

    def make_scores():
        raw = (
            jnp.einsum("sqhd,skhd->shqk", queries, key_rows, preferred_element_type=jnp.float32)
            * head_scale
        )
        return jnp.where(key_valid, raw, -1e30)

    scores = make_scores()
    row_max = jnp.max(scores, axis=-1, keepdims=True)
    expo_vals = jnp.exp(scores - row_max)
    row_sum = jnp.sum(expo_vals, axis=-1, keepdims=True)
    row_lse = row_max + jnp.log(row_sum)
    attn_probs = (expo_vals / row_sum).astype(jnp.bfloat16)
    attended = (
        jnp.einsum("shqk,skhd->sqhd", attn_probs, value_rows, preferred_element_type=jnp.float32)
        .reshape(rows_here, width)
        .astype(jnp.bfloat16)
    )
    branch = jnp.dot(attended, w_out, preferred_element_type=jnp.float32) + bias_out
    normed_one, inverse_one = center_scale(tok_rows.astype(jnp.float32) + branch)
    hidden_one = normed_one * gain_one + shift_one
    hidden_low = hidden_one.astype(jnp.bfloat16)
    pre_act = jnp.dot(hidden_low, w_up, preferred_element_type=jnp.float32) + bias_up
    act_low = jax.nn.gelu(pre_act, approximate=False).astype(jnp.bfloat16)
    ffn_out = jnp.dot(act_low, w_down, preferred_element_type=jnp.float32) + bias_down
    normed_two, inverse_two = center_scale(hidden_one + ffn_out)
    output = (normed_two * gain_two + shift_two) * valid_col
    output_seq = output.reshape(seq_here, length, width)
    picked = (
        jnp.take_along_axis(output_seq, mlm_positions[:, :, None], axis=1)
        .reshape(-1, width)
        .astype(jnp.bfloat16)
    )
    logits = contract_cols(picked, table)
    logit_max = jnp.max(logits, axis=-1, keepdims=True)
    logit_exp = jnp.exp(logits - logit_max)
    logit_probs = logit_exp / jnp.sum(logit_exp, axis=-1, keepdims=True)
    slots = mlm_positions.shape[1]
    used = (
        (jnp.arange(slots)[None, :] < (span_lengths // 4)[:, None])
        .reshape(-1, 1)
        .astype(jnp.float32)
    )
    label_hot = (mlm_labels.reshape(-1, 1) == jnp.arange(VOCAB)[None, :]).astype(jnp.float32)
    d_logits = ((logit_probs - label_hot) * used).astype(jnp.bfloat16)
    d_picked = jnp.dot(d_logits, table, preferred_element_type=jnp.float32)
    select = (mlm_positions[:, :, None] == jnp.arange(length)[None, None, :]).astype(jnp.float32)
    d_output_seq = jnp.einsum(
        "gor,gon->grn",
        select,
        d_picked.reshape(seq_here, slots, width),
        precision=lax.Precision.HIGHEST,
    )
    cls_low = output_seq[:, 0, :].astype(jnp.bfloat16)
    cls_all = lax.all_gather(cls_low, ("fsdp", "rep"), axis=0, tiled=True)
    span_scale = 2.0 / math.sqrt(width)
    sims = contract_cols(cls_low, cls_all) * span_scale
    mine = lax.axis_index(("fsdp", "rep")) * seq_here + jnp.arange(seq_here)
    columns = jnp.arange(cls_all.shape[0])
    sims = jnp.where(columns[None, :] == mine[:, None], -1e30, sims)
    sims_probs = jax.nn.softmax(sims, axis=-1)
    partner_hot = (columns[None, :] == span_pairs[:, None]).astype(jnp.float32)
    d_sims = (sims_probs - partner_hot).astype(jnp.bfloat16)
    d_cls = jnp.dot(d_sims, cls_all, preferred_element_type=jnp.float32) * span_scale
    d_cls_terms = contract_rows(d_sims, cls_low) * span_scale
    d_cls = d_cls + lax.psum_scatter(d_cls_terms, ("fsdp", "rep"), scatter_dimension=0, tiled=True)
    d_output_seq = d_output_seq.at[:, 0, :].add(d_cls)
    d_output = d_output_seq.reshape(rows_here, width) * valid_col
    mats_back, vecs_back = (
        lax.all_gather(mats_low, ("fsdp", "rep"), axis=0, tiled=True),
        lax.all_gather(vecs_low, ("fsdp", "rep"), axis=0, tiled=True),
    )
    w_qkv, w_out, w_up, w_down = split_mats(mats_back)
    bias_q, bias_v, bias_out, gain_one, shift_one, bias_up, bias_down, gain_two, shift_two = (
        split_vecs(vecs_back)
    )
    d_gain_two = jnp.sum(d_output * normed_two, axis=0)
    d_shift_two = jnp.sum(d_output, axis=0)
    d_resid_two = norm_back(d_output * gain_two, normed_two, inverse_two)
    d_ffn = d_resid_two.astype(jnp.bfloat16)
    d_bias_down = jnp.sum(d_ffn.astype(jnp.float32), axis=0)
    d_w_down = contract_rows(act_low, d_ffn)
    d_act = contract_cols(d_ffn, w_down)
    d_pre = (d_act * gelu_slope(pre_act)).astype(jnp.bfloat16)
    d_bias_up = jnp.sum(d_pre.astype(jnp.float32), axis=0)
    d_w_up = contract_rows(hidden_low, d_pre)
    d_hidden = contract_cols(d_pre, w_up) + d_resid_two
    d_gain_one = jnp.sum(d_hidden * normed_one, axis=0)
    d_shift_one = jnp.sum(d_hidden, axis=0)
    d_resid_one = norm_back(d_hidden * gain_one, normed_one, inverse_one)
    d_branch = d_resid_one.astype(jnp.bfloat16)
    d_bias_out = jnp.sum(d_branch.astype(jnp.float32), axis=0)
    d_w_out = contract_rows(attended, d_branch)
    d_attended = (
        contract_cols(d_branch, w_out)
        .astype(jnp.bfloat16)
        .reshape(seq_here, length, heads_count, HEAD_DIM)
    )
    probs_again = jnp.exp(make_scores() - row_lse)
    probs_low = probs_again.astype(jnp.bfloat16)
    d_probs = jnp.einsum(
        "sqhd,skhd->shqk", d_attended, value_rows, preferred_element_type=jnp.float32
    )
    d_values = jnp.einsum(
        "shqk,sqhd->skhd", probs_low, d_attended, preferred_element_type=jnp.float32
    )
    row_delta = jnp.sum(d_probs * probs_again, axis=-1, keepdims=True)
    d_scores = (probs_again * (d_probs - row_delta)).astype(jnp.bfloat16)
    d_queries = (
        jnp.einsum("shqk,skhd->sqhd", d_scores, key_rows, preferred_element_type=jnp.float32)
        * head_scale
    )
    d_keys = (
        jnp.einsum("shqk,sqhd->skhd", d_scores, queries, preferred_element_type=jnp.float32)
        * head_scale
    )
    d_qkv = jnp.concatenate(
        [
            d_queries.reshape(rows_here, width),
            d_keys.reshape(rows_here, width),
            d_values.reshape(rows_here, width),
        ],
        axis=1,
    ).astype(jnp.bfloat16)
    d_qkv_float = d_qkv.astype(jnp.float32)
    d_bias_q = jnp.sum(d_qkv_float[:, :width], axis=0)
    d_bias_v = jnp.sum(d_qkv_float[:, 2 * width :], axis=0)
    d_w_qkv = contract_rows(tok_rows, d_qkv)
    grad_input = ((contract_cols(d_qkv, w_qkv) + d_resid_one) * valid_col).reshape(
        seq_here, length, width
    )
    d_mats = jnp.concatenate(
        [d_w_qkv.reshape(-1), d_w_out.reshape(-1), d_w_up.reshape(-1), d_w_down.reshape(-1)]
    )
    d_vecs = jnp.concatenate(
        [
            d_bias_q,
            d_bias_v,
            d_bias_out,
            d_gain_one,
            d_shift_one,
            d_bias_up,
            d_bias_down,
            d_gain_two,
            d_shift_two,
        ]
    )
    grad_mats, grad_vecs = (
        lax.psum_scatter(d_mats, ("fsdp", "rep"), scatter_dimension=0, tiled=True),
        lax.psum_scatter(d_vecs, ("fsdp", "rep"), scatter_dimension=0, tiled=True),
    )
    grad_embed = embed_reduce(d_logits, picked)
    step_float = float(ADAM_STEP)
    step_mats = adam_step(layer_mats, grad_mats, mom1_mats, mom2_mats, step_float, decay_rate)
    step_vecs = adam_step(vectors, grad_vecs, mom1_vecs, mom2_vecs, step_float, 0.0)
    step_embed = adam_step(embedding, grad_embed, mom1_embed, mom2_embed, step_float, decay_rate)
    return (grad_input, grad_mats, grad_vecs, grad_embed, step_mats, step_vecs, step_embed)


def solution(mesh):
    placed = (
        P(("fsdp", "rep"), None, None),
        P(("fsdp", "rep")),
        P(("fsdp", "rep"), None),
        P(("fsdp", "rep"), None),
        P(("fsdp", "rep")),
        P(("fsdp", "rep")),
        P(("fsdp", "rep")),
        P(("fsdp", "rep")),
        P(("fsdp", "rep")),
        P(("fsdp", "rep")),
        P(("fsdp", "rep")),
        P(("fsdp", "rep")),
        P(("fsdp", "rep")),
        P(("fsdp", "rep")),
    )
    return jax.shard_map(
        on_device,
        mesh=mesh,
        in_specs=placed,
        out_specs=(
            P(("fsdp", "rep"), None, None),
            P(("fsdp", "rep")),
            P(("fsdp", "rep")),
            P(("fsdp", "rep")),
            P(("fsdp", "rep")),
            P(("fsdp", "rep")),
            P(("fsdp", "rep")),
        ),
        check_vma=False,
    )
```

profile of v0, /device:TPU:0, one launch (start us, length us, event | category | flops | bytes accessed | tf_op | source)
XLA Modules:
  0.0 3019.5 jit_solution(1283670812512029057)
XLA Ops:
  7.2 2.0 convert_element_type.181
  9.2 15.0 broadcast.246
  24.2 22.8 dynamic-update-slice.4
  47.1 1.1 copy-done.10
  48.1 0.8 convert_element_type.158
  50.4 0.7 reshape.365
  51.3 44.1 %all-reduce = bf16[9216]{0:T(1024)(128)(2,1)S(1)} all-reduce(bf16[9216]{0:T(1024)(128)(2,1)S(1)} %dynamic-update-slice.3), channel_id=1, replica_groups=mesh['fsdp'=16,'rep'=2] {'fsdp','rep'}, use_global_device_ids=true, to_apply=%add | all-reduce | flops 9216 | bytes 36864
  97.3 0.7 fusion.80
  98.5 0.8 broadcast_multiply_fusion
  99.4 629.0 %all-reduce.11.cloned.1.call-done = bf16[23440896]{0:T(1024)(128)(2,1)} async-done(((bf16[23440896]{0:T(1024)(128)(2,1)}), bf16[23440896]{0:T(1024)(128)(2,1)}) %all-reduce.11.cloned.1.call-update) | async-done | bytes 46881808
  728.4 79.6 %reshape.383 = bf16[30522,768,1]{1,0,2:T(8,128)(2,1)} reshape(bf16[23440896]{0:T(1024)(128)(2,1)} %all-reduce.11.cloned.1.call-done) | data formatting | bytes 93763584 | tf_op jit(solution)/shard_map/reshape | solution.py:122
  808.0 79.4 %reshape.351 = bf16[30522,768]{1,0:T(8,128)(2,1)} reshape(bf16[23440896]{0:T(1024)(128)(2,1)} %all-reduce.11.cloned.1.call-done) | data formatting | bytes 93763584 | tf_op jit(solution)/shard_map/reshape | solution.py:122
  887.4 1.3 slice-done
  888.7 1.9 slice.134
  890.5 2.0 slice-done.1
  892.5 5.2 slice.127
  897.7 8.4 fusion.86
  906.1 9.4 slice.142
  915.5 3.1 fusion.2
  918.6 1.6 copy.45
  920.5 1.5 fusion.87
  925.4 8.3 slice.139
  933.7 11.1 fusion.5
  944.9 1.5 fusion.90
  947.0 1.0 gather_fusion
  948.1 66.7 %all-gather = bf16[64,1,768]{2,1,0:T(2,128)(2,1)S(1)} all-gather(bf16[2,1,768]{2,1,0:T(2,128)(2,1)S(1)} %slice.185), channel_id=2, replica_groups=mesh['fsdp'=16,'rep'=2] {'fsdp','rep'}, dimensions={0}, use_global_device_ids=true | all-gather | bytes 101376 | tf_op jit(solution)/shard_map/all_gather | solution.py:190
  1015.3 1.0 convolution_multiply_fusion.3
  1016.3 24.7 fusion.91
  1041.1 4.6 fusion
  1045.6 0.9 copy-done
  1046.5 3.7 multiply_convert_fusion
  1050.3 18.7 fusion.93
  1069.6 33.6 %fusion.54 = f32[30522,768]{1,0:T(8,128)} fusion(bf16[64,30522]{1,0:T(8,128)(2,1)} %multiply_convert_fusion, bf16[64,768]{1,0:T(8,128)(2,1)S(1)} %gather_fusion, pred[64]{0:T(512)(128)(4,1)S(1)} %copy-done.59), kind=kOutput, calls=%fused_computation.122 | convolution fusion | flops 3000483840 | bytes 97768768 | tf_op jit(solution)/shard_map/dot_general | solution.py:66
  1103.2 95.8 %reshape.363 = f32[23440896]{0:T(1024)} reshape(f32[30522,768]{1,0:T(8,128)} %fusion.54) | data formatting | bytes 187527168 | tf_op jit(solution)/shard_map/reshape | solution.py:86
  1199.0 0.9 fusion.34
  1200.1 0.9 multiply_reduce_fusion.1
  1201.0 0.8 multiply_reduce_fusion.8
  1201.8 0.9 convert_reduce_fusion.1
  1202.7 7.3 convert_reduce_fusion
  1210.0 2.2 multiply_reduce_fusion.2
  1212.3 0.9 convert_reduce_fusion.2
  1214.0 0.6 fusion.32
  1215.7 0.6 fusion.29
  1216.7 1.9 fusion.46
  1218.7 5.2 convolution_bitcast_fusion
  1223.9 5.1 fusion.76
  1229.0 1.2 copy.59
  1230.5 1.2 copy.56
  1231.7 0.8 bitcast_dynamic-update-slice_fusion.2
  1232.5 2.4 reshape.360
  1234.9 1.8 bitcast_dynamic-update-slice_fusion.1
  1236.7 1.8 bitcast_dynamic-update-slice_fusion
  1238.5 5.4 fusion.94
  1243.9 8.1 reshape.359
  1252.0 9.5 copy.73
  1261.5 10.7 reshape.362
  1272.2 30.0 pad_maximum_fusion
  1302.3 1.1 copy-done.6
  1304.1 39.6 %all-reduce.4 = f32[9216]{0:T(1024)S(1)} all-reduce(f32[9216]{0:T(1024)S(1)} %constant_dynamic-update-slice_fusion.3), channel_id=5, replica_groups=mesh['fsdp'=16,'rep'=2] {'fsdp','rep'}, use_global_device_ids=true, to_apply=%region_26.27.clone | all-reduce | flops 9216 | bytes 73728
  1343.8 0.7 multiply_add_fusion.1
  1344.4 4.1 fusion.25
  1348.6 1651.8 %all-reduce.15.cloned.1.call-done = (f32[7077888]{0:T(1024)}, f32[23440896]{0:T(1024)}) async-done(((f32[7077888]{0:T(1024)}, f32[23440896]{0:T(1024)}), (f32[7077888]{0:T(1024)}, f32[23440896]{0:T(1024)})) %all-reduce.15.cloned.1.call-update) | async-done | bytes 122075152
  3000.3 3.7 fusion.41
  3004.0 8.5 fusion.22
  (215 shorter events, 12.8 us)
Async XLA Ops:
  7.2 721.2 %all-reduce.11.cloned.1.call-start = ((), (), s32[]{:S(2)}) async-start(), calls=%async_computation.1 | async-start | bytes 93765632
  47.0 2.1 copy-start.51
  47.0 2.7 copy-start.67
  47.0 3.3 copy-start.65
  47.0 4.1 copy-start.48
  47.0 51.6 %copy-start.27 = (bf16[2,128,768]{2,1,0:T(8,128)(2,1)S(1)}, bf16[2,128,768]{2,1,0:T(8,128)(2,1)}, u32[]{:S(2)}) copy-start(bf16[2,128,768]{2,1,0:T(8,128)(2,1)} %param.16) | copy-start | bytes 1179652
  47.0 840.4 %all-gather.3.cloned.1.call-start = ((), (), s32[]{:S(2)}) async-start(), calls=%async_computation | async-start | bytes 14598144 | tf_op jit(solution)/shard_map/all_gather | solution.py:114
  48.9 1150.1 %all-reduce.13.cloned.1.call-start = ((), (), s32[]{:S(2)}) async-start(), calls=%async_computation.2 | async-start | bytes 393216
  96.7 848.2 %copy-start.28 = (f32[768]{0:T(1024)}, f32[768]{0:T(1024)S(1)}, u32[]{:S(2)}) copy-start(f32[768]{0:T(1024)S(1)} %get-tuple-element.49) | copy-start | bytes 9220
  96.7 848.2 %copy-start.31 = (f32[768]{0:T(1024)}, f32[768]{0:T(1024)S(1)}, u32[]{:S(2)}) copy-start(f32[768]{0:T(1024)S(1)} %get-tuple-element.48) | copy-start | bytes 9220
  96.7 850.1 %copy-start.33 = (f32[768]{0:T(1024)}, f32[768]{0:T(1024)S(1)}, u32[]{:S(2)}) copy-start(f32[768]{0:T(1024)S(1)} %get-tuple-element.46) | copy-start | bytes 9220
  890.5 2.0 slice-start.1
  906.1 9.4 copy-start.9
  918.6 3.4 copy-start.66
  922.9 1.6 copy-start.15
  924.1 9.5 copy-start.21
  925.1 287.2 %copy-start.4 = (f32[256,768]{1,0:T(8,128)}, f32[256,768]{1,0:T(8,128)S(1)}, u32[]{:S(2)}) copy-start(f32[256,768]{1,0:T(8,128)S(1)} %get-tuple-element.61) | copy-start | bytes 2359300
  925.1 287.2 %copy-start.35 = (f32[256]{0:T(256)}, f32[256]{0:T(256)S(1)}, u32[]{:S(2)}) copy-start(f32[256]{0:T(256)S(1)} %broadcast_multiply_fusion.5) | copy-start | bytes 3076
  925.4 286.9 %copy-start.44 = (f32[256]{0:T(256)}, f32[256]{0:T(256)S(1)}, u32[]{:S(2)}) copy-start(f32[256]{0:T(256)S(1)} %add_rsqrt_fusion.1) | copy-start | bytes 3076
  925.4 8.3 copy-start.47
  925.4 19.5 slice-start.2
  933.7 11.2 slice-start.3
  933.7 11.2 copy-start.53
  944.9 1.8 copy-start.37
  944.9 1.8 copy-start.42
  944.9 3.1 copy-start.64
  946.5 68.3 %copy-start.68 = (s32[2]{0:T(128)S(1)}, s32[2]{0:T(128)}, u32[]{:S(2)}) copy-start(s32[2]{0:T(128)} %iota_add_fusion) | copy-start | bytes 28
  946.5 68.8 %copy-start.60 = (s32[2]{0:T(128)S(1)}, s32[2]{0:T(128)}, u32[]{:S(2)}) copy-start(s32[2]{0:T(128)} %param.20) | copy-start | bytes 28
  1016.3 1984.1 %all-reduce.15.cloned.1.call-start = ((), (), s32[]{:S(2)}) async-start(), calls=%async_computation.3 | async-start | bytes 244154368
  1041.0 5.5 copy-start
  1041.0 5.5 copy-start.61
  1041.0 5.5 copy-start.62
  1050.3 18.7 copy-start.52
  1050.3 19.3 copy-start.59
  1103.2 96.9 %copy-start.34 = (f32[768]{0:T(1024)S(1)}, f32[768]{0:T(1024)}, u32[]{:S(2)}) copy-start(f32[768]{0:T(1024)} %copy-done.33) | copy-start | bytes 9220
  1103.2 97.8 %copy-start.50 = (f32[2,128]{1,0:T(2,128)S(1)}, f32[2,128]{1,0:T(2,128)}, u32[]{:S(2)}) copy-start(f32[2,128]{1,0:T(2,128)} %get-tuple-element.54) | copy-start | bytes 3076
  1200.1 9.9 slice-start.4
  1202.7 7.3 copy-start.11
  1202.7 7.3 slice-start.5
  1202.7 7.4 copy-start.29
  1210.0 2.3 copy-start.23
  1210.0 3.1 copy-start.8
  1212.3 1.7 copy-start.2
  1215.7 3.0 copy-start.5
  1215.7 3.0 copy-start.24
  1215.7 3.0 copy-start.30
  1215.7 3.0 copy-start.32
  1215.7 3.0 copy-start.36
  1215.7 3.0 copy-start.45
  1218.7 5.2 copy-start.12
  1218.7 5.2 copy-start.14
  1232.5 6.0 copy-start.16
  1302.2 1.7 copy-start.41
  1302.2 1.8 copy-start.56
  1302.2 1.8 copy-start.55
  1302.2 1.8 copy-start.46
  1302.3 1.8 copy-start.40
  1302.3 1.8 copy-start.38
  1302.3 1.8 copy-start.39
  1302.3 41.4 %copy-start.49 = (f32[288]{0:T(512)S(1)}, f32[288]{0:T(512)}, u32[]{:S(2)}) copy-start(f32[288]{0:T(512)} %param.22) | copy-start | bytes 3460
  1302.3 41.4 %copy-start.57 = (f32[288]{0:T(512)S(1)}, f32[288]{0:T(512)}, u32[]{:S(2)}) copy-start(f32[288]{0:T(512)} %param.27) | copy-start | bytes 3460
  1302.3 41.4 %copy-start.58 = (f32[288]{0:T(512)S(1)}, f32[288]{0:T(512)}, u32[]{:S(2)}) copy-start(f32[288]{0:T(512)} %param.26) | copy-start | bytes 3460
  1302.3 42.1 %copy-start.43 = (f32[256]{0:T(256)S(1)}, f32[256]{0:T(256)}, u32[]{:S(2)}) copy-start(f32[256]{0:T(256)} %get-tuple-element.56) | copy-start | bytes 3076
  1348.5 1655.5 %copy-start.3 = (f32[732528]{0:T(1024)S(1)}, f32[732528]{0:T(1024)}, u32[]{:S(2)}) copy-start(f32[732528]{0:T(1024)} %param.23) | copy-start | bytes 8790340
  (15 other events, 20.0 us)
Sparse Core Ops, SparseCore 0:
  47.1 681.2 all-reduce.10
  731.9 102.2 all-gather.2
  1016.4 118.8 all-reduce.12
  1302.3 1697.9 all-reduce.14
where the time goes:
time: 3040 us; the launch traced here: 3020 us
  waiting for transfers between devices  2280 us (75%)
  local copies, waits for them, and re-layouts  378 us (12%)
  blocking collectives  150 us (5%)
  matrix products  131 us (4%)
  other arithmetic  63.5 us (2%)
    unnamed x7, waiting for transfers between devices  2280 us
    reshape x2, local copies, waits for them, and re-layouts, on_device(): table = embed_all.reshape(VOCAB, width)  159 us
    reshape x1, local copies, waits for them, and re-layouts, embed_reduce(): block = contract_rows(d_logits, picked).reshape(-1)  95.8 us
    unnamed x2, blocking collectives  83.7 us
    all_gather x1, blocking collectives, on_device(): cls_all = lax.all_gather(cls_low, ('fsdp', 'rep'), axis=0, tiled=True)  66.7 us
  transfers between devices with their start and end apart: 4, of which 2 were waited for; matrix products, arithmetic and copies ran while one was open for 12% of the time, Pallas kernels for 0%

commit v1 on v0

v1 whole, which is shorter than its diff:
```python
import functools
import math

import jax
import jax.numpy as jnp
from jax import lax
from jax.sharding import Mesh, PartitionSpec as P

D = 768
FF = 3072
HEAD_DIM = 64
VOCAB = 30522
ADAM_STEP = 10


norm_eps = 1e-12
beta_one = 0.9
beta_two = 0.999
adam_eps = 1e-06
decay_rate = 0.01


def split_mats(flat):
    first = 3 * D * D
    second = first + D * D
    third = second + D * FF
    return (
        flat[:first].reshape(D, 3 * D),
        flat[first:second].reshape(D, D),
        flat[second:third].reshape(D, FF),
        flat[third:].reshape(FF, D),
    )


def split_vecs(flat):
    widths_list = [D, D, D, D, D, FF, D, D, D]
    pieces = []
    offset = 0
    for piece_width in widths_list:
        pieces.append(flat[offset : offset + piece_width].astype(jnp.float32))
        offset = offset + piece_width
    return pieces


def center_scale(resid):
    center = resid - jnp.mean(resid, axis=-1, keepdims=True)
    inverse = lax.rsqrt(jnp.mean(center * center, axis=-1, keepdims=True) + norm_eps)
    return (center * inverse, inverse)


def norm_back(d_normed, normed, inverse):
    return inverse * (
        d_normed
        - jnp.mean(d_normed, axis=-1, keepdims=True)
        - normed * jnp.mean(d_normed * normed, axis=-1, keepdims=True)
    )


def gelu_slope(value):
    return (
        0.5 * (1.0 + lax.erf(value * 0.7071067811865476))
        + value * jnp.exp(-0.5 * value * value) * 0.3989422804014327
    )


def contract_rows(left, right):
    return lax.dot_general(
        left, right, (((0,), (0,)), ((), ())), preferred_element_type=jnp.float32
    )


def contract_cols(left, right):
    return lax.dot_general(
        left, right, (((1,), (1,)), ((), ())), preferred_element_type=jnp.float32
    )


def adam_step(weight, grad, first, second, step_float, decay):
    first_new = beta_one * first + (1.0 - beta_one) * grad
    second_new = beta_two * second + (1.0 - beta_two) * grad * grad
    first_hat = first_new / (1.0 - beta_one**step_float)
    second_hat = second_new / (1.0 - beta_two**step_float)
    return first_hat / (jnp.sqrt(second_hat) + adam_eps) + decay * weight


def flip(value, name):
    return lax.ppermute(value, name, [(0, 1), (1, 0)])


def gather_bits(shard, order, names):
    grown = shard
    for name in order:
        other = flip(grown, name)
        first = lax.axis_index(name) == 0
        grown = jnp.stack([jnp.where(first, grown, other), jnp.where(first, other, grown)])
    axes = list(reversed(order))
    rank = len(axes)
    turn = [axes.index(name) for name in names] + list(range(rank, grown.ndim))
    return grown.transpose(turn).reshape((2**rank,) + shard.shape)


def reduce_bits(blocks, order, names):
    left = list(names)
    held = blocks.reshape((2,) * len(left) + blocks.shape[1:])
    for name in order:
        axis = left.index(name)
        here = lax.axis_index(name)
        send = lax.dynamic_index_in_dim(held, 1 - here, axis, keepdims=False)
        keep = lax.dynamic_index_in_dim(held, here, axis, keepdims=False)
        other = flip(send, name)
        held = (keep.astype(jnp.float32) + other.astype(jnp.float32)).astype(blocks.dtype)
        left.remove(name)
    return held


def bit_orders(names, core):
    outer = [name for name in names if name != core]
    count = len(outer)
    if count == 4:
        picks = ((0, 1, 3, 2), (3, 2, 0, 1), (0, 1, 2, 3))
        return [[outer[k] for k in pick] + [core] for pick in picks]
    step = max(1, count // 3)
    return [outer[step * k :] + outer[: step * k] + [core] for k in range(3)]


def on_device(
    names,
    core,
    block_input,
    span_lengths,
    mlm_positions,
    mlm_labels,
    span_pairs,
    layer_mats,
    vectors,
    embedding,
    mom1_mats,
    mom2_mats,
    mom1_vecs,
    mom2_vecs,
    mom1_embed,
    mom2_embed,
):
    seq_here, length, width = block_input.shape
    rows_here = seq_here * length
    heads_count = width // HEAD_DIM
    head_scale = HEAD_DIM ** (-0.5)
    devices = 2 ** len(names)
    me = lax.axis_index(names)
    orders = bit_orders(names, core)
    slots = mlm_positions.shape[1]
    picks_here = seq_here * slots
    low = jnp.bfloat16

    mat_rows = layer_mats.shape[0] // width
    third = mat_rows // 3
    vec_here = vectors.shape[0]
    mats_low = layer_mats.astype(low).reshape(3, third, width)

    def pad_row(row):
        return jnp.pad(row, (0, width - row.shape[0])).astype(low)[None]

    labels_flat = mlm_labels.reshape(-1)
    small = jnp.concatenate(
        [
            pad_row(vectors.astype(low)),
            pad_row(labels_flat // 256),
            pad_row(labels_flat % 256),
            pad_row(jnp.concatenate([span_pairs // 256, span_pairs % 256, span_lengths // 4])),
            jnp.zeros((4, width), low),
        ]
    )
    gathered = [
        gather_bits(mats_low[0], orders[0], names),
        gather_bits(mats_low[1], orders[1], names),
        gather_bits(jnp.concatenate([mats_low[2], small]), orders[2], names),
    ]
    small_all = gathered[2][:, third:, :]
    mats_all = jnp.stack([gathered[0], gathered[1], gathered[2][:, :third, :]], axis=1).reshape(-1)
    vecs_all = small_all[:, 0, :vec_here].reshape(-1)
    labels_all = (
        small_all[:, 1, :picks_here].astype(jnp.int32) * 256
        + small_all[:, 2, :picks_here].astype(jnp.int32)
    ).reshape(-1)
    ints_all = small_all[:, 3, : 3 * seq_here].astype(jnp.int32)
    pairs_all = (ints_all[:, :seq_here] * 256 + ints_all[:, seq_here : 2 * seq_here]).reshape(-1)
    quarter_all = ints_all[:, 2 * seq_here :].reshape(-1)

    embed_here = embedding.shape[0]
    shifted_rows = -(-embed_here // width)
    shift = (me * (embed_here % width)) % width
    first_row = me * (embed_here // width) + (me * (embed_here % width)) // width
    embed_low = embedding.astype(low)
    ring = range(devices)
    from_left = lax.ppermute(embed_low[-width:], names, [(k, (k + 1) % devices) for k in ring])
    from_right = lax.ppermute(embed_low[:width], names, [((k + 1) % devices, k) for k in ring])
    shifted = jnp.concatenate(
        [
            from_left,
            embed_low,
            from_right,
            jnp.zeros((shifted_rows * width - embed_here,), low),
        ]
    ).reshape(shifted_rows + 2, width)
    lanes = jnp.arange(width)
    same_row = (lanes < width - shift)[None, :]
    rolled = jnp.where(same_row, shifted[1:], shifted[:-1])
    turn = ((lanes[:, None] + shift) % width == lanes[None, :]).astype(low)
    table = jnp.dot(rolled, turn, preferred_element_type=jnp.float32).astype(low)
    row_start = jnp.arange(shifted_rows + 1) * width - shift
    owned = (row_start >= 0) & (row_start < embed_here)
    touched = (row_start + width > 0) & (row_start < embed_here)
    table_owned = jnp.where(owned[:, None], table, 0)

    w_qkv, w_out, w_up, w_down = split_mats(mats_all)
    bias_q, bias_v, bias_out, gain_one, shift_one, bias_up, bias_down, gain_two, shift_two = (
        split_vecs(vecs_all)
    )
    valid = jnp.arange(length)[None, :] < span_lengths[:, None]
    valid_col = valid.reshape(rows_here, 1).astype(jnp.float32)
    tok_rows = (block_input * valid[:, :, None].astype(low)).reshape(rows_here, width)
    qkv_bias = jnp.concatenate([bias_q, jnp.zeros((width,), jnp.float32), bias_v])
    projected = (jnp.dot(tok_rows, w_qkv, preferred_element_type=jnp.float32) + qkv_bias).astype(
        low
    )
    shaped = projected.reshape(seq_here, length, 3, heads_count, HEAD_DIM)
    queries = shaped[:, :, 0]
    key_rows = shaped[:, :, 1]
    value_rows = shaped[:, :, 2]
    key_valid = valid[:, None, None, :]

    def make_scores():
        raw = (
            jnp.einsum("sqhd,skhd->shqk", queries, key_rows, preferred_element_type=jnp.float32)
            * head_scale
        )
        return jnp.where(key_valid, raw, -1e30)

    scores = make_scores()
    row_max = jnp.max(scores, axis=-1, keepdims=True)
    expo_vals = jnp.exp(scores - row_max)
    row_sum = jnp.sum(expo_vals, axis=-1, keepdims=True)
    row_lse = row_max + jnp.log(row_sum)
    attn_probs = (expo_vals / row_sum).astype(low)
    attended = (
        jnp.einsum("shqk,skhd->sqhd", attn_probs, value_rows, preferred_element_type=jnp.float32)
        .reshape(rows_here, width)
        .astype(low)
    )
    branch = jnp.dot(attended, w_out, preferred_element_type=jnp.float32) + bias_out
    normed_one, inverse_one = center_scale(tok_rows.astype(jnp.float32) + branch)
    hidden_one = normed_one * gain_one + shift_one
    hidden_low = hidden_one.astype(low)
    pre_act = jnp.dot(hidden_low, w_up, preferred_element_type=jnp.float32) + bias_up
    act_low = jax.nn.gelu(pre_act, approximate=False).astype(low)
    ffn_out = jnp.dot(act_low, w_down, preferred_element_type=jnp.float32) + bias_down
    normed_two, inverse_two = center_scale(hidden_one + ffn_out)
    output = (normed_two * gain_two + shift_two) * valid_col
    output_seq = output.reshape(seq_here, length, width)

    picked_here = jnp.take_along_axis(output_seq, mlm_positions[:, :, None], axis=1).reshape(
        -1, width
    )
    cls_pad = -seq_here % 8
    heads_rows = jnp.concatenate(
        [picked_here, output_seq[:, 0, :], jnp.zeros((cls_pad, width), jnp.float32)]
    ).astype(low)
    cut = width // 3
    heads_all = jnp.concatenate(
        [
            gather_bits(heads_rows[:, k * cut : (k + 1) * cut], orders[k], names)
            for k in range(3)
        ],
        axis=2,
    )
    picked = heads_all[:, :picks_here, :].reshape(-1, width)
    cls_all = heads_all[:, picks_here : picks_here + seq_here, :].reshape(-1, width)

    logits = contract_cols(picked, table)
    masked = jnp.where(owned[None, :], logits, -jnp.inf)
    part_max = jnp.max(masked, axis=-1)
    part_sum = jnp.sum(jnp.exp(masked - part_max[:, None]), axis=-1)
    stats = jnp.stack([part_max, part_sum]).reshape(1, -1, 128)
    stats_all = lax.all_to_all(
        jnp.broadcast_to(stats, (devices,) + stats.shape[1:]), names, 0, 0, tiled=True
    ).reshape(devices, 2, -1)
    full_max = jnp.max(stats_all[:, 0], axis=0)
    full_sum = jnp.sum(stats_all[:, 1] * jnp.exp(stats_all[:, 0] - full_max), axis=0)
    row_of = labels_all - first_row
    hot = row_of[:, None] == jnp.arange(shifted_rows + 1)[None, :]
    used = (jnp.arange(slots)[None, :] < quarter_all[:, None]).reshape(-1, 1)
    probs = jnp.exp(logits - full_max[:, None]) / full_sum[:, None]
    d_logits = jnp.where(
        used & touched[None, :], probs - hot.astype(jnp.float32), 0.0
    ).astype(low)
    d_picked_part = jnp.dot(d_logits, table_owned, preferred_element_type=jnp.float32).astype(low)
    blocks = d_picked_part.reshape(devices, picks_here, width)
    d_picked = jnp.concatenate(
        [
            reduce_bits(blocks[:, :, k * cut : (k + 1) * cut], orders[k][::-1], names)
            for k in range(3)
        ],
        axis=1,
    ).astype(jnp.float32)

    select = (mlm_positions[:, :, None] == jnp.arange(length)[None, None, :]).astype(jnp.float32)
    d_output_seq = jnp.einsum(
        "gor,gon->grn",
        select,
        d_picked.reshape(seq_here, slots, width),
        precision=lax.Precision.HIGHEST,
    )
    span_scale = 2.0 / math.sqrt(width)
    columns = jnp.arange(cls_all.shape[0])
    sims = contract_cols(cls_all, cls_all) * span_scale
    sims = jnp.where(columns[None, :] == columns[:, None], -1e30, sims)
    partner_hot = (columns[None, :] == pairs_all[:, None]).astype(jnp.float32)
    d_sims = (jax.nn.softmax(sims, axis=-1) - partner_hot).astype(low)
    mine = me * seq_here
    d_sims_rows = lax.dynamic_slice_in_dim(d_sims, mine, seq_here, 0)
    d_sims_cols = lax.dynamic_slice_in_dim(d_sims, mine, seq_here, 1)
    d_cls = (
        jnp.dot(d_sims_rows, cls_all, preferred_element_type=jnp.float32)
        + contract_rows(d_sims_cols, cls_all)
    ) * span_scale
    d_output_seq = d_output_seq.at[:, 0, :].add(d_cls)
    d_output = d_output_seq.reshape(rows_here, width) * valid_col
    d_gain_two = jnp.sum(d_output * normed_two, axis=0)
    d_shift_two = jnp.sum(d_output, axis=0)
    d_resid_two = norm_back(d_output * gain_two, normed_two, inverse_two)
    d_ffn = d_resid_two.astype(low)
    d_bias_down = jnp.sum(d_ffn.astype(jnp.float32), axis=0)
    d_w_down = contract_rows(act_low, d_ffn)
    d_act = contract_cols(d_ffn, w_down)
    d_pre = (d_act * gelu_slope(pre_act)).astype(low)
    d_bias_up = jnp.sum(d_pre.astype(jnp.float32), axis=0)
    d_w_up = contract_rows(hidden_low, d_pre)
    d_hidden = contract_cols(d_pre, w_up) + d_resid_two
    d_gain_one = jnp.sum(d_hidden * normed_one, axis=0)
    d_shift_one = jnp.sum(d_hidden, axis=0)
    d_resid_one = norm_back(d_hidden * gain_one, normed_one, inverse_one)
    d_branch = d_resid_one.astype(low)
    d_bias_out = jnp.sum(d_branch.astype(jnp.float32), axis=0)
    d_w_out = contract_rows(attended, d_branch)
    d_attended = (
        contract_cols(d_branch, w_out).astype(low).reshape(seq_here, length, heads_count, HEAD_DIM)
    )
    probs_again = jnp.exp(make_scores() - row_lse)
    probs_low = probs_again.astype(low)
    d_probs = jnp.einsum(
        "sqhd,skhd->shqk", d_attended, value_rows, preferred_element_type=jnp.float32
    )
    d_values = jnp.einsum(
        "shqk,sqhd->skhd", probs_low, d_attended, preferred_element_type=jnp.float32
    )
    row_delta = jnp.sum(d_probs * probs_again, axis=-1, keepdims=True)
    d_scores = (probs_again * (d_probs - row_delta)).astype(low)
    d_queries = (
        jnp.einsum("shqk,skhd->sqhd", d_scores, key_rows, preferred_element_type=jnp.float32)
        * head_scale
    )
    d_keys = (
        jnp.einsum("shqk,sqhd->skhd", d_scores, queries, preferred_element_type=jnp.float32)
        * head_scale
    )
    d_qkv = jnp.concatenate(
        [
            d_queries.reshape(rows_here, width),
            d_keys.reshape(rows_here, width),
            d_values.reshape(rows_here, width),
        ],
        axis=1,
    ).astype(low)
    d_qkv_float = d_qkv.astype(jnp.float32)
    d_bias_q = jnp.sum(d_qkv_float[:, :width], axis=0)
    d_bias_v = jnp.sum(d_qkv_float[:, 2 * width :], axis=0)
    d_w_qkv = contract_rows(tok_rows, d_qkv)
    grad_input = ((contract_cols(d_qkv, w_qkv) + d_resid_one) * valid_col).reshape(
        seq_here, length, width
    )

    d_mats = jnp.concatenate(
        [
            piece.astype(low).reshape(-1, width)
            for piece in (d_w_qkv, d_w_out, d_w_up, d_w_down)
        ]
    ).reshape(devices, 3, third, width)
    d_vecs = jnp.concatenate(
        [
            d_bias_q,
            d_bias_v,
            d_bias_out,
            d_gain_one,
            d_shift_one,
            d_bias_up,
            d_bias_down,
            d_gain_two,
            d_shift_two,
        ]
    ).reshape(devices, 1, vec_here)
    d_small = jnp.pad(d_vecs, ((0, 0), (0, 7), (0, width - vec_here))).astype(low)
    summed = [
        reduce_bits(d_mats[:, 0], orders[0][::-1], names),
        reduce_bits(d_mats[:, 1], orders[1][::-1], names),
        reduce_bits(jnp.concatenate([d_mats[:, 2], d_small], axis=1), orders[2][::-1], names),
    ]
    grad_vecs = summed[2][third, :vec_here].astype(jnp.float32)
    grad_mats = (
        jnp.concatenate([summed[0], summed[1], summed[2][:third]]).astype(jnp.float32).reshape(-1)
    )

    picked_turned = jnp.dot(picked, turn.T, preferred_element_type=jnp.float32).astype(low)
    d_rolled = contract_rows(d_logits, picked_turned)
    grad_embed = jnp.where(same_row, d_rolled[:-1], d_rolled[1:]).reshape(-1)[:embed_here]

    step_float = float(ADAM_STEP)
    step_mats = adam_step(layer_mats, grad_mats, mom1_mats, mom2_mats, step_float, decay_rate)
    step_vecs = adam_step(vectors, grad_vecs, mom1_vecs, mom2_vecs, step_float, 0.0)
    step_embed = adam_step(embedding, grad_embed, mom1_embed, mom2_embed, step_float, decay_rate)
    return (grad_input, grad_mats, grad_vecs, grad_embed, step_mats, step_vecs, step_embed)


def solution(mesh):
    fsdp_bits = mesh.shape["fsdp"].bit_length() - 1
    rep_bits = mesh.shape["rep"].bit_length() - 1
    names = tuple(f"f{k}" for k in reversed(range(fsdp_bits)))
    core = names[-1]
    names = names + tuple(f"r{k}" for k in reversed(range(rep_bits)))
    bits = Mesh(mesh.devices.reshape((2,) * len(names)), names)
    seqs = P(names, None, None)
    pairs = P(names, None)
    flat = P(names)
    return jax.shard_map(
        functools.partial(on_device, names, core),
        mesh=bits,
        in_specs=(seqs, flat, pairs, pairs) + (flat,) * 10,
        out_specs=(seqs,) + (flat,) * 6,
        check_vma=False,
    )
```

time: 3040 us -> 569 us (0.19)
  waiting for transfers between devices: 2280 us -> 177 us
  local copies, waits for them, and re-layouts: 378 us -> 154 us
  blocking collectives: 150 us -> 0 us
  matrix products: 131 us -> 70.5 us
  starting transfers between devices: 0.16 us -> 56.9 us
  other arithmetic: 63.5 us -> 102 us
    unnamed x7 -> x0, waiting for transfers between devices: 2280 us -> none
    reshape x7 -> x9, local copies, waits for them, and re-layouts: 276 us -> 24.7 us  [the longest x2 12.4 us: on_device(): piece.astype(low).reshape(-1, width)]
    ppermute x0 -> x62, waiting for transfers between devices: none -> 165 us  [the longest x60 165 us: flip(): return lax.ppermute(value, name, [(0, 1), (1, 0)])]
    unnamed x2 -> x0, blocking collectives: 83.7 us -> none
    all_gather x1 -> x0, blocking collectives: 66.7 us -> none  [on_device(): cls_all = lax.all_gather(cls_low, ('fsdp', 'rep'), axis=0, tiled=True)]
    ppermute x0 -> x62, starting transfers between devices: none -> 53.1 us  [the longest x60 47.7 us: flip(): return lax.ppermute(value, name, [(0, 1), (1, 0)])]
    dot_general x6, matrix products: 52.2 us -> 19 us  [contract_rows(): lax.dot_general(left, right, (((0,), (0,)), ((), ())), preferred_element_...]
    unnamed x161 -> x207, local copies, waits for them, and re-layouts: 54.3 us -> 21.5 us
  transfers between devices with their start and end apart: 4 -> 63, of which waited for: 2 -> 38; matrix products, arithmetic and copies ran while one was open for 12% -> 21% of each run, Pallas kernels for 0% -> 0%
where the time goes in v1:
time: 569 us; the launch traced here: 563 us
  waiting for transfers between devices  177 us (31%)
  local copies, waits for them, and re-layouts  154 us (27%)
  other arithmetic  102 us (18%)
  matrix products  70.5 us (12%)
  starting transfers between devices  56.9 us (10%)
    ppermute x60, waiting for transfers between devices, flip(): return lax.ppermute(value, name, [(0, 1), (1, 0)])  165 us
    ppermute x60, starting transfers between devices, flip(): return lax.ppermute(value, name, [(0, 1), (1, 0)])  47.7 us
    concatenate x2, local copies, waits for them, and re-layouts, on_device(): jnp.concatenate([from_left, embed_low, from_right, jnp.zeros((shifted_row...  31.8 us
    slice x1, local copies, waits for them, and re-layouts, split_mats(): flat[second:third].reshape(D, FF)  22.8 us
    unnamed x207, local copies, waits for them, and re-layouts  21.5 us
    dot_general x6, matrix products, contract_rows(): lax.dot_general(left, right, (((0,), (0,)), ((), ())), preferred_element_...  19 us
    concatenate x1, other arithmetic, on_device(): jnp.concatenate([piece.astype(low).reshape(-1, width) for piece in (d_w_q...  17.7 us
    dot_general x6, matrix products, contract_cols(): lax.dot_general(left, right, (((1,), (1,)), ((), ())), preferred_element_...  17.6 us
  transfers between devices with their start and end apart: 63, of which 38 were waited for; matrix products, arithmetic and copies ran while one was open for 21% of the time, Pallas kernels for 0%

profile of v1, /device:TPU:0, one launch (start us, length us, event | category | flops | bytes accessed | tf_op | source)
XLA Modules:
  0.0 563.2 jit_solution(407440497728908936)
XLA Ops:
  2.0 3.0 collective-permute-start.5
  5.2 2.7 collective-permute-start
  12.5 6.7 %collective-permute-done = bf16[96,768]{1,0:T(8,128)(2,1)S(1)} collective-permute-done((bf16[96,768]{1,0:T(8,128)(2,1)S(1)}, bf16[96,768]{1,0:T(8,128)(2,1)S(1)}, u32[]{:S(2)}, u32[]{:S(2)}) %collective-permute-start) | collective-permute-done | bytes 147488 | tf_op jit(solution)/shard_map/ppermute | solution.py:87
  19.4 2.2 collective-permute-done.10
  22.4 3.5 collective-permute-start.7
  25.9 12.7 %collective-permute-done.1 = bf16[2,96,768]{2,1,0:T(8,128)(2,1)S(1)} collective-permute-done((bf16[2,96,768]{2,1,0:T(8,128)(2,1)S(1)}, bf16[2,96,768]{2,1,0:T(8,128)(2,1)S(1)}, u32[]{:S(2)}, u32[]{:S(2)}) %collective-permute-start.1) | collective-permute-done | bytes 294944 | tf_op jit(solution)/shard_map/ppermute | solution.py:87
  39.3 4.7 collective-permute-done.11
  44.0 7.7 %collective-permute-done.7 = bf16[2,2,96,768]{3,2,1,0:T(8,128)(2,1)S(1)} collective-permute-done((bf16[2,2,96,768]{3,2,1,0:T(8,128)(2,1)S(1)}, bf16[2,2,96,768]{3,2,1,0:T(8,128)(2,1)S(1)}, u32[]{:S(2)}, u32[]{:S(2)}) %collective-permute-start.7) | collective-permute-done | bytes 589856 | tf_op jit(solution)/shard_map/ppermute | solution.py:87
  54.6 14.9 %collective-permute-done.12 = bf16[2,2,104,768]{3,2,1,0:T(8,128)(2,1)S(1)} collective-permute-done((bf16[2,2,104,768]{3,2,1,0:T(8,128)(2,1)S(1)}, bf16[2,2,104,768]{3,2,1,0:T(8,128)(2,1)S(1)}, u32[]{:S(2)}, u32[]{:S(2)}) %collective-permute-start.12) | collective-permute-done | bytes 639008 | tf_op jit(solution)/shard_map/ppermute | solution.py:87
  71.4 7.6 %collective-permute-done.8 = bf16[2,2,2,96,768]{4,3,2,1,0:T(8,128)(2,1)S(1)} collective-permute-done((bf16[2,2,2,96,768]{4,3,2,1,0:T(8,128)(2,1)S(1)}, bf16[2,2,2,96,768]{4,3,2,1,0:T(8,128)(2,1)S(1)}, u32[]{:S(2)}, u32[]{:S(2)}) %collective-permute-start.8) | collective-permute-done | bytes 1179680 | tf_op jit(solution)/shard_map/ppermute | solution.py:87
  81.0 11.9 %collective-permute-done.3 = bf16[2,2,2,96,768]{4,3,2,1,0:T(8,128)(2,1)S(1)} collective-permute-done((bf16[2,2,2,96,768]{4,3,2,1,0:T(8,128)(2,1)S(1)}, bf16[2,2,2,96,768]{4,3,2,1,0:T(8,128)(2,1)S(1)}, u32[]{:S(2)}, u32[]{:S(2)}) %collective-permute-start.3) | collective-permute-done | bytes 1179680 | tf_op jit(solution)/shard_map/ppermute | solution.py:87
  96.4 5.0 collective-permute-start.30
  109.9 16.0 %concatenate.57 = bf16[734064]{0:T(1024)(128)(2,1)} concatenate(bf16[768]{0:T(1024)(128)(2,1)S(1)} %collective-permute-done.31, bf16[732528]{0:T(1024)(128)(2,1)S(1)} %convert_element_type.581, bf16[768]{0:T(1024)(128)(2,1)S(1)} %collective-permute-done.30), dimensions={0} | concatenate | bytes 2936256 | tf_op jit(solution)/shard_map/concatenate | solution.py:197
  126.0 3.9 slice.273
  129.8 15.7 %concatenate.56 = bf16[733440]{0:T(1024)(128)(2,1)} concatenate(bf16[732528]{0:T(1024)(128)(2,1)S(1)} %convert_element_type.581, bf16[768]{0:T(1024)(128)(2,1)S(1)} %collective-permute-done.30, bf16[144]{0:T(256)(128)(2,1)S(1)} %broadcast_in_dim.164), dimensions={0} | concatenate | bytes 2933760 | tf_op jit(solution)/shard_map/concatenate | solution.py:197
  145.6 3.9 slice.270
  149.5 4.6 fusion.49
  154.1 2.9 select_bitcast_fusion.3
  157.5 2.6 copy.162
  160.5 2.6 copy.161
  168.4 2.7 slice_bitcast_fusion
  172.4 6.7 %pad_maximum_fusion = bf16[32,3,96,768]{3,2,0,1:T(8,128)(2,1)S(1)} fusion(bf16[32,1,96,768]{3,2,0,1:T(8,128)(2,1)} %slice_bitcast_fusion, bf16[32,1,96,768]{3,2,0,1:T(8,128)(2,1)} %bitcast.458, bf16[32,1,96,768]{3,2,0,1:T(8,128)(2,1)} %bitcast.459), kind=kLoop, calls=%fused_computation.1 | loop fusion | flops 14155776 | bytes 28311552 | tf_op jit(solution)/shard_map/stack | solution.py:179
  179.4 5.6 %copy.171 = bf16[32,3,96,768]{3,2,1,0:T(8,128)(2,1)} copy(bf16[32,3,96,768]{3,2,0,1:T(8,128)(2,1)S(1)} %pad_maximum_fusion) | data formatting | bytes 28311552 | tf_op jit(solution)/shard_map/stack | solution.py:179
  189.1 5.1 reshape.500
  196.0 3.1 fusion.20
  205.0 22.8 %slice.255 = bf16[2304,3072]{1,0:T(8,128)(2,1)} reshape(bf16[32,3,96,768]{3,2,1,0:T(8,128)(2,1)} %copy.171) | data formatting | bytes 28311552 | tf_op jit(solution)/shard_map/slice | solution.py:30
  229.9 11.2 %fusion.23 = (bf16[256,3072]{1,0:T(8,128)(2,1)S(1)}, f32[256,3072]{1,0:T(8,128)}) fusion(f32[3072]{0:T(1024)S(1)} %copy-done.71, bf16[2304,3072]{1,0:T(8,128)(2,1)} %slice.255, f32[256,768]{1,0:T(8,128)S(1)} %get-tuple-element.148, f32[768]{0:T(1024)S(1)} %get-tuple-element.130, f32[768]{0:T(1024)S(1)} %get-tuple-element.131, f32[256]{0:T(256)S(1)} %add_rsqrt_fusion.1, ...), kind=kOutput, calls=%fused_computation.45 | convolution fusion | flops 1260847104 | bytes 10244096 | tf_op jit(solution)/shard_map/dot_general | solution.py:254
  241.2 4.3 fusion.177
  248.4 4.1 collective-permute-done.15
  255.1 2.3 collective-permute-done.25
  263.4 3.2 collective-permute-done.22
  268.6 4.9 collective-permute-done.23
  280.6 3.3 select_reduce_fusion
  287.9 3.7 all-to-all-start
  294.4 12.3 %all-to-all-done = f32[32,32,128]{2,1,0:T(8,128)S(1)} async-done(((f32[32,32,128]{2,1,0:T(8,128)}), f32[32,32,128]{2,1,0:T(8,128)S(1)}, u32[]{:S(2)}, u32[]{:S(2)}) %all-to-all-start) | async-done | bytes 524320 | tf_op jit(solution)/shard_map/all_to_all | solution.py:284
  309.7 5.5 select_convert_fusion
  315.3 4.0 convolution_convert_fusion.4
  325.6 5.8 %collective-permute-done.43 = bf16[2,2,2,64,256]{4,3,0,1,2:T(8,128)(2,1)S(1)} collective-permute-done((bf16[2,2,2,64,256]{4,3,0,1,2:T(8,128)(2,1)S(1)}, bf16[2,2,2,64,256]{4,3,0,1,2:T(8,128)(2,1)S(1)}, u32[]{:S(2)}, u32[]{:S(2)}) %collective-permute-start.43) | collective-permute-done | bytes 262176 | tf_op jit(solution)/shard_map/ppermute | solution.py:87
  338.8 3.0 collective-permute-done.39
  343.1 3.0 collective-permute-start.36
  356.9 4.9 fusion.179
  361.9 5.2 multiply_reduce_fusion.2
  377.9 3.7 convolution_convert_fusion.1
  386.4 3.6 convolution_convert_fusion
  390.1 8.9 %reshape.522 = bf16[3072,768]{1,0:T(8,128)(2,1)} reshape(bf16[768,3072]{1,0:T(8,128)(2,1)} %convolution_convert_fusion.1) | data formatting | bytes 9437184 | tf_op jit(solution)/shard_map/reshape | solution.py:384
  398.9 2.2 slice_reduce_fusion
  416.9 3.6 reshape.521
  420.5 17.7 %pad_maximum_fusion.1 = bf16[9216,768]{1,0:T(8,128)(2,1)S(1)} fusion(bf16[3072,768]{1,0:T(8,128)(2,1)} %convolution_convert_fusion, bf16[3072,768]{1,0:T(8,128)(2,1)} %reshape.522, bf16[768,768]{1,0:T(8,128)(2,1)} %convolution_convert_fusion.5, bf16[2304,768]{1,0:T(8,128)(2,1)} %reshape.521), kind=kLoop, calls=%fused_computation.2 | loop fusion | flops 56623104 | bytes 28311552 | tf_op jit(solution)/shard_map/concatenate | solution.py:382
  448.4 8.9 %fusion.85 = f32[955,768]{1,0:T(8,128)S(1)} fusion(bf16[2048,955]{0,1:T(8,128)(2,1)} %copy-done.26, bf16[2048,768]{1,0:T(8,128)(2,1)} %bitcast.477, s32[768]{0:T(1024)S(1)} %copy-done.79), kind=kOutput, calls=%fused_computation.165 | convolution fusion | flops 5422252032 | bytes 9994240 | tf_op jit(solution)/shard_map/dot_general | solution.py:67
  459.3 2.8 reshape.525
  462.1 3.1 fusion.2
  467.2 2.5 fusion.1
  470.9 2.6 fusion
  476.1 7.5 %fusion.40 = (f32[732528]{0:T(1024)}, f32[732528]{0:T(1024)}) fusion(f32[732528]{0:T(1024)S(1)} %copy-done.4, f32[732528]{0:T(1024)} %param.29, f32[732528]{0:T(1024)} %param.28, f32[732672]{0:T(1024)S(1)} %reshape.525), kind=kLoop, calls=%fused_computation.71 | loop fusion | flops 9522864 | bytes 17580672 | tf_op jit(solution)/shard_map/add | solution.py:83
  485.6 9.4 %collective-permute-done.48 = bf16[2,2,2,96,768]{4,3,0,1,2:T(8,128)(2,1)} collective-permute-done((bf16[2,2,2,96,768]{4,3,0,1,2:T(8,128)(2,1)}, bf16[2,2,2,96,768]{4,3,0,1,2:T(8,128)(2,1)}, u32[]{:S(2)}, u32[]{:S(2)}) %collective-permute-start.48) | collective-permute-done | bytes 1179680 | tf_op jit(solution)/shard_map/ppermute | solution.py:87
  502.0 3.9 collective-permute-done.58
  507.4 10.7 %collective-permute-done.49 = bf16[2,2,96,768]{3,2,0,1:T(8,128)(2,1)S(1)} collective-permute-done((bf16[2,2,96,768]{3,2,0,1:T(8,128)(2,1)S(1)}, bf16[2,2,96,768]{3,2,0,1:T(8,128)(2,1)S(1)}, u32[]{:S(2)}, u32[]{:S(2)}) %collective-permute-start.49) | collective-permute-done | bytes 589856 | tf_op jit(solution)/shard_map/ppermute | solution.py:87
  520.1 9.7 %collective-permute-done.54 = bf16[2,2,96,768]{3,2,1,0:T(8,128)(2,1)S(1)} collective-permute-done((bf16[2,2,96,768]{3,2,1,0:T(8,128)(2,1)S(1)}, bf16[2,2,96,768]{3,2,1,0:T(8,128)(2,1)S(1)}, u32[]{:S(2)}, u32[]{:S(2)}) %collective-permute-start.54) | collective-permute-done | bytes 589856 | tf_op jit(solution)/shard_map/ppermute | solution.py:87
  530.9 5.1 collective-permute-done.50
  536.2 2.7 collective-permute-done.55
  540.5 4.6 collective-permute-done.51
  545.1 5.7 %collective-permute-done.60 = bf16[2,104,768]{2,1,0:T(8,128)(2,1)S(1)} collective-permute-done((bf16[2,104,768]{2,1,0:T(8,128)(2,1)S(1)}, bf16[2,104,768]{2,1,0:T(8,128)(2,1)S(1)}, u32[]{:S(2)}, u32[]{:S(2)}) %collective-permute-start.60) | collective-permute-done | bytes 319520 | tf_op jit(solution)/shard_map/ppermute | solution.py:87
  551.1 8.2 %collective-permute-done.61 = bf16[104,768]{1,0:T(8,128)(2,1)S(1)} collective-permute-done((bf16[104,768]{1,0:T(8,128)(2,1)S(1)}, bf16[104,768]{1,0:T(8,128)(2,1)S(1)}, u32[]{:S(2)}, u32[]{:S(2)}) %collective-permute-start.61) | collective-permute-done | bytes 159776 | tf_op jit(solution)/shard_map/ppermute | solution.py:87
  560.3 2.7 fusion.91
  (554 shorter events, 168.5 us)
Async XLA Ops:
  2.0 8.8 %collective-permute-start.5 = (bf16[96,768]{1,0:T(8,128)(2,1)S(1)}, bf16[96,768]{1,0:T(8,128)(2,1)S(1)}, u32[]{:S(2)}, u32[]{:S(2)}) collective-permute-start(bf16[96,768]{1,0:T(8,128)(2,1)S(1)} %slice.239), channel_id=1, source_target_pairs={{0,1},{1,0},{2,3},{3,2},{4,5},{5,4},{6,7},{7,6},{8,9},{9,8},{10,11... | collective-permute-start | bytes 442376 | tf_op jit(solution)/shard_map/ppermute | solution.py:87
  5.2 14.0 %collective-permute-start = (bf16[96,768]{1,0:T(8,128)(2,1)S(1)}, bf16[96,768]{1,0:T(8,128)(2,1)S(1)}, u32[]{:S(2)}, u32[]{:S(2)}) collective-permute-start(bf16[96,768]{1,0:T(8,128)(2,1)S(1)} %slice.237), channel_id=1, source_target_pairs={{0,16},{16,0},{1,17},{17,1},{2,18},{18,2},{3,19},{19,3},{4,20},{20... | collective-permute-start | bytes 442376 | tf_op jit(solution)/shard_map/ppermute | solution.py:87
  10.4 11.2 %collective-permute-start.10 = (bf16[104,768]{1,0:T(8,128)(2,1)S(1)}, bf16[104,768]{1,0:T(8,128)(2,1)S(1)}, u32[]{:S(2)}, u32[]{:S(2)}) collective-permute-start(bf16[104,768]{1,0:T(8,128)(2,1)S(1)} %concatenate.52), channel_id=1, source_target_pairs={{0,16},{16,0},{1,17},{17,1},{2,18},{18,2},{3,19},{19,3},{4,20},{20... | collective-permute-start | bytes 479240 | tf_op jit(solution)/shard_map/ppermute | solution.py:87
  10.9 11.4 %collective-permute-start.6 = (bf16[2,96,768]{2,1,0:T(8,128)(2,1)S(1)}, bf16[2,96,768]{2,1,0:T(8,128)(2,1)S(1)}, u32[]{:S(2)}, u32[]{:S(2)}) collective-permute-start(bf16[2,96,768]{2,1,0:T(8,128)(2,1)S(1)} %pad_maximum_fusion.17), channel_id=1, source_target_pairs={{0,4},{4,0},{1,5},{5,1},{2,6},{6,2},{3,7},{7,3},{8,12},{12,8},{9,1... | collective-permute-start | bytes 884744 | tf_op jit(solution)/shard_map/ppermute | solution.py:87
  19.3 19.3 %collective-permute-start.1 = (bf16[2,96,768]{2,1,0:T(8,128)(2,1)S(1)}, bf16[2,96,768]{2,1,0:T(8,128)(2,1)S(1)}, u32[]{:S(2)}, u32[]{:S(2)}) collective-permute-start(bf16[2,96,768]{2,1,0:T(8,128)(2,1)S(1)} %pad_maximum_fusion.16), channel_id=1, source_target_pairs={{0,8},{8,0},{1,9},{9,1},{2,10},{10,2},{3,11},{11,3},{4,12},{12,4},... | collective-permute-start | bytes 884744 | tf_op jit(solution)/shard_map/ppermute | solution.py:87
  21.6 22.3 %collective-permute-start.11 = (bf16[2,104,768]{2,1,0:T(8,128)(2,1)S(1)}, bf16[2,104,768]{2,1,0:T(8,128)(2,1)S(1)}, u32[]{:S(2)}, u32[]{:S(2)}) collective-permute-start(bf16[2,104,768]{2,1,0:T(8,128)(2,1)S(1)} %pad_maximum_fusion.15), channel_id=1, source_target_pairs={{0,8},{8,0},{1,9},{9,1},{2,10},{10,2},{3,11},{11,3},{4,12},{12,4},... | collective-permute-start | bytes 958472 | tf_op jit(solution)/shard_map/ppermute | solution.py:87
  22.4 29.4 %collective-permute-start.7 = (bf16[2,2,96,768]{3,2,1,0:T(8,128)(2,1)S(1)}, bf16[2,2,96,768]{3,2,1,0:T(8,128)(2,1)S(1)}, u32[]{:S(2)}, u32[]{:S(2)}) collective-permute-start(bf16[2,2,96,768]{3,2,1,0:T(8,128)(2,1)S(1)} %pad_maximum_fusion.11), channel_id=1, source_target_pairs={{0,16},{16,0},{1,17},{17,1},{2,18},{18,2},{3,19},{19,3},{4,20},{20... | collective-permute-start | bytes 1769480 | tf_op jit(solution)/shard_map/ppermute | solution.py:87
  38.7 15.0 %collective-permute-start.2 = (bf16[2,2,96,768]{3,2,1,0:T(8,128)(2,1)S(1)}, bf16[2,2,96,768]{3,2,1,0:T(8,128)(2,1)S(1)}, u32[]{:S(2)}, u32[]{:S(2)}) collective-permute-start(bf16[2,2,96,768]{3,2,1,0:T(8,128)(2,1)S(1)} %pad_maximum_fusion.10), channel_id=1, source_target_pairs={{0,1},{1,0},{2,3},{3,2},{4,5},{5,4},{6,7},{7,6},{8,9},{9,8},{10,11... | collective-permute-start | bytes 1769480 | tf_op jit(solution)/shard_map/ppermute | solution.py:87
  52.0 27.1 %collective-permute-start.8 = (bf16[2,2,2,96,768]{4,3,2,1,0:T(8,128)(2,1)S(1)}, bf16[2,2,2,96,768]{4,3,2,1,0:T(8,128)(2,1)S(1)}, u32[]{:S(2)}, u32[]{:S(2)}) collective-permute-start(bf16[2,2,2,96,768]{4,3,2,1,0:T(8,128)(2,1)S(1)} %pad_maximum_fusion.8), channel_id=1, source_target_pairs={{0,8},{8,0},{1,9},{9,1},{2,10},{10,2},{3,11},{11,3},{4,12},{12,4},... | collective-permute-start | bytes 3538952 | tf_op jit(solution)/shard_map/ppermute | solution.py:87
  52.1 17.4 %collective-permute-start.12 = (bf16[2,2,104,768]{3,2,1,0:T(8,128)(2,1)S(1)}, bf16[2,2,104,768]{3,2,1,0:T(8,128)(2,1)S(1)}, u32[]{:S(2)}, u32[]{:S(2)}) collective-permute-start(bf16[2,2,104,768]{3,2,1,0:T(8,128)(2,1)S(1)} %pad_maximum_fusion.9), channel_id=1, source_target_pairs={{0,4},{4,0},{1,5},{5,1},{2,6},{6,2},{3,7},{7,3},{8,12},{12,8},{9,1... | collective-permute-start | bytes 1916936 | tf_op jit(solution)/shard_map/ppermute | solution.py:87
  53.9 39.0 %collective-permute-start.3 = (bf16[2,2,2,96,768]{4,3,2,1,0:T(8,128)(2,1)S(1)}, bf16[2,2,2,96,768]{4,3,2,1,0:T(8,128)(2,1)S(1)}, u32[]{:S(2)}, u32[]{:S(2)}) collective-permute-start(bf16[2,2,2,96,768]{4,3,2,1,0:T(8,128)(2,1)S(1)} %pad_maximum_fusion.7), channel_id=1, source_target_pairs={{0,4},{4,0},{1,5},{5,1},{2,6},{6,2},{3,7},{7,3},{8,12},{12,8},{9,1... | collective-permute-start | bytes 3538952 | tf_op jit(solution)/shard_map/ppermute | solution.py:87
  70.9 31.7 %collective-permute-start.13 = (bf16[2,2,2,104,768]{4,3,2,1,0:T(8,128)(2,1)}, bf16[2,2,2,104,768]{4,3,2,1,0:T(8,128)(2,1)}, u32[]{:S(2)}, u32[]{:S(2)}) collective-permute-start(bf16[2,2,2,104,768]{4,3,2,1,0:T(8,128)(2,1)} %pad_maximum_fusion.6), channel_id=1, source_target_pairs={{0,1},{1,0},{2,3},{3,2},{4,5},{5,4},{6,7},{7,6},{8,9},{9,8},{10,11... | collective-permute-start | bytes 3833864 | tf_op jit(solution)/shard_map/ppermute | solution.py:87
  81.0 73.1 %collective-permute-start.9 = (bf16[2,2,2,2,96,768]{5,4,3,2,1,0:T(8,128)(2,1)}, bf16[2,2,2,2,96,768]{5,4,3,2,1,0:T(8,128)(2,1)}, u32[]{:S(2)}, u32[]{:S(2)}) collective-permute-start(bf16[2,2,2,2,96,768]{5,4,3,2,1,0:T(8,128)(2,1)} %pad_maximum_fusion.5), channel_id=1, source_target_pairs={{0,2},{2,0},{1,3},{3,1},{4,6},{6,4},{5,7},{7,5},{8,10},{10,8},{9,1... | collective-permute-start | bytes 7077896 | tf_op jit(solution)/shard_map/ppermute | solution.py:87
  95.8 58.3 %collective-permute-start.4 = (bf16[2,2,2,2,96,768]{5,4,3,2,1,0:T(8,128)(2,1)}, bf16[2,2,2,2,96,768]{5,4,3,2,1,0:T(8,128)(2,1)}, u32[]{:S(2)}, u32[]{:S(2)}) collective-permute-start(bf16[2,2,2,2,96,768]{5,4,3,2,1,0:T(8,128)(2,1)} %pad_maximum_fusion.4), channel_id=1, source_target_pairs={{0,2},{2,0},{1,3},{3,1},{4,6},{6,4},{5,7},{7,5},{8,10},{10,8},{9,1... | collective-permute-start | bytes 7077896 | tf_op jit(solution)/shard_map/ppermute | solution.py:87
  95.9 14.1 %collective-permute-start.31 = (bf16[768]{0:T(1024)(128)(2,1)S(1)}, bf16[768]{0:T(1024)(128)(2,1)S(1)}, u32[]{:S(2)}, u32[]{:S(2)}) collective-permute-start(bf16[768]{0:T(1024)(128)(2,1)S(1)} %get-tuple-element.57), channel_id=1, source_target_pairs={{0,1},{1,2},{2,3},{3,4},{4,5},{5,6},{6,7},{7,8},{8,9},{9,10},{10,1... | collective-permute-start | bytes 4616 | tf_op jit(solution)/shard_map/ppermute | solution.py:195
  96.4 13.5 %collective-permute-start.30 = (bf16[768]{0:T(1024)(128)(2,1)S(1)}, bf16[768]{0:T(1024)(128)(2,1)S(1)}, u32[]{:S(2)}, u32[]{:S(2)}) collective-permute-start(bf16[768]{0:T(1024)(128)(2,1)S(1)} %get-tuple-element.58), channel_id=1, source_target_pairs={{1,0},{2,1},{3,2},{4,3},{5,4},{6,5},{7,6},{8,7},{9,8},{10,9},{11,1... | collective-permute-start | bytes 4616 | tf_op jit(solution)/shard_map/ppermute | solution.py:196
  106.9 56.2 %collective-permute-start.14 = (bf16[2,2,2,2,104,768]{5,4,3,2,1,0:T(8,128)(2,1)}, bf16[2,2,2,2,104,768]{5,4,3,2,1,0:T(8,128)(2,1)}, u32[]{:S(2)}, u32[]{:S(2)}) collective-permute-start(bf16[2,2,2,2,104,768]{5,4,3,2,1,0:T(8,128)(2,1)} %pad_maximum_fusion.3), channel_id=1, source_target_pairs={{0,2},{2,0},{1,3},{3,1},{4,6},{6,4},{5,7},{7,5},{8,10},{10,8},{9,1... | collective-permute-start | bytes 7667720 | tf_op jit(solution)/shard_map/ppermute | solution.py:87
  172.4 73.5 %copy-start.54 = (f32[768]{0:T(1024)}, f32[768]{0:T(1024)S(1)}, u32[]{:S(2)}) copy-start(f32[768]{0:T(1024)S(1)} %get-tuple-element.127) | copy-start | bytes 9220
  247.4 5.1 collective-permute-start.15
  248.3 4.2 collective-permute-start.20
  252.5 5.0 collective-permute-start.25
  254.4 4.4 collective-permute-start.21
  254.5 5.5 collective-permute-start.16
  257.5 4.4 collective-permute-start.26
  258.9 7.8 %collective-permute-start.22 = (bf16[2,2,72,256]{3,2,1,0:T(8,128)(2,1)S(1)}, bf16[2,2,72,256]{3,2,1,0:T(8,128)(2,1)S(1)}, u32[]{:S(2)}, u32[]{:S(2)}) collective-permute-start(bf16[2,2,72,256]{3,2,1,0:T(8,128)(2,1)S(1)} %pad_maximum_fusion.22), channel_id=1, source_target_pairs={{0,16},{16,0},{1,17},{17,1},{2,18},{18,2},{3,19},{19,3},{4,20},{20... | collective-permute-start | bytes 442376 | tf_op jit(solution)/shard_map/ppermute | solution.py:87
  260.0 6.8 %collective-permute-start.17 = (bf16[2,2,72,256]{3,2,1,0:T(8,128)(2,1)S(1)}, bf16[2,2,72,256]{3,2,1,0:T(8,128)(2,1)S(1)}, u32[]{:S(2)}, u32[]{:S(2)}) collective-permute-start(bf16[2,2,72,256]{3,2,1,0:T(8,128)(2,1)S(1)} %pad_maximum_fusion.21), channel_id=1, source_target_pairs={{0,1},{1,0},{2,3},{3,2},{4,5},{5,4},{6,7},{7,6},{8,9},{9,8},{10,11... | collective-permute-start | bytes 442376 | tf_op jit(solution)/shard_map/ppermute | solution.py:87
  262.0 6.5 %collective-permute-start.27 = (bf16[2,2,72,256]{3,2,1,0:T(8,128)(2,1)S(1)}, bf16[2,2,72,256]{3,2,1,0:T(8,128)(2,1)S(1)}, u32[]{:S(2)}, u32[]{:S(2)}) collective-permute-start(bf16[2,2,72,256]{3,2,1,0:T(8,128)(2,1)S(1)} %pad_maximum_fusion.23), channel_id=1, source_target_pairs={{0,4},{4,0},{1,5},{5,1},{2,6},{6,2},{3,7},{7,3},{8,12},{12,8},{9,1... | collective-permute-start | bytes 442376 | tf_op jit(solution)/shard_map/ppermute | solution.py:87
  266.7 6.8 %collective-permute-start.23 = (bf16[2,2,2,72,256]{4,3,2,1,0:T(8,128)(2,1)S(1)}, bf16[2,2,2,72,256]{4,3,2,1,0:T(8,128)(2,1)S(1)}, u32[]{:S(2)}, u32[]{:S(2)}) collective-permute-start(bf16[2,2,2,72,256]{4,3,2,1,0:T(8,128)(2,1)S(1)} %pad_maximum_fusion.19), channel_id=1, source_target_pairs={{0,8},{8,0},{1,9},{9,1},{2,10},{10,2},{3,11},{11,3},{4,12},{12,4},... | collective-permute-start | bytes 884744 | tf_op jit(solution)/shard_map/ppermute | solution.py:87
  266.9 6.8 %collective-permute-start.18 = (bf16[2,2,2,72,256]{4,3,2,1,0:T(8,128)(2,1)S(1)}, bf16[2,2,2,72,256]{4,3,2,1,0:T(8,128)(2,1)S(1)}, u32[]{:S(2)}, u32[]{:S(2)}) collective-permute-start(bf16[2,2,2,72,256]{4,3,2,1,0:T(8,128)(2,1)S(1)} %pad_maximum_fusion.18), channel_id=1, source_target_pairs={{0,4},{4,0},{1,5},{5,1},{2,6},{6,2},{3,7},{7,3},{8,12},{12,8},{9,1... | collective-permute-start | bytes 884744 | tf_op jit(solution)/shard_map/ppermute | solution.py:87
  268.5 6.8 %collective-permute-start.28 = (bf16[2,2,2,72,256]{4,3,2,1,0:T(8,128)(2,1)S(1)}, bf16[2,2,2,72,256]{4,3,2,1,0:T(8,128)(2,1)S(1)}, u32[]{:S(2)}, u32[]{:S(2)}) collective-permute-start(bf16[2,2,2,72,256]{4,3,2,1,0:T(8,128)(2,1)S(1)} %pad_maximum_fusion.20), channel_id=1, source_target_pairs={{0,1},{1,0},{2,3},{3,2},{4,5},{5,4},{6,7},{7,6},{8,9},{9,8},{10,11... | collective-permute-start | bytes 884744 | tf_op jit(solution)/shard_map/ppermute | solution.py:87
  273.6 2.1 collective-permute-start.24
  273.9 2.7 collective-permute-start.19
  275.4 2.1 collective-permute-start.29
  287.9 18.7 %all-to-all-start = ((f32[32,32,128]{2,1,0:T(8,128)}), f32[32,32,128]{2,1,0:T(8,128)S(1)}, u32[]{:S(2)}, u32[]{:S(2)}) async-start(f32[32,32,128]{2,1,0:T(8,128)} %broadcast_in_dim.168), calls=%async_computation | async-start | bytes 1048576 | tf_op jit(solution)/shard_map/all_to_all | solution.py:284
  319.8 2.7 collective-permute-start.42
  321.3 2.5 collective-permute-start.32
  321.7 3.6 collective-permute-start.37
  322.7 8.7 %collective-permute-start.43 = (bf16[2,2,2,64,256]{4,3,0,1,2:T(8,128)(2,1)S(1)}, bf16[2,2,2,64,256]{4,3,0,1,2:T(8,128)(2,1)S(1)}, u32[]{:S(2)}, u32[]{:S(2)}) collective-permute-start(bf16[2,2,2,64,256]{4,3,0,1,2:T(8,128)(2,1)S(1)} %dynamic-slice_bitcast_fusion.9), channel_id=1, source_target_pairs={{0,1},{1,0},{2,3},{3,2},{4,5},{5,4},{6,7},{7,6},{8,9},{9,8},{10,11... | collective-permute-start | bytes 786440 | tf_op jit(solution)/shard_map/ppermute | solution.py:87
  324.1 8.4 %collective-permute-start.33 = (bf16[2,2,2,64,256]{4,3,0,1,2:T(8,128)(2,1)S(1)}, bf16[2,2,2,64,256]{4,3,0,1,2:T(8,128)(2,1)S(1)}, u32[]{:S(2)}, u32[]{:S(2)}) collective-permute-start(bf16[2,2,2,64,256]{4,3,0,1,2:T(8,128)(2,1)S(1)} %dynamic-slice_bitcast_fusion.11), channel_id=1, source_target_pairs={{0,4},{4,0},{1,5},{5,1},{2,6},{6,2},{3,7},{7,3},{8,12},{12,8},{9,1... | collective-permute-start | bytes 786440 | tf_op jit(solution)/shard_map/ppermute | solution.py:87
  325.5 8.2 %collective-permute-start.38 = (bf16[2,2,2,64,256]{4,3,2,1,0:T(8,128)(2,1)S(1)}, bf16[2,2,2,64,256]{4,3,2,1,0:T(8,128)(2,1)S(1)}, u32[]{:S(2)}, u32[]{:S(2)}) collective-permute-start(bf16[2,2,2,64,256]{4,3,2,1,0:T(8,128)(2,1)S(1)} %dynamic-slice_bitcast_fusion.10), channel_id=1, source_target_pairs={{0,8},{8,0},{1,9},{9,1},{2,10},{10,2},{3,11},{11,3},{4,12},{12,4},... | collective-permute-start | bytes 786440 | tf_op jit(solution)/shard_map/ppermute | solution.py:87
  331.4 5.0 collective-permute-start.44
  332.6 5.0 collective-permute-start.34
  333.8 8.0 %collective-permute-start.39 = (bf16[2,2,64,256]{3,2,1,0:T(8,128)(2,1)S(1)}, bf16[2,2,64,256]{3,2,1,0:T(8,128)(2,1)S(1)}, u32[]{:S(2)}, u32[]{:S(2)}) collective-permute-start(bf16[2,2,64,256]{3,2,1,0:T(8,128)(2,1)S(1)} %dynamic-slice_bitcast_fusion.16), channel_id=1, source_target_pairs={{0,16},{16,0},{1,17},{17,1},{2,18},{18,2},{3,19},{19,3},{4,20},{20... | collective-permute-start | bytes 393224 | tf_op jit(solution)/shard_map/ppermute | solution.py:87
  336.5 6.3 %collective-permute-start.45 = (bf16[2,64,256]{2,1,0:T(8,128)(2,1)S(1)}, bf16[2,64,256]{2,1,0:T(8,128)(2,1)S(1)}, u32[]{:S(2)}, u32[]{:S(2)}) collective-permute-start(bf16[2,64,256]{2,1,0:T(8,128)(2,1)S(1)} %dynamic-slice_bitcast_fusion.18), channel_id=1, source_target_pairs={{0,8},{8,0},{1,9},{9,1},{2,10},{10,2},{3,11},{11,3},{4,12},{12,4},... | collective-permute-start | bytes 196616 | tf_op jit(solution)/shard_map/ppermute | solution.py:87
  337.7 5.4 collective-permute-start.35
  341.9 4.3 collective-permute-start.40
  342.9 4.9 collective-permute-start.46
  343.1 5.1 collective-permute-start.36
  346.3 4.0 collective-permute-start.41
  442.9 19.1 %collective-permute-start.47 = (bf16[2,2,2,2,96,768]{5,4,0,1,3,2:T(8,128)(2,1)}, bf16[2,2,2,2,96,768]{5,4,0,1,3,2:T(8,128)(2,1)}, u32[]{:S(2)}, u32[]{:S(2)}) collective-permute-start(bf16[2,2,2,2,96,768]{5,4,0,1,3,2:T(8,128)(2,1)} %bitcast.439), channel_id=1, source_target_pairs={{0,2},{2,0},{1,3},{3,1},{4,6},{6,4},{5,7},{7,5},{8,10},{10,8},{9,1... | collective-permute-start | bytes 7077896 | tf_op jit(solution)/shard_map/ppermute | solution.py:87
  446.2 21.0 %collective-permute-start.52 = (bf16[2,2,2,2,96,768]{5,4,3,2,0,1:T(8,128)(2,1)}, bf16[2,2,2,2,96,768]{5,4,3,2,0,1:T(8,128)(2,1)}, u32[]{:S(2)}, u32[]{:S(2)}) collective-permute-start(bf16[2,2,2,2,96,768]{5,4,3,2,0,1:T(8,128)(2,1)} %bitcast.438), channel_id=1, source_target_pairs={{0,2},{2,0},{1,3},{3,1},{4,6},{6,4},{5,7},{7,5},{8,10},{10,8},{9,1... | collective-permute-start | bytes 7077896 | tf_op jit(solution)/shard_map/ppermute | solution.py:87
  448.4 22.5 %collective-permute-start.57 = (bf16[2,2,2,2,104,768]{5,4,3,2,1,0:T(8,128)(2,1)}, bf16[2,2,2,2,104,768]{5,4,3,2,1,0:T(8,128)(2,1)}, u32[]{:S(2)}, u32[]{:S(2)}) collective-permute-start(bf16[2,2,2,2,104,768]{5,4,3,2,1,0:T(8,128)(2,1)} %fusion.42), channel_id=1, source_target_pairs={{0,2},{2,0},{1,3},{3,1},{4,6},{6,4},{5,7},{7,5},{8,10},{10,8},{9,1... | collective-permute-start | bytes 7667720 | tf_op jit(solution)/shard_map/ppermute | solution.py:87
  466.2 28.7 %collective-permute-start.48 = (bf16[2,2,2,96,768]{4,3,0,1,2:T(8,128)(2,1)}, bf16[2,2,2,96,768]{4,3,0,1,2:T(8,128)(2,1)}, u32[]{:S(2)}, u32[]{:S(2)}) collective-permute-start(bf16[2,2,2,96,768]{4,3,0,1,2:T(8,128)(2,1)} %dynamic-slice_bitcast_fusion.2), channel_id=1, source_target_pairs={{0,4},{4,0},{1,5},{5,1},{2,6},{6,2},{3,7},{7,3},{8,12},{12,8},{9,1... | collective-permute-start | bytes 3538952 | tf_op jit(solution)/shard_map/ppermute | solution.py:87
  470.9 28.7 %collective-permute-start.53 = (bf16[2,2,2,96,768]{4,3,2,1,0:T(8,128)(2,1)}, bf16[2,2,2,96,768]{4,3,2,1,0:T(8,128)(2,1)}, u32[]{:S(2)}, u32[]{:S(2)}) collective-permute-start(bf16[2,2,2,96,768]{4,3,2,1,0:T(8,128)(2,1)} %dynamic-slice_bitcast_fusion.1), channel_id=1, source_target_pairs={{0,8},{8,0},{1,9},{9,1},{2,10},{10,2},{3,11},{11,3},{4,12},{12,4},... | collective-permute-start | bytes 3538952 | tf_op jit(solution)/shard_map/ppermute | solution.py:87
  474.7 31.1 %collective-permute-start.58 = (bf16[2,2,2,104,768]{4,3,2,1,0:T(8,128)(2,1)}, bf16[2,2,2,104,768]{4,3,2,1,0:T(8,128)(2,1)S(1)}, u32[]{:S(2)}, u32[]{:S(2)}) collective-permute-start(bf16[2,2,2,104,768]{4,3,2,1,0:T(8,128)(2,1)} %dynamic-slice_bitcast_fusion), channel_id=1, source_target_pairs={{0,1},{1,0},{2,3},{3,2},{4,5},{5,4},{6,7},{7,6},{8,9},{9,8},{10,11... | collective-permute-start | bytes 3833864 | tf_op jit(solution)/shard_map/ppermute | solution.py:87
  496.6 21.5 %collective-permute-start.49 = (bf16[2,2,96,768]{3,2,0,1:T(8,128)(2,1)S(1)}, bf16[2,2,96,768]{3,2,0,1:T(8,128)(2,1)S(1)}, u32[]{:S(2)}, u32[]{:S(2)}) collective-permute-start(bf16[2,2,96,768]{3,2,0,1:T(8,128)(2,1)S(1)} %dynamic-slice_bitcast_fusion.5), channel_id=1, source_target_pairs={{0,1},{1,0},{2,3},{3,2},{4,5},{5,4},{6,7},{7,6},{8,9},{9,8},{10,11... | collective-permute-start | bytes 1769480 | tf_op jit(solution)/shard_map/ppermute | solution.py:87
  501.2 28.6 %collective-permute-start.54 = (bf16[2,2,96,768]{3,2,1,0:T(8,128)(2,1)S(1)}, bf16[2,2,96,768]{3,2,1,0:T(8,128)(2,1)S(1)}, u32[]{:S(2)}, u32[]{:S(2)}) collective-permute-start(bf16[2,2,96,768]{3,2,1,0:T(8,128)(2,1)S(1)} %dynamic-slice_bitcast_fusion.4), channel_id=1, source_target_pairs={{0,16},{16,0},{1,17},{17,1},{2,18},{18,2},{3,19},{19,3},{4,20},{20... | collective-permute-start | bytes 1769480 | tf_op jit(solution)/shard_map/ppermute | solution.py:87
  506.2 32.8 %collective-permute-start.59 = (bf16[2,2,104,768]{3,2,1,0:T(8,128)(2,1)S(1)}, bf16[2,2,104,768]{3,2,1,0:T(8,128)(2,1)S(1)}, u32[]{:S(2)}, u32[]{:S(2)}) collective-permute-start(bf16[2,2,104,768]{3,2,1,0:T(8,128)(2,1)S(1)} %dynamic-slice_bitcast_fusion.3), channel_id=1, source_target_pairs={{0,4},{4,0},{1,5},{5,1},{2,6},{6,2},{3,7},{7,3},{8,12},{12,8},{9,1... | collective-permute-start | bytes 1916936 | tf_op jit(solution)/shard_map/ppermute | solution.py:87
  518.3 17.8 %collective-permute-start.50 = (bf16[2,96,768]{2,1,0:T(8,128)(2,1)S(1)}, bf16[2,96,768]{2,1,0:T(8,128)(2,1)S(1)}, u32[]{:S(2)}, u32[]{:S(2)}) collective-permute-start(bf16[2,96,768]{2,1,0:T(8,128)(2,1)S(1)} %dynamic-slice_bitcast_fusion.8), channel_id=1, source_target_pairs={{0,8},{8,0},{1,9},{9,1},{2,10},{10,2},{3,11},{11,3},{4,12},{12,4},... | collective-permute-start | bytes 884744 | tf_op jit(solution)/shard_map/ppermute | solution.py:87
  530.0 8.9 %collective-permute-start.55 = (bf16[2,96,768]{2,1,0:T(8,128)(2,1)S(1)}, bf16[2,96,768]{2,1,0:T(8,128)(2,1)S(1)}, u32[]{:S(2)}, u32[]{:S(2)}) collective-permute-start(bf16[2,96,768]{2,1,0:T(8,128)(2,1)S(1)} %dynamic-slice_bitcast_fusion.7), channel_id=1, source_target_pairs={{0,4},{4,0},{1,5},{5,1},{2,6},{6,2},{3,7},{7,3},{8,12},{12,8},{9,1... | collective-permute-start | bytes 884744 | tf_op jit(solution)/shard_map/ppermute | solution.py:87
  536.1 9.0 %collective-permute-start.51 = (bf16[96,768]{1,0:T(8,128)(2,1)S(1)}, bf16[96,768]{1,0:T(8,128)(2,1)S(1)}, u32[]{:S(2)}, u32[]{:S(2)}) collective-permute-start(bf16[96,768]{1,0:T(8,128)(2,1)S(1)} %dynamic-slice_bitcast_fusion.14), channel_id=1, source_target_pairs={{0,16},{16,0},{1,17},{17,1},{2,18},{18,2},{3,19},{19,3},{4,20},{20... | collective-permute-start | bytes 442376 | tf_op jit(solution)/shard_map/ppermute | solution.py:87
  539.2 11.7 %collective-permute-start.60 = (bf16[2,104,768]{2,1,0:T(8,128)(2,1)S(1)}, bf16[2,104,768]{2,1,0:T(8,128)(2,1)S(1)}, u32[]{:S(2)}, u32[]{:S(2)}) collective-permute-start(bf16[2,104,768]{2,1,0:T(8,128)(2,1)S(1)} %dynamic-slice_bitcast_fusion.6), channel_id=1, source_target_pairs={{0,8},{8,0},{1,9},{9,1},{2,10},{10,2},{3,11},{11,3},{4,12},{12,4},... | collective-permute-start | bytes 958472 | tf_op jit(solution)/shard_map/ppermute | solution.py:87
  539.4 11.7 %collective-permute-start.56 = (bf16[96,768]{1,0:T(8,128)(2,1)S(1)}, bf16[96,768]{1,0:T(8,128)(2,1)S(1)}, u32[]{:S(2)}, u32[]{:S(2)}) collective-permute-start(bf16[96,768]{1,0:T(8,128)(2,1)S(1)} %dynamic-slice_bitcast_fusion.13), channel_id=1, source_target_pairs={{0,1},{1,0},{2,3},{3,2},{4,5},{5,4},{6,7},{7,6},{8,9},{9,8},{10,11... | collective-permute-start | bytes 442376 | tf_op jit(solution)/shard_map/ppermute | solution.py:87
  551.0 8.4 %collective-permute-start.61 = (bf16[104,768]{1,0:T(8,128)(2,1)S(1)}, bf16[104,768]{1,0:T(8,128)(2,1)S(1)}, u32[]{:S(2)}, u32[]{:S(2)}) collective-permute-start(bf16[104,768]{1,0:T(8,128)(2,1)S(1)} %dynamic-slice_bitcast_fusion.12), channel_id=1, source_target_pairs={{0,16},{16,0},{1,17},{17,1},{2,18},{18,2},{3,19},{19,3},{4,20},{20... | collective-permute-start | bytes 479240 | tf_op jit(solution)/shard_map/ppermute | solution.py:87
  (97 other events, 861.3 us)

commit v2 on v1

--- a/solution.py
+++ b/solution.py
@@ -4,6 +4,8 @@
 import jax
 import jax.numpy as jnp
 from jax import lax
+from jax.experimental import pallas as pl
+from jax.experimental.pallas import tpu as pltpu
 from jax.sharding import Mesh, PartitionSpec as P
 
 D = 768
@@ -117,10 +119,527 @@
     outer = [name for name in names if name != core]
     count = len(outer)
     if count == 4:
-        picks = ((0, 1, 3, 2), (3, 2, 0, 1), (0, 1, 2, 3))
+        picks = ((0, 3, 2, 1), (0, 2, 3, 1), (0, 2, 1, 3))
         return [[outer[k] for k in pick] + [core] for pick in picks]
     step = max(1, count // 3)
     return [outer[step * k :] + outer[: step * k] + [core] for k in range(3)]
+
+
+def device_mask(name, names):
+    return 1 << (len(names) - 1 - names.index(name))
+
+
+def gather_relative(shard, order, names):
+    grown, masks = shard[None], [0]
+    for name in order[:-2]:
+        grown = jnp.concatenate([grown, flip(grown, name)])
+        masks = masks + [mask | device_mask(name, names) for mask in masks]
+    pieces = [(grown, masks)]
+    for name in order[-2:]:
+        bit = device_mask(name, names)
+        pieces = pieces + [(flip(piece, name), [mask | bit for mask in own]) for piece, own in pieces]
+    return pieces
+
+
+def reduce_relative(keep, send, order):
+    for name in order:
+        other = flip(send, name)
+        half = keep.shape[0] // 2
+        total = [
+            keep[part].astype(jnp.float32) + other[part].astype(jnp.float32)
+            for part in ((slice(half, None), slice(0, half)) if half else (slice(0, None),))
+        ]
+        if half:
+            send, keep = (value.astype(keep.dtype) for value in total)
+    return total[0][0]
+
+
+def dot_nn(left, right):
+    return lax.dot_general(
+        left, right, (((1,), (0,)), ((), ())), preferred_element_type=jnp.float32
+    )
+
+
+def interleave(count, rows):
+    span = rows // count
+    to = lax.broadcasted_iota(jnp.int32, (rows, rows), 0)
+    source = lax.broadcasted_iota(jnp.int32, (rows, rows), 1)
+    return (source == count * lax.rem(to, span) + lax.div(to, span)).astype(jnp.bfloat16)
+
+
+def valid_rows(len_ref, rows, seq_here):
+    length = rows // seq_here
+    row = lax.broadcasted_iota(jnp.int32, (rows, 1), 0)
+    valid = jnp.zeros((rows, 1), jnp.float32)
+    for seq in range(seq_here):
+        inside = (row >= seq * length) & (row < seq * length + len_ref[seq])
+        valid = jnp.where(inside, 1.0, valid)
+    return valid
+
+
+def stack_pair(value):
+    lane = lax.broadcasted_iota(jnp.int32, value.shape, 1)
+    zero = jnp.zeros_like(value)
+    left = lane < HEAD_DIM
+    return jnp.concatenate([jnp.where(left, value, zero), jnp.where(left, zero, value)], axis=0)
+
+
+def join_pair(stacked):
+    half = stacked.shape[0] // 2
+    lane = lax.broadcasted_iota(jnp.int32, (half, stacked.shape[1]), 1)
+    return jnp.where(lane < HEAD_DIM, stacked[:half], stacked[half:])
+
+
+def pair_scores(stacked, keys, limit):
+    raw = contract_cols(stacked, keys) * HEAD_DIM ** (-0.5)
+    column = lax.broadcasted_iota(jnp.int32, raw.shape, 1)
+    return jnp.where(column < limit, raw, -1e30)
+
+
+def center_rows(resid):
+    center = resid - jnp.mean(resid, axis=-1, keepdims=True)
+    inverse = lax.rsqrt(jnp.mean(center * center, axis=-1, keepdims=True) + norm_eps)
+    return center * inverse, inverse
+
+
+def gelu_phi(value):
+    return 0.5 * (1.0 + lax.erf(value * 0.7071067811865476))
+
+
+def forward_kernel(plan, seq_here, *refs):
+    me_ref, len_ref, place_ref, x_ref, vec_ref = refs[:5]
+    blocks = refs[5 : 5 + len(plan)]
+    heads_ref, wall_ref, qkv_ref, att_ref, n1_ref, pre_ref, n2_ref, stat_ref = refs[
+        5 + len(plan) : 13 + len(plan)
+    ]
+    raw, turned, in_sem, out_sem = refs[13 + len(plan) :]
+    rows, width = x_ref.shape
+    length = rows // seq_here
+    pairs = width // (2 * HEAD_DIM)
+    me = me_ref[0]
+    for (part, unit, masks), block in zip(plan, blocks):
+        for place, mask in enumerate(masks):
+            row = pl.multiple_of((3 * (me ^ mask) + part) * unit, 16)
+            pltpu.make_async_copy(block.at[place], raw.at[pl.ds(row, unit)], in_sem).start()
+    valid = valid_rows(len_ref, rows, seq_here)
+    x = (x_ref[...].astype(jnp.float32) * valid).astype(jnp.bfloat16)
+    pltpu.make_async_copy(raw, raw, in_sem).wait()
+
+    split3, split4 = interleave(3, 384), interleave(4, 256)
+    for b in range(width // 128):
+        block = dot_nn(split3, raw[384 * b : 384 * b + 384, :]).astype(jnp.bfloat16)
+        for p in range(3):
+            turned[width * p + 128 * b : width * p + 128 * b + 128, :] = block[
+                128 * p : 128 * p + 128
+            ]
+    up = 4 * width
+    for b in range(width // 64):
+        block = dot_nn(split4, raw[up + 256 * b : up + 256 * b + 256, :]).astype(jnp.bfloat16)
+        for p in range(4):
+            row = width * (3 + p) + 64 * b
+            turned[row : row + 64, :] = block[64 * p : 64 * p + 64]
+    saves = [
+        pltpu.make_async_copy(source, target, out_sem.at[k])
+        for k, (source, target) in enumerate(
+            (
+                (turned.at[0 : 3 * width], wall_ref.at[0 : 3 * width]),
+                (raw.at[3 * width : up], wall_ref.at[3 * width : up]),
+                (turned.at[3 * width : 7 * width], wall_ref.at[up : 2 * up]),
+                (raw.at[2 * up : 3 * up], wall_ref.at[2 * up : 3 * up]),
+            )
+        )
+    ]
+    for save in saves:
+        save.start()
+
+    for p, bias in ((0, 0), (1, None), (2, 1)):
+        value = dot_nn(x, turned[width * p : width * (p + 1), :])
+        if bias is not None:
+            value = value + vec_ref[bias : bias + 1, :]
+        qkv_ref[:, width * p : width * (p + 1)] = value.astype(jnp.bfloat16)
+
+    stats = jnp.zeros((2 * length, 128), jnp.float32)
+    lane = lax.broadcasted_iota(jnp.int32, stats.shape, 1)
+    for seq in range(seq_here):
+        here = slice(seq * length, (seq + 1) * length)
+        for g in range(pairs):
+            cols = [slice(width * p + 128 * g, width * p + 128 * g + 128) for p in range(3)]
+            query, key, value = (qkv_ref[here, c] for c in cols)
+            scores = pair_scores(stack_pair(query), key, len_ref[seq])
+            top = jnp.max(scores, axis=-1, keepdims=True)
+            expo = jnp.exp(scores - top)
+            total = jnp.sum(expo, axis=-1, keepdims=True)
+            stats = jnp.where(lane == seq * pairs + g, top + jnp.log(total), stats)
+            probs = (expo / total).astype(jnp.bfloat16)
+            att_ref[here, 128 * g : 128 * g + 128] = join_pair(dot_nn(probs, value)).astype(
+                jnp.bfloat16
+            )
+
+    branch = dot_nn(att_ref[...], raw[3 * width : up, :]) + vec_ref[2:3, :]
+    normed, inverse = center_rows(x.astype(jnp.float32) + branch)
+    n1_ref[...] = normed
+    stat_one = seq_here * pairs
+    hidden = normed * vec_ref[3:4, :] + vec_ref[4:5, :]
+    hidden_low = hidden.astype(jnp.bfloat16)
+    total = hidden + vec_ref[9:10, :]
+    for p in range(4):
+        pre = dot_nn(hidden_low, turned[width * (3 + p) : width * (4 + p), :])
+        pre = pre + vec_ref[5 + p : 6 + p, :]
+        pre_ref[:, width * p : width * (p + 1)] = pre
+        act = (pre * gelu_phi(pre)).astype(jnp.bfloat16)
+        total = total + dot_nn(act, raw[2 * up + width * p : 2 * up + width * (p + 1), :])
+    normed, inverse_two = center_rows(total)
+    n2_ref[...] = normed
+    wide = lax.broadcasted_iota(jnp.int32, (rows, 128), 1)
+    ends = jnp.where(
+        wide == stat_one, inverse, jnp.where(wide == stat_one + 1, inverse_two, 0.0)
+    )
+    stat_ref[0] = stats
+    stat_ref[1] = ends
+    output = ((normed * vec_ref[10:11, :] + vec_ref[11:12, :]) * valid).astype(jnp.bfloat16)
+    spot = lax.broadcasted_iota(jnp.int32, (place_ref.shape[0], rows), 1)
+    choose = (spot == place_ref[...]).astype(jnp.bfloat16)
+    heads_ref[...] = dot_nn(choose, output).astype(jnp.bfloat16)
+    for save in saves:
+        save.wait()
+
+
+def backward_kernel(plan, unit, seq_here, *refs):
+    me_ref, len_ref, place_ref, x_ref, vec_ref, top_ref = refs[:6]
+    wall_ref, qkv_ref, att_ref, n1_ref, pre_ref, n2_ref, stat_ref = refs[6:13]
+    gin_ref, dvec_ref = refs[13:15]
+    sinks = refs[15:21]
+    wall, grads, parts, dqkv, in_sem, out_sem = refs[21:]
+    rows, width = x_ref.shape
+    length = rows // seq_here
+    pairs = width // (2 * HEAD_DIM)
+    low = jnp.bfloat16
+    me = me_ref[0]
+    up = 4 * width
+    loads = [
+        pltpu.make_async_copy(wall_ref.at[a:b], wall.at[a:b], in_sem.at[k])
+        for k, (a, b) in enumerate(((2 * up, 3 * up), (up, 2 * up), (0, up)))
+    ]
+    for load in loads:
+        load.start()
+
+    def emit(first, last):
+        for u in range(first // unit, last // unit):
+            part = u % 3
+            relative = (u // 3) ^ me
+            spot = jnp.int32(0)
+            bits, core_bit = plan[part]
+            for k, bit in enumerate(bits):
+                spot = spot + jnp.where((relative & bit) != 0, 1 << (len(bits) - 1 - k), 0)
+            across = (relative & core_bit) != 0
+            source = grads.at[u * unit : (u + 1) * unit]
+
+            @pl.when(across)
+            def _(part=part, source=source, spot=spot):
+                pltpu.make_async_copy(
+                    source, sinks[2 * part + 1].at[spot], out_sem.at[2 * part + 1]
+                ).start()
+
+            @pl.when(jnp.logical_not(across))
+            def _(part=part, source=source, spot=spot):
+                pltpu.make_async_copy(
+                    source, sinks[2 * part].at[spot], out_sem.at[2 * part]
+                ).start()
+
+    valid = valid_rows(len_ref, rows, seq_here)
+    x = (x_ref[...].astype(jnp.float32) * valid).astype(low)
+    stat_one = seq_here * pairs
+    wide = lax.broadcasted_iota(jnp.int32, (rows, 128), 1)
+    ends = stat_ref[1]
+    inverse_one = jnp.sum(jnp.where(wide == stat_one, ends, 0.0), axis=-1, keepdims=True)
+    inverse_two = jnp.sum(jnp.where(wide == stat_one + 1, ends, 0.0), axis=-1, keepdims=True)
+
+    spot = lax.broadcasted_iota(jnp.int32, (rows, place_ref.shape[1]), 0)
+    choose = (spot == place_ref[...]).astype(jnp.float32)
+    d_output = valid * lax.dot_general(
+        choose,
+        top_ref[...],
+        (((1,), (0,)), ((), ())),
+        precision=lax.Precision.HIGHEST,
+        preferred_element_type=jnp.float32,
+    )
+    normed = n2_ref[...]
+
+    def sums(row, value):
+        dvec_ref[row : row + 1, :] = jnp.sum(value, axis=0, keepdims=True)
+
+    sums(10, d_output * normed)
+    sums(11, d_output)
+    d_resid = norm_back(d_output * vec_ref[10:11, :], normed, inverse_two)
+    d_ffn = d_resid.astype(low)
+    sums(9, d_ffn.astype(jnp.float32))
+    normed = n1_ref[...]
+    hidden_low = (normed * vec_ref[3:4, :] + vec_ref[4:5, :]).astype(low)
+    d_hidden = d_resid
+    for load in loads[:2]:
+        load.wait()
+    for p in range(4):
+        pre = pre_ref[:, width * p : width * (p + 1)]
+        phi = gelu_phi(pre)
+        act = (pre * phi).astype(low)
+        down = slice(2 * up + width * p, 2 * up + width * (p + 1))
+        grads[down, :] = contract_rows(act, d_ffn).astype(low)
+        slope = phi + pre * jnp.exp(-0.5 * pre * pre) * 0.3989422804014327
+        d_pre = (contract_cols(d_ffn, wall[down, :]) * slope).astype(low)
+        sums(5 + p, d_pre.astype(jnp.float32))
+        parts[width * p : width * (p + 1), :] = contract_rows(hidden_low, d_pre).astype(low)
+        d_hidden = d_hidden + contract_cols(d_pre, wall[up + width * p : up + width * (p + 1), :])
+    emit(2 * up, 3 * up)
+    split4 = interleave(4, 256)
+    for b in range(width // 64):
+        block = jnp.concatenate(
+            [parts[width * p + 64 * b : width * p + 64 * b + 64, :] for p in range(4)], axis=0
+        )
+        grads[up + 256 * b : up + 256 * b + 256, :] = contract_rows(split4, block).astype(low)
+    emit(up, 2 * up)
+
+    sums(3, d_hidden * normed)
+    sums(4, d_hidden)
+    d_resid = norm_back(d_hidden * vec_ref[3:4, :], normed, inverse_one)
+    d_branch = d_resid.astype(low)
+    sums(2, d_branch.astype(jnp.float32))
+    grads[3 * width : up, :] = contract_rows(att_ref[...], d_branch).astype(low)
+    loads[2].wait()
+    d_att = contract_cols(d_branch, wall[3 * width : up, :]).astype(low)
+    lane = lax.broadcasted_iota(jnp.int32, (2 * length, 128), 1)
+    stats = stat_ref[0]
+    for seq in range(seq_here):
+        here = slice(seq * length, (seq + 1) * length)
+        for g in range(pairs):
+            cols = [slice(width * p + 128 * g, width * p + 128 * g + 128) for p in range(3)]
+            query, key, value = (qkv_ref[here, c] for c in cols)
+            query = stack_pair(query)
+            log_sum = jnp.sum(
+                jnp.where(lane == seq * pairs + g, stats, 0.0), axis=-1, keepdims=True
+            )
+            probs = jnp.exp(pair_scores(query, key, len_ref[seq]) - log_sum)
+            d_heads = stack_pair(d_att[here, 128 * g : 128 * g + 128])
+            d_probs = contract_cols(d_heads, value)
+            dqkv[here, cols[2]] = contract_rows(probs.astype(low), d_heads).astype(low)
+            delta = jnp.sum(d_probs * probs, axis=-1, keepdims=True)
+            d_scores = (probs * (d_probs - delta)).astype(low)
+            scale = HEAD_DIM ** (-0.5)
+            dqkv[here, cols[0]] = (join_pair(dot_nn(d_scores, key)) * scale).astype(low)
+            dqkv[here, cols[1]] = (contract_rows(d_scores, query) * scale).astype(low)
+    sums(0, dqkv[:, :width].astype(jnp.float32))
+    sums(1, dqkv[:, 2 * width :].astype(jnp.float32))
+    total = d_resid
+    for p in range(3):
+        d_part = dqkv[:, width * p : width * (p + 1)]
+        parts[width * p : width * (p + 1), :] = contract_rows(x, d_part).astype(low)
+        total = total + contract_cols(d_part, wall[width * p : width * (p + 1), :])
+    split3 = interleave(3, 384)
+    for b in range(width // 128):
+        block = jnp.concatenate(
+            [parts[width * p + 128 * b : width * p + 128 * b + 128, :] for p in range(3)], axis=0
+        )
+        grads[384 * b : 384 * b + 384, :] = contract_rows(split3, block).astype(low)
+    emit(0, up)
+    gin_ref[...] = total * valid
+    for k, sink in enumerate(sinks):
+        pltpu.make_async_copy(sink, sink, out_sem.at[k]).wait()
+
+
+def call_forward(me, lengths, places, rows, vecs, gathered, seq_here):
+    count, width = rows.shape
+    pieces = [(part, piece, masks) for part, own in enumerate(gathered) for piece, masks in own]
+    plan = tuple((part, piece.shape[1], tuple(masks)) for part, piece, masks in pieces)
+    total = 12 * width
+    vmem = pl.BlockSpec(memory_space=pltpu.VMEM)
+    smem = pl.BlockSpec(memory_space=pltpu.SMEM)
+    hbm = pl.BlockSpec(memory_space=pl.ANY)
+    low, full = jnp.bfloat16, jnp.float32
+    return pl.pallas_call(
+        functools.partial(forward_kernel, plan, seq_here),
+        out_shape=[
+            jax.ShapeDtypeStruct((places.shape[0], width), low),
+            jax.ShapeDtypeStruct((total, width), low),
+            jax.ShapeDtypeStruct((count, 3 * width), low),
+            jax.ShapeDtypeStruct((count, width), low),
+            jax.ShapeDtypeStruct((count, width), full),
+            jax.ShapeDtypeStruct((count, 4 * width), full),
+            jax.ShapeDtypeStruct((count, width), full),
+            jax.ShapeDtypeStruct((2, count, 128), full),
+        ],
+        in_specs=[smem, smem, vmem, vmem, vmem] + [hbm] * len(pieces),
+        out_specs=[vmem, hbm] + [vmem] * 6,
+        scratch_shapes=[
+            pltpu.VMEM((total, width), low),
+            pltpu.VMEM((7 * width, width), low),
+            pltpu.SemaphoreType.DMA,
+            pltpu.SemaphoreType.DMA((4,)),
+        ],
+        compiler_params=pltpu.CompilerParams(vmem_limit_bytes=56 * 2**20),
+        cost_estimate=pl.CostEstimate(
+            flops=2 * count * total * width, bytes_accessed=48 * 2**20, transcendentals=0
+        ),
+    )(me, lengths, places, rows, vecs, *[piece for _, piece, _ in pieces])
+
+
+def call_backward(me, lengths, places, rows, vecs, top, saved, plan, unit, seq_here):
+    count, width = rows.shape
+    total = 12 * width
+    vmem = pl.BlockSpec(memory_space=pltpu.VMEM)
+    smem = pl.BlockSpec(memory_space=pltpu.SMEM)
+    hbm = pl.BlockSpec(memory_space=pl.ANY)
+    low, full = jnp.bfloat16, jnp.float32
+    half = total // unit // 6
+    return pl.pallas_call(
+        functools.partial(backward_kernel, plan, unit, seq_here),
+        out_shape=[
+            jax.ShapeDtypeStruct((count, width), full),
+            jax.ShapeDtypeStruct((12, width), full),
+        ]
+        + [jax.ShapeDtypeStruct((half, unit, width), low)] * 6,
+        in_specs=[smem, smem, vmem, vmem, vmem, vmem, hbm] + [vmem] * 6,
+        out_specs=[vmem, vmem] + [hbm] * 6,
+        scratch_shapes=[
+            pltpu.VMEM((total, width), low),
+            pltpu.VMEM((total, width), low),
+            pltpu.VMEM((4 * width, width), low),
+            pltpu.VMEM((count, 3 * width), low),
+            pltpu.SemaphoreType.DMA((3,)),
+            pltpu.SemaphoreType.DMA((6,)),
+        ],
+        compiler_params=pltpu.CompilerParams(vmem_limit_bytes=60 * 2**20),
+        cost_estimate=pl.CostEstimate(
+            flops=4 * count * total * width, bytes_accessed=48 * 2**20, transcendentals=0
+        ),
+    )(me, lengths, places, rows, vecs, top, *saved)
+
+
+def plain_forward(mats_all, vecs_all, block_input, span_lengths):
+    seq_here, length, width = block_input.shape
+    rows_here = seq_here * length
+    heads_count = width // HEAD_DIM
+    head_scale = HEAD_DIM ** (-0.5)
+    low = jnp.bfloat16
+    w_qkv, w_out, w_up, w_down = split_mats(mats_all)
+    bias_q, bias_v, bias_out, gain_one, shift_one, bias_up, bias_down, gain_two, shift_two = (
+        split_vecs(vecs_all)
+    )
+    valid = jnp.arange(length)[None, :] < span_lengths[:, None]
+    valid_col = valid.reshape(rows_here, 1).astype(jnp.float32)
+    tok_rows = (block_input * valid[:, :, None].astype(low)).reshape(rows_here, width)
+    qkv_bias = jnp.concatenate([bias_q, jnp.zeros((width,), jnp.float32), bias_v])
+    projected = (jnp.dot(tok_rows, w_qkv, preferred_element_type=jnp.float32) + qkv_bias).astype(
+        low
+    )
+    shaped = projected.reshape(seq_here, length, 3, heads_count, HEAD_DIM)
+    queries = shaped[:, :, 0]
+    key_rows = shaped[:, :, 1]
+    value_rows = shaped[:, :, 2]
+    key_valid = valid[:, None, None, :]
+
+    def make_scores():
+        raw = (
+            jnp.einsum("sqhd,skhd->shqk", queries, key_rows, preferred_element_type=jnp.float32)
+            * head_scale
+        )
+        return jnp.where(key_valid, raw, -1e30)
+
+    scores = make_scores()
+    row_max = jnp.max(scores, axis=-1, keepdims=True)
+    expo_vals = jnp.exp(scores - row_max)
+    row_sum = jnp.sum(expo_vals, axis=-1, keepdims=True)
+    row_lse = row_max + jnp.log(row_sum)
+    attn_probs = (expo_vals / row_sum).astype(low)
+    attended = (
+        jnp.einsum("shqk,skhd->sqhd", attn_probs, value_rows, preferred_element_type=jnp.float32)
+        .reshape(rows_here, width)
+        .astype(low)
+    )
+    branch = jnp.dot(attended, w_out, preferred_element_type=jnp.float32) + bias_out
+    normed_one, inverse_one = center_scale(tok_rows.astype(jnp.float32) + branch)
+    hidden_one = normed_one * gain_one + shift_one
+    hidden_low = hidden_one.astype(low)
+    pre_act = jnp.dot(hidden_low, w_up, preferred_element_type=jnp.float32) + bias_up
+    act_low = jax.nn.gelu(pre_act, approximate=False).astype(low)
+    ffn_out = jnp.dot(act_low, w_down, preferred_element_type=jnp.float32) + bias_down
+    normed_two, inverse_two = center_scale(hidden_one + ffn_out)
+    output = (normed_two * gain_two + shift_two) * valid_col
+
+    def plain_backward(d_output):
+        d_gain_two = jnp.sum(d_output * normed_two, axis=0)
+        d_shift_two = jnp.sum(d_output, axis=0)
+        d_resid_two = norm_back(d_output * gain_two, normed_two, inverse_two)
+        d_ffn = d_resid_two.astype(low)
+        d_bias_down = jnp.sum(d_ffn.astype(jnp.float32), axis=0)
+        d_w_down = contract_rows(act_low, d_ffn)
+        d_act = contract_cols(d_ffn, w_down)
+        d_pre = (d_act * gelu_slope(pre_act)).astype(low)
+        d_bias_up = jnp.sum(d_pre.astype(jnp.float32), axis=0)
+        d_w_up = contract_rows(hidden_low, d_pre)
+        d_hidden = contract_cols(d_pre, w_up) + d_resid_two
+        d_gain_one = jnp.sum(d_hidden * normed_one, axis=0)
+        d_shift_one = jnp.sum(d_hidden, axis=0)
+        d_resid_one = norm_back(d_hidden * gain_one, normed_one, inverse_one)
+        d_branch = d_resid_one.astype(low)
+        d_bias_out = jnp.sum(d_branch.astype(jnp.float32), axis=0)
+        d_w_out = contract_rows(attended, d_branch)
+        d_attended = (
+            contract_cols(d_branch, w_out).astype(low).reshape(seq_here, length, heads_count, HEAD_DIM)
+        )
+        probs_again = jnp.exp(make_scores() - row_lse)
+        probs_low = probs_again.astype(low)
+        d_probs = jnp.einsum(
+            "sqhd,skhd->shqk", d_attended, value_rows, preferred_element_type=jnp.float32
+        )
+        d_values = jnp.einsum(
+            "shqk,sqhd->skhd", probs_low, d_attended, preferred_element_type=jnp.float32
+        )
+        row_delta = jnp.sum(d_probs * probs_again, axis=-1, keepdims=True)
+        d_scores = (probs_again * (d_probs - row_delta)).astype(low)
+        d_queries = (
+            jnp.einsum("shqk,skhd->sqhd", d_scores, key_rows, preferred_element_type=jnp.float32)
+            * head_scale
+        )
+        d_keys = (
+            jnp.einsum("shqk,sqhd->skhd", d_scores, queries, preferred_element_type=jnp.float32)
+            * head_scale
+        )
+        d_qkv = jnp.concatenate(
+            [
+                d_queries.reshape(rows_here, width),
+                d_keys.reshape(rows_here, width),
+                d_values.reshape(rows_here, width),
+            ],
+            axis=1,
+        ).astype(low)
+        d_qkv_float = d_qkv.astype(jnp.float32)
+        d_bias_q = jnp.sum(d_qkv_float[:, :width], axis=0)
+        d_bias_v = jnp.sum(d_qkv_float[:, 2 * width :], axis=0)
+        d_w_qkv = contract_rows(tok_rows, d_qkv)
+        grad_input = ((contract_cols(d_qkv, w_qkv) + d_resid_one) * valid_col).reshape(
+            seq_here, length, width
+        )
+        d_mats = jnp.concatenate(
+            [
+                piece.astype(low).reshape(-1, width)
+                for piece in (d_w_qkv, d_w_out, d_w_up, d_w_down)
+            ]
+        )
+        d_vecs = jnp.concatenate(
+            [
+                d_bias_q,
+                d_bias_v,
+                d_bias_out,
+                d_gain_one,
+                d_shift_one,
+                d_bias_up,
+                d_bias_down,
+                d_gain_two,
+                d_shift_two,
+            ]
+        )
+        return grad_input, d_mats, d_vecs
+
+    return output, plain_backward
 
 
 def on_device(
@@ -143,8 +662,6 @@
 ):
     seq_here, length, width = block_input.shape
     rows_here = seq_here * length
-    heads_count = width // HEAD_DIM
-    head_scale = HEAD_DIM ** (-0.5)
     devices = 2 ** len(names)
     me = lax.axis_index(names)
     orders = bit_orders(names, core)
@@ -152,8 +669,8 @@
     picks_here = seq_here * slots
     low = jnp.bfloat16
 
-    mat_rows = layer_mats.shape[0] // width
-    third = mat_rows // 3
+    third = layer_mats.shape[0] // width // 3
+    by_kernel = third % 16 == 0
     vec_here = vectors.shape[0]
     mats_low = layer_mats.astype(low).reshape(3, third, width)
 
@@ -170,13 +687,11 @@
             jnp.zeros((4, width), low),
         ]
     )
-    gathered = [
-        gather_bits(mats_low[0], orders[0], names),
-        gather_bits(mats_low[1], orders[1], names),
-        gather_bits(jnp.concatenate([mats_low[2], small]), orders[2], names),
-    ]
-    small_all = gathered[2][:, third:, :]
-    mats_all = jnp.stack([gathered[0], gathered[1], gathered[2][:, :third, :]], axis=1).reshape(-1)
+    small_all = gather_bits(small, orders[0], names)
+    if by_kernel:
+        gathered = [gather_relative(mats_low[k], orders[k], names) for k in range(3)]
+    else:
+        gathered = [gather_bits(mats_low[k], orders[k], names) for k in range(3)]
     vecs_all = small_all[:, 0, :vec_here].reshape(-1)
     labels_all = (
         small_all[:, 1, :picks_here].astype(jnp.int32) * 256
@@ -212,59 +727,35 @@
     touched = (row_start + width > 0) & (row_start < embed_here)
     table_owned = jnp.where(owned[:, None], table, 0)
 
-    w_qkv, w_out, w_up, w_down = split_mats(mats_all)
-    bias_q, bias_v, bias_out, gain_one, shift_one, bias_up, bias_down, gain_two, shift_two = (
-        split_vecs(vecs_all)
-    )
-    valid = jnp.arange(length)[None, :] < span_lengths[:, None]
-    valid_col = valid.reshape(rows_here, 1).astype(jnp.float32)
-    tok_rows = (block_input * valid[:, :, None].astype(low)).reshape(rows_here, width)
-    qkv_bias = jnp.concatenate([bias_q, jnp.zeros((width,), jnp.float32), bias_v])
-    projected = (jnp.dot(tok_rows, w_qkv, preferred_element_type=jnp.float32) + qkv_bias).astype(
-        low
-    )
-    shaped = projected.reshape(seq_here, length, 3, heads_count, HEAD_DIM)
-    queries = shaped[:, :, 0]
-    key_rows = shaped[:, :, 1]
-    value_rows = shaped[:, :, 2]
-    key_valid = valid[:, None, None, :]
-
-    def make_scores():
-        raw = (
-            jnp.einsum("sqhd,skhd->shqk", queries, key_rows, preferred_element_type=jnp.float32)
-            * head_scale
-        )
-        return jnp.where(key_valid, raw, -1e30)
-
-    scores = make_scores()
-    row_max = jnp.max(scores, axis=-1, keepdims=True)
-    expo_vals = jnp.exp(scores - row_max)
-    row_sum = jnp.sum(expo_vals, axis=-1, keepdims=True)
-    row_lse = row_max + jnp.log(row_sum)
-    attn_probs = (expo_vals / row_sum).astype(low)
-    attended = (
-        jnp.einsum("shqk,skhd->sqhd", attn_probs, value_rows, preferred_element_type=jnp.float32)
-        .reshape(rows_here, width)
-        .astype(low)
-    )
-    branch = jnp.dot(attended, w_out, preferred_element_type=jnp.float32) + bias_out
-    normed_one, inverse_one = center_scale(tok_rows.astype(jnp.float32) + branch)
-    hidden_one = normed_one * gain_one + shift_one
-    hidden_low = hidden_one.astype(low)
-    pre_act = jnp.dot(hidden_low, w_up, preferred_element_type=jnp.float32) + bias_up
-    act_low = jax.nn.gelu(pre_act, approximate=False).astype(low)
-    ffn_out = jnp.dot(act_low, w_down, preferred_element_type=jnp.float32) + bias_down
-    normed_two, inverse_two = center_scale(hidden_one + ffn_out)
-    output = (normed_two * gain_two + shift_two) * valid_col
-    output_seq = output.reshape(seq_here, length, width)
-
-    picked_here = jnp.take_along_axis(output_seq, mlm_positions[:, :, None], axis=1).reshape(
-        -1, width
-    )
-    cls_pad = -seq_here % 8
-    heads_rows = jnp.concatenate(
-        [picked_here, output_seq[:, 0, :], jnp.zeros((cls_pad, width), jnp.float32)]
-    ).astype(low)
+    heads_pad = -(picks_here + seq_here) % 8
+    seq_start = jnp.arange(seq_here, dtype=jnp.int32) * length
+    if by_kernel:
+        lone = me.astype(jnp.int32).reshape(1)
+        tok_rows = block_input.reshape(rows_here, width)
+        vec_rows = vecs_all.astype(jnp.float32).reshape(-1, width)
+        places = jnp.concatenate(
+            [
+                (mlm_positions + seq_start[:, None]).reshape(-1),
+                seq_start,
+                jnp.full((heads_pad,), -1, jnp.int32),
+            ]
+        )
+        heads_rows, *saved = call_forward(
+            lone, span_lengths, places[:, None], tok_rows, vec_rows, gathered, seq_here
+        )
+    else:
+        mats_all = jnp.stack(gathered, axis=1).reshape(-1)
+        output, plain_backward = plain_forward(mats_all, vecs_all, block_input, span_lengths)
+        output_seq = output.reshape(seq_here, length, width)
+        picked_here = jnp.take_along_axis(output_seq, mlm_positions[:, :, None], axis=1)
+        heads_rows = jnp.concatenate(
+            [
+                picked_here.reshape(-1, width),
+                output_seq[:, 0, :],
+                jnp.zeros((heads_pad, width), jnp.float32),
+            ]
+        ).astype(low)
+
     cut = width // 3
     heads_all = jnp.concatenate(
         [
@@ -303,13 +794,6 @@
         axis=1,
     ).astype(jnp.float32)
 
-    select = (mlm_positions[:, :, None] == jnp.arange(length)[None, None, :]).astype(jnp.float32)
-    d_output_seq = jnp.einsum(
-        "gor,gon->grn",
-        select,
-        d_picked.reshape(seq_here, slots, width),
-        precision=lax.Precision.HIGHEST,
-    )
     span_scale = 2.0 / math.sqrt(width)
     columns = jnp.arange(cls_all.shape[0])
     sims = contract_cols(cls_all, cls_all) * span_scale
@@ -323,91 +807,44 @@
         jnp.dot(d_sims_rows, cls_all, preferred_element_type=jnp.float32)
         + contract_rows(d_sims_cols, cls_all)
     ) * span_scale
-    d_output_seq = d_output_seq.at[:, 0, :].add(d_cls)
-    d_output = d_output_seq.reshape(rows_here, width) * valid_col
-    d_gain_two = jnp.sum(d_output * normed_two, axis=0)
-    d_shift_two = jnp.sum(d_output, axis=0)
-    d_resid_two = norm_back(d_output * gain_two, normed_two, inverse_two)
-    d_ffn = d_resid_two.astype(low)
-    d_bias_down = jnp.sum(d_ffn.astype(jnp.float32), axis=0)
-    d_w_down = contract_rows(act_low, d_ffn)
-    d_act = contract_cols(d_ffn, w_down)
-    d_pre = (d_act * gelu_slope(pre_act)).astype(low)
-    d_bias_up = jnp.sum(d_pre.astype(jnp.float32), axis=0)
-    d_w_up = contract_rows(hidden_low, d_pre)
-    d_hidden = contract_cols(d_pre, w_up) + d_resid_two
-    d_gain_one = jnp.sum(d_hidden * normed_one, axis=0)
-    d_shift_one = jnp.sum(d_hidden, axis=0)
-    d_resid_one = norm_back(d_hidden * gain_one, normed_one, inverse_one)
-    d_branch = d_resid_one.astype(low)
-    d_bias_out = jnp.sum(d_branch.astype(jnp.float32), axis=0)
-    d_w_out = contract_rows(attended, d_branch)
-    d_attended = (
-        contract_cols(d_branch, w_out).astype(low).reshape(seq_here, length, heads_count, HEAD_DIM)
-    )
-    probs_again = jnp.exp(make_scores() - row_lse)
-    probs_low = probs_again.astype(low)
-    d_probs = jnp.einsum(
-        "sqhd,skhd->shqk", d_attended, value_rows, preferred_element_type=jnp.float32
-    )
-    d_values = jnp.einsum(
-        "shqk,sqhd->skhd", probs_low, d_attended, preferred_element_type=jnp.float32
-    )
-    row_delta = jnp.sum(d_probs * probs_again, axis=-1, keepdims=True)
-    d_scores = (probs_again * (d_probs - row_delta)).astype(low)
-    d_queries = (
-        jnp.einsum("shqk,skhd->sqhd", d_scores, key_rows, preferred_element_type=jnp.float32)
-        * head_scale
-    )
-    d_keys = (
-        jnp.einsum("shqk,sqhd->skhd", d_scores, queries, preferred_element_type=jnp.float32)
-        * head_scale
-    )
-    d_qkv = jnp.concatenate(
-        [
-            d_queries.reshape(rows_here, width),
-            d_keys.reshape(rows_here, width),
-            d_values.reshape(rows_here, width),
-        ],
-        axis=1,
-    ).astype(low)
-    d_qkv_float = d_qkv.astype(jnp.float32)
-    d_bias_q = jnp.sum(d_qkv_float[:, :width], axis=0)
-    d_bias_v = jnp.sum(d_qkv_float[:, 2 * width :], axis=0)
-    d_w_qkv = contract_rows(tok_rows, d_qkv)
-    grad_input = ((contract_cols(d_qkv, w_qkv) + d_resid_one) * valid_col).reshape(
-        seq_here, length, width
-    )
-
-    d_mats = jnp.concatenate(
-        [
-            piece.astype(low).reshape(-1, width)
-            for piece in (d_w_qkv, d_w_out, d_w_up, d_w_down)
+    if by_kernel:
+        top = jnp.concatenate([d_picked, d_cls, jnp.zeros((heads_pad, width), jnp.float32)])
+        back_orders = [order[::-1] for order in orders]
+        plan = tuple(
+            (
+                tuple(device_mask(name, names) for name in order[1:]),
+                device_mask(order[0], names),
+            )
+            for order in back_orders
+        )
+        grad_input, d_vecs, *sinks = call_backward(
+            lone, span_lengths, places[None], tok_rows, vec_rows, top, saved, plan, third, seq_here
+        )
+        grad_input = grad_input.reshape(seq_here, length, width)
+        summed = [
+            reduce_relative(sinks[2 * k], sinks[2 * k + 1], back_orders[k]) for k in range(3)
         ]
-    ).reshape(devices, 3, third, width)
-    d_vecs = jnp.concatenate(
-        [
-            d_bias_q,
-            d_bias_v,
-            d_bias_out,
-            d_gain_one,
-            d_shift_one,
-            d_bias_up,
-            d_bias_down,
-            d_gain_two,
-            d_shift_two,
+    else:
+        select = (mlm_positions[:, :, None] == jnp.arange(length)[None, None, :]).astype(
+            jnp.float32
+        )
+        d_output_seq = jnp.einsum(
+            "gor,gon->grn",
+            select,
+            d_picked.reshape(seq_here, slots, width),
+            precision=lax.Precision.HIGHEST,
+        )
+        d_output_seq = d_output_seq.at[:, 0, :].add(d_cls)
+        valid = jnp.arange(length)[None, :] < span_lengths[:, None]
+        d_output = d_output_seq.reshape(rows_here, width) * valid.reshape(rows_here, 1)
+        grad_input, d_mats, d_vecs = plain_backward(d_output)
+        d_mats = d_mats.reshape(devices, 3, third, width)
+        summed = [
+            reduce_bits(d_mats[:, k], orders[k][::-1], names).astype(jnp.float32)
+            for k in range(3)
         ]
-    ).reshape(devices, 1, vec_here)
-    d_small = jnp.pad(d_vecs, ((0, 0), (0, 7), (0, width - vec_here))).astype(low)
-    summed = [
-        reduce_bits(d_mats[:, 0], orders[0][::-1], names),
-        reduce_bits(d_mats[:, 1], orders[1][::-1], names),
-        reduce_bits(jnp.concatenate([d_mats[:, 2], d_small], axis=1), orders[2][::-1], names),
-    ]
-    grad_vecs = summed[2][third, :vec_here].astype(jnp.float32)
-    grad_mats = (
-        jnp.concatenate([summed[0], summed[1], summed[2][:third]]).astype(jnp.float32).reshape(-1)
-    )
+    grad_mats = jnp.concatenate(summed).reshape(-1)
+    grad_vecs = reduce_bits(d_vecs.reshape(devices, vec_here), orders[0][::-1], names)
 
     picked_turned = jnp.dot(picked, turn.T, preferred_element_type=jnp.float32).astype(low)
     d_rolled = contract_rows(d_logits, picked_turned)

time: 569 us -> 438 us (0.77)
  local copies, waits for them, and re-layouts: 154 us -> 48.2 us
  other arithmetic: 102 us -> 49.9 us
  matrix products: 70.5 us -> 21.3 us
  Pallas kernels: 0 us -> 43.7 us
  starting transfers between devices: 56.9 us -> 75.7 us
  waiting for transfers between devices: 177 us -> 190 us
    pallas_call x0 -> x2, Pallas kernels: none -> 43.7 us  [the longest x1 25.5 us: call_backward(): pl.pallas_call(functools.partial(backward_kernel, plan, unit, seq_here),...]
    slice x12 -> x4, local copies, waits for them, and re-layouts: 28.3 us -> 0.47 us  [on_device(): mats_low[k]]
    dot_general x11 -> x0, matrix products: 25 us -> none  [the longest x1 11.2 us: on_device(): jnp.dot(hidden_low, w_up, preferred_element_type=jnp.float32) + bias_up]
    ppermute x60 -> x73, starting transfers between devices: 47.7 us -> 71.7 us  [flip(): return lax.ppermute(value, name, [(0, 1), (1, 0)])]
    reshape x6 -> x2, local copies, waits for them, and re-layouts: 20.6 us -> 1.33 us  [the longest x1 1.27 us: on_device(): (mlm_positions + seq_start[:, None]).reshape(-1)]
    concatenate x4 -> x8, other arithmetic: 18.6 us -> 1.13 us  [the longest x1 0.8 us: on_device(): jnp.concatenate([d_picked, d_cls, jnp.zeros((heads_pad, width), jnp.float...]
    concatenate x2, local copies, waits for them, and re-layouts: 31.8 us -> 14.5 us  [on_device(): jnp.concatenate([from_left, embed_low, from_right, jnp.zeros((shifted_row...]
    dot_general x6 -> x2, matrix products: 17.6 us -> 3.44 us  [contract_cols(): lax.dot_general(left, right, (((1,), (1,)), ((), ())), preferred_element_...]
  transfers between devices with their start and end apart: 63 -> 76, of which waited for: 38 -> 42; matrix products, arithmetic and copies ran while one was open for 21% -> 20% of each run, Pallas kernels for 0% -> 0%
where the time goes in v2:
time: 438 us; the launch traced here: 432 us
  waiting for transfers between devices  190 us (43%)
  starting transfers between devices  75.7 us (17%)
  other arithmetic  49.9 us (11%)
  local copies, waits for them, and re-layouts  48.2 us (11%)
  Pallas kernels  43.7 us (10%)
  matrix products  21.3 us (5%)
    ppermute x73, waiting for transfers between devices, flip(): return lax.ppermute(value, name, [(0, 1), (1, 0)])  174 us
    ppermute x73, starting transfers between devices, flip(): return lax.ppermute(value, name, [(0, 1), (1, 0)])  71.7 us
    pallas_call x1, Pallas kernels, call_backward(): pl.pallas_call(functools.partial(backward_kernel, plan, unit, seq_here),...  25.5 us
    pallas_call x1, Pallas kernels, call_forward(): pl.pallas_call(functools.partial(forward_kernel, plan, seq_here), out_sha...  18.2 us
    concatenate x2, local copies, waits for them, and re-layouts, on_device(): jnp.concatenate([from_left, embed_low, from_right, jnp.zeros((shifted_row...  14.5 us
    convert_element_type x12, other arithmetic, reduce_relative(): send, keep = (value.astype(keep.dtype) for value in total)  13 us
    dot_general x2, matrix products, contract_rows(): lax.dot_general(left, right, (((0,), (0,)), ((), ())), preferred_element_...  9.04 us
  transfers between devices with their start and end apart: 76, of which 42 were waited for; matrix products, arithmetic and copies ran while one was open for 20% of the time, Pallas kernels for 0%

profile of v2, /device:TPU:0, one launch (start us, length us, event | category | flops | bytes accessed | tf_op | source)
XLA Modules:
  0.0 431.9 jit_solution(12892048594015389382)
XLA Ops:
  3.0 4.1 collective-permute-start
  8.7 3.0 collective-permute-start.11
  13.3 2.0 convert_element_type.492
  17.2 1.8 collective-permute-start.1
  22.0 3.4 collective-permute-done.5
  27.0 1.6 collective-permute-done.11
  28.6 1.6 collective-permute-start.12
  30.6 1.6 collective-permute-start.18
  33.5 8.1 %collective-permute-done.18 = bf16[2,96,768]{2,1,0:T(8,128)(2,1)S(1)} collective-permute-done((bf16[2,96,768]{2,1,0:T(8,128)(2,1)S(1)}, bf16[2,96,768]{2,1,0:T(8,128)(2,1)S(1)}, u32[]{:S(2)}, u32[]{:S(2)}) %collective-permute-start.18) | collective-permute-done | bytes 294944 | tf_op jit(solution)/shard_map/ppermute | solution.py:89
  43.5 1.6 collective-permute-start.7
  46.6 7.5 %collective-permute-done.19 = bf16[4,96,768]{2,1,0:T(8,128)(2,1)S(1)} collective-permute-done((bf16[4,96,768]{2,1,0:T(8,128)(2,1)S(1)}, bf16[4,96,768]{2,1,0:T(8,128)(2,1)S(1)}, u32[]{:S(2)}, u32[]{:S(2)}) %collective-permute-start.19) | collective-permute-done | bytes 589856 | tf_op jit(solution)/shard_map/ppermute | solution.py:89
  54.3 1.6 collective-permute-start.20
  56.7 1.7 collective-permute-start.14
  59.7 1.6 collective-permute-start.2
  64.6 1.8 collective-permute-start.3
  67.0 45.4 %collective-permute-done.3 = bf16[2,2,2,8,768]{4,3,2,1,0:T(8,128)(2,1)S(1)} collective-permute-done((bf16[2,2,2,8,768]{4,3,2,1,0:T(8,128)(2,1)S(1)}, bf16[2,2,2,8,768]{4,3,2,1,0:T(8,128)(2,1)S(1)}, u32[]{:S(2)}, u32[]{:S(2)}) %collective-permute-start.3) | collective-permute-done | bytes 98336 | tf_op jit(solution)/shard_map/ppermute | solution.py:89
  112.9 6.1 %collective-permute-done.39 = bf16[768]{0:T(1024)(128)(2,1)S(1)} collective-permute-done((bf16[768]{0:T(1024)(128)(2,1)S(1)}, bf16[768]{0:T(1024)(128)(2,1)S(1)}, u32[]{:S(2)}, u32[]{:S(2)}) %collective-permute-start.39) | collective-permute-done | bytes 1568 | tf_op jit(solution)/shard_map/ppermute | solution.py:710
  119.2 3.3 collective-permute-done.38
  125.8 7.3 %concatenate.76 = bf16[734064]{0:T(1024)(128)(2,1)S(1)} concatenate(bf16[768]{0:T(1024)(128)(2,1)S(1)} %collective-permute-done.39, bf16[732528]{0:T(1024)(128)(2,1)S(1)} %convert_element_type.492, bf16[768]{0:T(1024)(128)(2,1)S(1)} %collective-permute-done.38), dimensions={0} | concatenate | bytes 2936256 | tf_op jit(solution)/shard_map/concatenate | solution.py:712
  133.1 2.4 slice.286
  135.5 7.2 %concatenate.75 = bf16[733440]{0:T(1024)(128)(2,1)S(1)} concatenate(bf16[732528]{0:T(1024)(128)(2,1)S(1)} %convert_element_type.492, bf16[768]{0:T(1024)(128)(2,1)S(1)} %collective-permute-done.38, bf16[144]{0:T(256)(128)(2,1)S(1)} %broadcast_in_dim.109), dimensions={0} | concatenate | bytes 2933760 | tf_op jit(solution)/shard_map/concatenate | solution.py:712
  142.7 2.4 slice.283
  145.1 4.4 %fusion.7 = bf16[955,768]{1,0:T(8,128)(2,1)} fusion(bf16[955,768]{1,0:T(8,128)(2,1)} %slice.283, bf16[955,768]{1,0:T(8,128)(2,1)} %slice.286, pred[768]{0:T(1024)(128)(4,1)S(1)} %iota_compare_fusion.12, s32[768]{0:T(1024)S(1)} %add_select_fusion), kind=kOutput, calls=%fused_computation.23 | convolution fusion | flops 1128620544 | bytes 4404480 | tf_op jit(solution)/shard_map/dot_general | solution.py:724
  150.5 18.2 %shard_map.189 = (bf16[72,768]{1,0:T(8,128)(2,1)}, bf16[9216,768]{1,0:T(8,128)(2,1)}, bf16[256,2304]{1,0:T(8,128)(2,1)}, bf16[256,768]{1,0:T(8,128)(2,1)}, f32[2...) custom-call(s32[1]{0:T(128)} %bitcast.refs_0_, s32[2]{0:T(128)} %refs_1_.3, ...), custom_call_target="tpu_custom_call" | custom-call | flops 3623878656 | bytes 50331648 | tf_op jit(solution)/shard_map/pallas_call | solution.py:457
  169.5 2.0 collective-permute-start.23
  172.2 3.2 collective-permute-done.23
  177.3 1.9 collective-permute-start.28
  179.3 2.2 collective-permute-done.33
  186.3 2.3 collective-permute-done.34
  188.6 1.7 collective-permute-start.35
  192.8 2.5 collective-permute-done.35
  195.4 1.7 collective-permute-done.30
  197.9 3.6 collective-permute-done.26
  202.4 4.0 collective-permute-done.31
  210.7 3.3 select_reduce_fusion
  214.0 1.8 exponential_reduce_fusion
  220.6 3.3 all-to-all-start
  223.9 1.6 fusion.50
  231.6 7.3 %all-to-all-done = f32[32,32,128]{2,1,0:T(8,128)} async-done(((f32[32,32,128]{2,1,0:T(8,128)}), f32[32,32,128]{2,1,0:T(8,128)}, u32[]{:S(2)}, u32[]{:S(2)}) %all-to-all-start) | async-done | bytes 524320 | tf_op jit(solution)/shard_map/all_to_all | solution.py:775
  240.9 5.5 %select_convert_fusion = bf16[2048,955]{0,1:T(8,128)(2,1)S(1)} fusion(f32[2048,955]{0,1:T(8,128)} %copy-done, s32[2048]{0:T(1024)S(1)} %copy-done.16, f32[2048]{0:T(1024)S(1)} %fusion.33, f32[2048]{0:T(1024)S(1)} %get-tuple-element.86, pred[2048]{0:T(1024)(128)(4,1)S(1)} %lt.153, pred[955]{0:T(1024)(128)(4,1)S(1)} %copy-done.32), kind=kLoop, calls=%fused_computation | loop fusion | flops 15646720 | bytes 11762619 | tf_op jit(solution)/shard_map/convert_element_type | solution.py:786
  246.5 4.2 convolution_convert_fusion.1
  257.8 4.9 %collective-permute-done.51 = bf16[2,2,2,64,256]{4,3,0,2,1:T(8,128)(2,1)S(1)} collective-permute-done((bf16[2,2,2,64,256]{4,3,0,2,1:T(8,128)(2,1)S(1)}, bf16[2,2,2,64,256]{4,3,0,2,1:T(8,128)(2,1)S(1)}, u32[]{:S(2)}, u32[]{:S(2)}) %collective-permute-start.51) | collective-permute-done | bytes 262176 | tf_op jit(solution)/shard_map/ppermute | solution.py:89
  266.1 4.3 collective-permute-done.46
  274.4 1.8 collective-permute-done.47
  278.0 2.6 collective-permute-start.44
  282.9 2.6 collective-permute-done.49
  286.4 25.5 %shard_map.190 = (f32[256,768]{1,0:T(8,128)}, f32[12,768]{1,0:T(8,128)}, bf16[16,96,768]{2,1,0:T(8,128)(2,1)}, bf16[16,96,768]{2,1,0:T(8,128)(2,1)}, bf16[16,96,...) custom-call(s32[1]{0:T(128)} %bitcast.refs_0_, ...), custom_call_target="tpu_custom_call" | custom-call | flops 7247757312 | bytes 50331648 | tf_op jit(solution)/shard_map/pallas_call | solution.py:492
  315.2 8.9 %fusion.19 = f32[955,768]{1,0:T(8,128)S(1)} fusion(bf16[2048,955]{0,1:T(8,128)(2,1)} %copy-done.2, bf16[2048,768]{1,0:T(8,128)(2,1)} %bitcast.249, s32[768]{0:T(1024)S(1)} %copy-done.21), kind=kOutput, calls=%fused_computation.50 | convolution fusion | flops 5422252032 | bytes 9994240 | tf_op jit(solution)/shard_map/dot_general | solution.py:69
  325.2 2.2 slice_select_fusion
  327.4 2.6 reshape.250
  330.9 4.2 add_convert_fusion.5
  335.9 3.5 add_convert_fusion.3
  340.7 2.5 add_convert_fusion.1
  344.5 4.5 %fusion.5 = (f32[732528]{0:T(1024)}, f32[732528]{0:T(1024)}) fusion(f32[732528]{0:T(1024)S(1)} %copy-done.1, f32[732528]{0:T(1024)S(1)} %copy-done.6, f32[732528]{0:T(1024)S(1)} %copy-done.7, f32[732672]{0:T(1024)S(1)} %reshape.250), kind=kLoop, calls=%fused_computation.14 | loop fusion | flops 9522864 | bytes 17580672 | tf_op jit(solution)/shard_map/add | solution.py:85
  350.5 13.9 %collective-permute-done.56 = bf16[8,96,768]{2,1,0:T(8,128)(2,1)} collective-permute-done((bf16[8,96,768]{2,1,0:T(8,128)(2,1)}, bf16[8,96,768]{2,1,0:T(8,128)(2,1)}, u32[]{:S(2)}, u32[]{:S(2)}) %collective-permute-start.56) | collective-permute-done | bytes 1179680 | tf_op jit(solution)/shard_map/ppermute | solution.py:89
  367.1 20.7 %collective-permute-done.61 = bf16[8,96,768]{2,1,0:T(8,128)(2,1)S(1)} collective-permute-done((bf16[8,96,768]{2,1,0:T(8,128)(2,1)}, bf16[8,96,768]{2,1,0:T(8,128)(2,1)S(1)}, u32[]{:S(2)}, u32[]{:S(2)}) %collective-permute-start.61) | collective-permute-done | bytes 1179680 | tf_op jit(solution)/shard_map/ppermute | solution.py:89
  389.8 1.6 collective-permute-start.67
  392.6 12.0 %collective-permute-done.62 = bf16[4,96,768]{2,1,0:T(8,128)(2,1)S(1)} collective-permute-done((bf16[4,96,768]{2,1,0:T(8,128)(2,1)S(1)}, bf16[4,96,768]{2,1,0:T(8,128)(2,1)S(1)}, u32[]{:S(2)}, u32[]{:S(2)}) %collective-permute-start.62) | collective-permute-done | bytes 589856 | tf_op jit(solution)/shard_map/ppermute | solution.py:89
  409.3 2.4 collective-permute-done.63
  412.9 2.0 collective-permute-done.68
  416.0 7.0 %collective-permute-done.59 = bf16[1,96,768]{2,1,0:T(8,128)(2,1)S(1)} collective-permute-done((bf16[1,96,768]{2,1,0:T(8,128)(2,1)S(1)}, bf16[1,96,768]{2,1,0:T(8,128)(2,1)S(1)}, u32[]{:S(2)}, u32[]{:S(2)}) %collective-permute-start.59) | collective-permute-done | bytes 147488 | tf_op jit(solution)/shard_map/ppermute | solution.py:89
  423.1 3.1 collective-permute-done.64
  426.3 1.9 collective-permute-done.69
  428.5 3.0 fusion.25
  (365 shorter events, 99.9 us)
Async XLA Ops:
  3.0 13.6 %collective-permute-start = (bf16[8,768]{1,0:T(8,128)(2,1)S(1)}, bf16[8,768]{1,0:T(8,128)(2,1)S(1)}, u32[]{:S(2)}, u32[]{:S(2)}) collective-permute-start(bf16[8,768]{1,0:T(8,128)(2,1)S(1)} %concatenate.64), channel_id=1, source_target_pairs={{0,16},{16,0},{1,17},{17,1},{2,18},{18,2},{3,19},{19,3},{4,20},{20... | collective-permute-start | bytes 36872 | tf_op jit(solution)/shard_map/ppermute | solution.py:89
  8.5 16.9 %collective-permute-start.5 = (bf16[1,96,768]{2,1,0:T(8,128)(2,1)S(1)}, bf16[1,96,768]{2,1,0:T(8,128)(2,1)S(1)}, u32[]{:S(2)}, u32[]{:S(2)}) collective-permute-start(bf16[1,96,768]{2,1,0:T(8,128)(2,1)S(1)} %slice.273), channel_id=1, source_target_pairs={{0,16},{16,0},{1,17},{17,1},{2,18},{18,2},{3,19},{19,3},{4,20},{20... | collective-permute-start | bytes 442376 | tf_op jit(solution)/shard_map/ppermute | solution.py:89
  8.7 19.8 %collective-permute-start.11 = (bf16[1,96,768]{2,1,0:T(8,128)(2,1)S(1)}, bf16[1,96,768]{2,1,0:T(8,128)(2,1)S(1)}, u32[]{:S(2)}, u32[]{:S(2)}) collective-permute-start(bf16[1,96,768]{2,1,0:T(8,128)(2,1)S(1)} %slice.275), channel_id=1, source_target_pairs={{0,16},{16,0},{1,17},{17,1},{2,18},{18,2},{3,19},{19,3},{4,20},{20... | collective-permute-start | bytes 442376 | tf_op jit(solution)/shard_map/ppermute | solution.py:89
  11.8 18.7 %collective-permute-start.17 = (bf16[1,96,768]{2,1,0:T(8,128)(2,1)S(1)}, bf16[1,96,768]{2,1,0:T(8,128)(2,1)S(1)}, u32[]{:S(2)}, u32[]{:S(2)}) collective-permute-start(bf16[1,96,768]{2,1,0:T(8,128)(2,1)S(1)} %slice.277), channel_id=1, source_target_pairs={{0,16},{16,0},{1,17},{17,1},{2,18},{18,2},{3,19},{19,3},{4,20},{20... | collective-permute-start | bytes 442376 | tf_op jit(solution)/shard_map/ppermute | solution.py:89
  25.4 18.0 %collective-permute-start.6 = (bf16[2,96,768]{2,1,0:T(8,128)(2,1)S(1)}, bf16[2,96,768]{2,1,0:T(8,128)(2,1)S(1)}, u32[]{:S(2)}, u32[]{:S(2)}) collective-permute-start(bf16[2,96,768]{2,1,0:T(8,128)(2,1)S(1)} %pad_maximum_fusion.8), channel_id=1, source_target_pairs={{0,1},{1,0},{2,3},{3,2},{4,5},{5,4},{6,7},{7,6},{8,9},{9,8},{10,11... | collective-permute-start | bytes 884744 | tf_op jit(solution)/shard_map/ppermute | solution.py:89
  28.6 13.2 %collective-permute-start.12 = (bf16[2,96,768]{2,1,0:T(8,128)(2,1)S(1)}, bf16[2,96,768]{2,1,0:T(8,128)(2,1)S(1)}, u32[]{:S(2)}, u32[]{:S(2)}) collective-permute-start(bf16[2,96,768]{2,1,0:T(8,128)(2,1)S(1)} %pad_maximum_fusion.9), channel_id=1, source_target_pairs={{0,4},{4,0},{1,5},{5,1},{2,6},{6,2},{3,7},{7,3},{8,12},{12,8},{9,1... | collective-permute-start | bytes 884744 | tf_op jit(solution)/shard_map/ppermute | solution.py:89
  30.6 11.1 %collective-permute-start.18 = (bf16[2,96,768]{2,1,0:T(8,128)(2,1)S(1)}, bf16[2,96,768]{2,1,0:T(8,128)(2,1)S(1)}, u32[]{:S(2)}, u32[]{:S(2)}) collective-permute-start(bf16[2,96,768]{2,1,0:T(8,128)(2,1)S(1)} %pad_maximum_fusion.10), channel_id=1, source_target_pairs={{0,4},{4,0},{1,5},{5,1},{2,6},{6,2},{3,7},{7,3},{8,12},{12,8},{9,1... | collective-permute-start | bytes 884744 | tf_op jit(solution)/shard_map/ppermute | solution.py:89
  41.7 12.4 %collective-permute-start.19 = (bf16[4,96,768]{2,1,0:T(8,128)(2,1)S(1)}, bf16[4,96,768]{2,1,0:T(8,128)(2,1)S(1)}, u32[]{:S(2)}, u32[]{:S(2)}) collective-permute-start(bf16[4,96,768]{2,1,0:T(8,128)(2,1)S(1)} %pad_maximum_fusion.4), channel_id=1, source_target_pairs={{0,8},{8,0},{1,9},{9,1},{2,10},{10,2},{3,11},{11,3},{4,12},{12,4},... | collective-permute-start | bytes 1769480 | tf_op jit(solution)/shard_map/ppermute | solution.py:89
  41.9 14.0 %collective-permute-start.13 = (bf16[4,96,768]{2,1,0:T(8,128)(2,1)S(1)}, bf16[4,96,768]{2,1,0:T(8,128)(2,1)S(1)}, u32[]{:S(2)}, u32[]{:S(2)}) collective-permute-start(bf16[4,96,768]{2,1,0:T(8,128)(2,1)S(1)} %pad_maximum_fusion.3), channel_id=1, source_target_pairs={{0,1},{1,0},{2,3},{3,2},{4,5},{5,4},{6,7},{7,6},{8,9},{9,8},{10,11... | collective-permute-start | bytes 1769480 | tf_op jit(solution)/shard_map/ppermute | solution.py:89
  43.5 15.0 %collective-permute-start.7 = (bf16[4,96,768]{2,1,0:T(8,128)(2,1)S(1)}, bf16[4,96,768]{2,1,0:T(8,128)(2,1)S(1)}, u32[]{:S(2)}, u32[]{:S(2)}) collective-permute-start(bf16[4,96,768]{2,1,0:T(8,128)(2,1)S(1)} %pad_maximum_fusion.2), channel_id=1, source_target_pairs={{0,4},{4,0},{1,5},{5,1},{2,6},{6,2},{3,7},{7,3},{8,12},{12,8},{9,1... | collective-permute-start | bytes 1769480 | tf_op jit(solution)/shard_map/ppermute | solution.py:89
  54.2 70.0 %collective-permute-start.21 = (bf16[8,96,768]{2,1,0:T(8,128)(2,1)S(1)}, bf16[8,96,768]{2,1,0:T(8,128)(2,1)}, u32[]{:S(2)}, u32[]{:S(2)}) collective-permute-start(bf16[8,96,768]{2,1,0:T(8,128)(2,1)S(1)} %constant_dynamic-update-slice_fusion.8.refs_13_), channel_id=1, source_target_pairs={{0,2},{2,0},{1,3},{3,1},{4,6},{6,4},{5,7},{7,5},{8,10},{10,8},{9,1... | collective-permute-start | bytes 3538952 | tf_op jit(solution)/shard_map/ppermute | solution.py:89
  54.3 70.3 %collective-permute-start.20 = (bf16[8,96,768]{2,1,0:T(8,128)(2,1)S(1)}, bf16[8,96,768]{2,1,0:T(8,128)(2,1)}, u32[]{:S(2)}, u32[]{:S(2)}) collective-permute-start(bf16[8,96,768]{2,1,0:T(8,128)(2,1)S(1)} %constant_dynamic-update-slice_fusion.8.refs_13_), channel_id=1, source_target_pairs={{0,1},{1,0},{2,3},{3,2},{4,5},{5,4},{6,7},{7,6},{8,9},{9,8},{10,11... | collective-permute-start | bytes 3538952 | tf_op jit(solution)/shard_map/ppermute | solution.py:89
  56.7 67.9 %collective-permute-start.14 = (bf16[8,96,768]{2,1,0:T(8,128)(2,1)}, bf16[8,96,768]{2,1,0:T(8,128)(2,1)}, u32[]{:S(2)}, u32[]{:S(2)}) collective-permute-start(bf16[8,96,768]{2,1,0:T(8,128)(2,1)} %constant_dynamic-update-slice_fusion.4.refs_9_), channel_id=1, source_target_pairs={{0,8},{8,0},{1,9},{9,1},{2,10},{10,2},{3,11},{11,3},{4,12},{12,4},... | collective-permute-start | bytes 3538952 | tf_op jit(solution)/shard_map/ppermute | solution.py:89
  59.4 65.7 %collective-permute-start.8 = (bf16[8,96,768]{2,1,0:T(8,128)(2,1)}, bf16[8,96,768]{2,1,0:T(8,128)(2,1)}, u32[]{:S(2)}, u32[]{:S(2)}) collective-permute-start(bf16[8,96,768]{2,1,0:T(8,128)(2,1)} %constant_dynamic-update-slice_fusion.refs_5_), channel_id=1, source_target_pairs={{0,8},{8,0},{1,9},{9,1},{2,10},{10,2},{3,11},{11,3},{4,12},{12,4},... | collective-permute-start | bytes 3538952 | tf_op jit(solution)/shard_map/ppermute | solution.py:89
  64.6 47.8 %collective-permute-start.3 = (bf16[2,2,2,8,768]{4,3,2,1,0:T(8,128)(2,1)S(1)}, bf16[2,2,2,8,768]{4,3,2,1,0:T(8,128)(2,1)S(1)}, u32[]{:S(2)}, u32[]{:S(2)}) collective-permute-start(bf16[2,2,2,8,768]{4,3,2,1,0:T(8,128)(2,1)S(1)} %pad_maximum_fusion.19), channel_id=1, source_target_pairs={{0,8},{8,0},{1,9},{9,1},{2,10},{10,2},{3,11},{11,3},{4,12},{12,4},... | collective-permute-start | bytes 294920 | tf_op jit(solution)/shard_map/ppermute | solution.py:89
  112.4 6.6 %collective-permute-start.39 = (bf16[768]{0:T(1024)(128)(2,1)S(1)}, bf16[768]{0:T(1024)(128)(2,1)S(1)}, u32[]{:S(2)}, u32[]{:S(2)}) collective-permute-start(bf16[768]{0:T(1024)(128)(2,1)S(1)} %copy-done.26), channel_id=1, source_target_pairs={{0,1},{1,2},{2,3},{3,4},{4,5},{5,6},{6,7},{7,8},{8,9},{9,10},{10,1... | collective-permute-start | bytes 4616 | tf_op jit(solution)/shard_map/ppermute | solution.py:710
  124.0 26.5 %collective-permute-start.15 = (bf16[8,96,768]{2,1,0:T(8,128)(2,1)}, bf16[8,96,768]{2,1,0:T(8,128)(2,1)}, u32[]{:S(2)}, u32[]{:S(2)}) collective-permute-start(bf16[8,96,768]{2,1,0:T(8,128)(2,1)} %constant_dynamic-update-slice_fusion.4.refs_9_), channel_id=1, source_target_pairs={{0,2},{2,0},{1,3},{3,1},{4,6},{6,4},{5,7},{7,5},{8,10},{10,8},{9,1... | collective-permute-start | bytes 3538952 | tf_op jit(solution)/shard_map/ppermute | solution.py:89
  124.2 26.3 %collective-permute-start.9 = (bf16[8,96,768]{2,1,0:T(8,128)(2,1)}, bf16[8,96,768]{2,1,0:T(8,128)(2,1)}, u32[]{:S(2)}, u32[]{:S(2)}) collective-permute-start(bf16[8,96,768]{2,1,0:T(8,128)(2,1)} %constant_dynamic-update-slice_fusion.refs_5_), channel_id=1, source_target_pairs={{0,2},{2,0},{1,3},{3,1},{4,6},{6,4},{5,7},{7,5},{8,10},{10,8},{9,1... | collective-permute-start | bytes 3538952 | tf_op jit(solution)/shard_map/ppermute | solution.py:89
  124.5 26.0 %collective-permute-start.22 = (bf16[8,96,768]{2,1,0:T(8,128)(2,1)}, bf16[8,96,768]{2,1,0:T(8,128)(2,1)}, u32[]{:S(2)}, u32[]{:S(2)}) collective-permute-start(bf16[8,96,768]{2,1,0:T(8,128)(2,1)} %collective-permute-done.20.refs_14_), channel_id=1, source_target_pairs={{0,2},{2,0},{1,3},{3,1},{4,6},{6,4},{5,7},{7,5},{8,10},{10,8},{9,1... | collective-permute-start | bytes 3538952 | tf_op jit(solution)/shard_map/ppermute | solution.py:89
  124.7 25.8 %collective-permute-start.16 = (bf16[8,96,768]{2,1,0:T(8,128)(2,1)}, bf16[8,96,768]{2,1,0:T(8,128)(2,1)}, u32[]{:S(2)}, u32[]{:S(2)}) collective-permute-start(bf16[8,96,768]{2,1,0:T(8,128)(2,1)} %collective-permute-done.14.refs_10_), channel_id=1, source_target_pairs={{0,2},{2,0},{1,3},{3,1},{4,6},{6,4},{5,7},{7,5},{8,10},{10,8},{9,1... | collective-permute-start | bytes 3538952 | tf_op jit(solution)/shard_map/ppermute | solution.py:89
  125.0 25.5 %collective-permute-start.10 = (bf16[8,96,768]{2,1,0:T(8,128)(2,1)}, bf16[8,96,768]{2,1,0:T(8,128)(2,1)}, u32[]{:S(2)}, u32[]{:S(2)}) collective-permute-start(bf16[8,96,768]{2,1,0:T(8,128)(2,1)} %collective-permute-done.8.refs_6_), channel_id=1, source_target_pairs={{0,2},{2,0},{1,3},{3,1},{4,6},{6,4},{5,7},{7,5},{8,10},{10,8},{9,1... | collective-permute-start | bytes 3538952 | tf_op jit(solution)/shard_map/ppermute | solution.py:89
  169.5 5.9 %collective-permute-start.23 = (bf16[72,256]{1,0:T(8,128)(2,1)S(1)}, bf16[72,256]{1,0:T(8,128)(2,1)S(1)}, u32[]{:S(2)}, u32[]{:S(2)}) collective-permute-start(bf16[72,256]{1,0:T(8,128)(2,1)S(1)} %slice.278), channel_id=1, source_target_pairs={{0,16},{16,0},{1,17},{17,1},{2,18},{18,2},{3,19},{19,3},{4,20},{20... | collective-permute-start | bytes 110600 | tf_op jit(solution)/shard_map/ppermute | solution.py:89
  176.2 5.3 %collective-permute-start.33 = (bf16[72,256]{1,0:T(8,128)(2,1)S(1)}, bf16[72,256]{1,0:T(8,128)(2,1)S(1)}, u32[]{:S(2)}, u32[]{:S(2)}) collective-permute-start(bf16[72,256]{1,0:T(8,128)(2,1)S(1)} %get-tuple-element.114), channel_id=1, source_target_pairs={{0,16},{16,0},{1,17},{17,1},{2,18},{18,2},{3,19},{19,3},{4,20},{20... | collective-permute-start | bytes 110600 | tf_op jit(solution)/shard_map/ppermute | solution.py:89
  177.3 5.3 %collective-permute-start.28 = (bf16[72,256]{1,0:T(8,128)(2,1)S(1)}, bf16[72,256]{1,0:T(8,128)(2,1)S(1)}, u32[]{:S(2)}, u32[]{:S(2)}) collective-permute-start(bf16[72,256]{1,0:T(8,128)(2,1)S(1)} %get-tuple-element.115), channel_id=1, source_target_pairs={{0,16},{16,0},{1,17},{17,1},{2,18},{18,2},{3,19},{19,3},{4,20},{20... | collective-permute-start | bytes 110600 | tf_op jit(solution)/shard_map/ppermute | solution.py:89
  179.2 6.3 %collective-permute-start.24 = (bf16[2,72,256]{2,1,0:T(8,128)(2,1)S(1)}, bf16[2,72,256]{2,1,0:T(8,128)(2,1)S(1)}, u32[]{:S(2)}, u32[]{:S(2)}) collective-permute-start(bf16[2,72,256]{2,1,0:T(8,128)(2,1)S(1)} %pad_maximum_fusion.20), channel_id=1, source_target_pairs={{0,1},{1,0},{2,3},{3,2},{4,5},{5,4},{6,7},{7,6},{8,9},{9,8},{10,11... | collective-permute-start | bytes 221192 | tf_op jit(solution)/shard_map/ppermute | solution.py:89
  183.4 5.2 %collective-permute-start.34 = (bf16[2,72,256]{2,1,0:T(8,128)(2,1)S(1)}, bf16[2,72,256]{2,1,0:T(8,128)(2,1)S(1)}, u32[]{:S(2)}, u32[]{:S(2)}) collective-permute-start(bf16[2,72,256]{2,1,0:T(8,128)(2,1)S(1)} %pad_maximum_fusion.22), channel_id=1, source_target_pairs={{0,4},{4,0},{1,5},{5,1},{2,6},{6,2},{3,7},{7,3},{8,12},{12,8},{9,1... | collective-permute-start | bytes 221192 | tf_op jit(solution)/shard_map/ppermute | solution.py:89
  184.1 6.2 %collective-permute-start.29 = (bf16[2,72,256]{2,1,0:T(8,128)(2,1)S(1)}, bf16[2,72,256]{2,1,0:T(8,128)(2,1)S(1)}, u32[]{:S(2)}, u32[]{:S(2)}) collective-permute-start(bf16[2,72,256]{2,1,0:T(8,128)(2,1)S(1)} %pad_maximum_fusion.21), channel_id=1, source_target_pairs={{0,4},{4,0},{1,5},{5,1},{2,6},{6,2},{3,7},{7,3},{8,12},{12,8},{9,1... | collective-permute-start | bytes 221192 | tf_op jit(solution)/shard_map/ppermute | solution.py:89
  185.6 5.9 %collective-permute-start.25 = (bf16[2,2,72,256]{3,2,1,0:T(8,128)(2,1)S(1)}, bf16[2,2,72,256]{3,2,1,0:T(8,128)(2,1)S(1)}, u32[]{:S(2)}, u32[]{:S(2)}) collective-permute-start(bf16[2,2,72,256]{3,2,1,0:T(8,128)(2,1)S(1)} %pad_maximum_fusion.15), channel_id=1, source_target_pairs={{0,4},{4,0},{1,5},{5,1},{2,6},{6,2},{3,7},{7,3},{8,12},{12,8},{9,1... | collective-permute-start | bytes 442376 | tf_op jit(solution)/shard_map/ppermute | solution.py:89
  188.6 6.6 %collective-permute-start.35 = (bf16[2,2,72,256]{3,2,1,0:T(8,128)(2,1)S(1)}, bf16[2,2,72,256]{3,2,1,0:T(8,128)(2,1)S(1)}, u32[]{:S(2)}, u32[]{:S(2)}) collective-permute-start(bf16[2,2,72,256]{3,2,1,0:T(8,128)(2,1)S(1)} %pad_maximum_fusion.17), channel_id=1, source_target_pairs={{0,8},{8,0},{1,9},{9,1},{2,10},{10,2},{3,11},{11,3},{4,12},{12,4},... | collective-permute-start | bytes 442376 | tf_op jit(solution)/shard_map/ppermute | solution.py:89
  190.3 6.8 %collective-permute-start.30 = (bf16[2,2,72,256]{3,2,1,0:T(8,128)(2,1)S(1)}, bf16[2,2,72,256]{3,2,1,0:T(8,128)(2,1)S(1)}, u32[]{:S(2)}, u32[]{:S(2)}) collective-permute-start(bf16[2,2,72,256]{3,2,1,0:T(8,128)(2,1)S(1)} %pad_maximum_fusion.16), channel_id=1, source_target_pairs={{0,1},{1,0},{2,3},{3,2},{4,5},{5,4},{6,7},{7,6},{8,9},{9,8},{10,11... | collective-permute-start | bytes 442376 | tf_op jit(solution)/shard_map/ppermute | solution.py:89
  191.5 10.1 %collective-permute-start.26 = (bf16[2,2,2,72,256]{4,3,2,1,0:T(8,128)(2,1)S(1)}, bf16[2,2,2,72,256]{4,3,2,1,0:T(8,128)(2,1)S(1)}, u32[]{:S(2)}, u32[]{:S(2)}) collective-permute-start(bf16[2,2,2,72,256]{4,3,2,1,0:T(8,128)(2,1)S(1)} %pad_maximum_fusion.11), channel_id=1, source_target_pairs={{0,8},{8,0},{1,9},{9,1},{2,10},{10,2},{3,11},{11,3},{4,12},{12,4},... | collective-permute-start | bytes 884744 | tf_op jit(solution)/shard_map/ppermute | solution.py:89
  195.3 6.8 %collective-permute-start.36 = (bf16[2,2,2,72,256]{4,3,2,1,0:T(8,128)(2,1)S(1)}, bf16[2,2,2,72,256]{4,3,2,1,0:T(8,128)(2,1)S(1)}, u32[]{:S(2)}, u32[]{:S(2)}) collective-permute-start(bf16[2,2,2,72,256]{4,3,2,1,0:T(8,128)(2,1)S(1)} %pad_maximum_fusion.13), channel_id=1, source_target_pairs={{0,1},{1,0},{2,3},{3,2},{4,5},{5,4},{6,7},{7,6},{8,9},{9,8},{10,11... | collective-permute-start | bytes 884744 | tf_op jit(solution)/shard_map/ppermute | solution.py:89
  197.2 9.3 %collective-permute-start.31 = (bf16[2,2,2,72,256]{4,3,2,1,0:T(8,128)(2,1)S(1)}, bf16[2,2,2,72,256]{4,3,2,1,0:T(8,128)(2,1)S(1)}, u32[]{:S(2)}, u32[]{:S(2)}) collective-permute-start(bf16[2,2,2,72,256]{4,3,2,1,0:T(8,128)(2,1)S(1)} %pad_maximum_fusion.12), channel_id=1, source_target_pairs={{0,8},{8,0},{1,9},{9,1},{2,10},{10,2},{3,11},{11,3},{4,12},{12,4},... | collective-permute-start | bytes 884744 | tf_op jit(solution)/shard_map/ppermute | solution.py:89
  201.7 5.0 %collective-permute-start.27 = (bf16[2,2,2,2,72,256]{5,4,3,2,1,0:T(8,128)(2,1)S(1)}, bf16[2,2,2,2,72,256]{5,4,3,2,1,0:T(8,128)(2,1)S(1)}, u32[]{:S(2)}, u32[]{:S(2)}) collective-permute-start(bf16[2,2,2,2,72,256]{5,4,3,2,1,0:T(8,128)(2,1)S(1)} %pad_maximum_fusion.5), channel_id=1, source_target_pairs={{0,2},{2,0},{1,3},{3,1},{4,6},{6,4},{5,7},{7,5},{8,10},{10,8},{9,1... | collective-permute-start | bytes 1769480 | tf_op jit(solution)/shard_map/ppermute | solution.py:89
  220.6 18.3 %all-to-all-start = ((f32[32,32,128]{2,1,0:T(8,128)}), f32[32,32,128]{2,1,0:T(8,128)}, u32[]{:S(2)}, u32[]{:S(2)}) async-start(f32[32,32,128]{2,1,0:T(8,128)} %broadcast_in_dim.113), calls=%async_computation | async-start | bytes 1048576 | tf_op jit(solution)/shard_map/all_to_all | solution.py:775
  254.1 8.7 %collective-permute-start.51 = (bf16[2,2,2,64,256]{4,3,0,2,1:T(8,128)(2,1)S(1)}, bf16[2,2,2,64,256]{4,3,0,2,1:T(8,128)(2,1)S(1)}, u32[]{:S(2)}, u32[]{:S(2)}) collective-permute-start(bf16[2,2,2,64,256]{4,3,0,2,1:T(8,128)(2,1)S(1)} %dynamic-slice_bitcast_fusion), channel_id=1, source_target_pairs={{0,1},{1,0},{2,3},{3,2},{4,5},{5,4},{6,7},{7,6},{8,9},{9,8},{10,11... | collective-permute-start | bytes 786440 | tf_op jit(solution)/shard_map/ppermute | solution.py:89
  255.5 9.3 %collective-permute-start.41 = (bf16[2,2,2,64,256]{4,3,0,2,1:T(8,128)(2,1)S(1)}, bf16[2,2,2,64,256]{4,3,0,2,1:T(8,128)(2,1)S(1)}, u32[]{:S(2)}, u32[]{:S(2)}) collective-permute-start(bf16[2,2,2,64,256]{4,3,0,2,1:T(8,128)(2,1)S(1)} %dynamic-slice_bitcast_fusion.2), channel_id=1, source_target_pairs={{0,8},{8,0},{1,9},{9,1},{2,10},{10,2},{3,11},{11,3},{4,12},{12,4},... | collective-permute-start | bytes 786440 | tf_op jit(solution)/shard_map/ppermute | solution.py:89
  256.7 13.6 %collective-permute-start.46 = (bf16[2,2,2,64,256]{4,3,0,1,2:T(8,128)(2,1)S(1)}, bf16[2,2,2,64,256]{4,3,0,1,2:T(8,128)(2,1)S(1)}, u32[]{:S(2)}, u32[]{:S(2)}) collective-permute-start(bf16[2,2,2,64,256]{4,3,0,1,2:T(8,128)(2,1)S(1)} %dynamic-slice_bitcast_fusion.1), channel_id=1, source_target_pairs={{0,8},{8,0},{1,9},{9,1},{2,10},{10,2},{3,11},{11,3},{4,12},{12,4},... | collective-permute-start | bytes 786440 | tf_op jit(solution)/shard_map/ppermute | solution.py:89
  262.9 9.2 %collective-permute-start.52 = (bf16[2,2,64,256]{3,2,0,1:T(8,128)(2,1)S(1)}, bf16[2,2,64,256]{3,2,0,1:T(8,128)(2,1)S(1)}, u32[]{:S(2)}, u32[]{:S(2)}) collective-permute-start(bf16[2,2,64,256]{3,2,0,1:T(8,128)(2,1)S(1)} %dynamic-slice_bitcast_fusion.3), channel_id=1, source_target_pairs={{0,8},{8,0},{1,9},{9,1},{2,10},{10,2},{3,11},{11,3},{4,12},{12,4},... | collective-permute-start | bytes 393224 | tf_op jit(solution)/shard_map/ppermute | solution.py:89
  264.9 8.5 %collective-permute-start.42 = (bf16[2,2,64,256]{3,2,0,1:T(8,128)(2,1)S(1)}, bf16[2,2,64,256]{3,2,0,1:T(8,128)(2,1)S(1)}, u32[]{:S(2)}, u32[]{:S(2)}) collective-permute-start(bf16[2,2,64,256]{3,2,0,1:T(8,128)(2,1)S(1)} %dynamic-slice_bitcast_fusion.5), channel_id=1, source_target_pairs={{0,4},{4,0},{1,5},{5,1},{2,6},{6,2},{3,7},{7,3},{8,12},{12,8},{9,1... | collective-permute-start | bytes 393224 | tf_op jit(solution)/shard_map/ppermute | solution.py:89
  270.5 5.7 %collective-permute-start.47 = (bf16[2,2,64,256]{3,2,0,1:T(8,128)(2,1)S(1)}, bf16[2,2,64,256]{3,2,0,1:T(8,128)(2,1)S(1)}, u32[]{:S(2)}, u32[]{:S(2)}) collective-permute-start(bf16[2,2,64,256]{3,2,0,1:T(8,128)(2,1)S(1)} %dynamic-slice_bitcast_fusion.4), channel_id=1, source_target_pairs={{0,1},{1,0},{2,3},{3,2},{4,5},{5,4},{6,7},{7,6},{8,9},{9,8},{10,11... | collective-permute-start | bytes 393224 | tf_op jit(solution)/shard_map/ppermute | solution.py:89
  272.1 5.4 %collective-permute-start.53 = (bf16[2,64,256]{2,1,0:T(8,128)(2,1)S(1)}, bf16[2,64,256]{2,1,0:T(8,128)(2,1)S(1)}, u32[]{:S(2)}, u32[]{:S(2)}) collective-permute-start(bf16[2,64,256]{2,1,0:T(8,128)(2,1)S(1)} %dynamic-slice_bitcast_fusion.6), channel_id=1, source_target_pairs={{0,4},{4,0},{1,5},{5,1},{2,6},{6,2},{3,7},{7,3},{8,12},{12,8},{9,1... | collective-permute-start | bytes 196616 | tf_op jit(solution)/shard_map/ppermute | solution.py:89
  277.5 4.9 %collective-permute-start.54 = (bf16[64,256]{1,0:T(8,128)(2,1)S(1)}, bf16[64,256]{1,0:T(8,128)(2,1)S(1)}, u32[]{:S(2)}, u32[]{:S(2)}) collective-permute-start(bf16[64,256]{1,0:T(8,128)(2,1)S(1)} %dynamic-slice_bitcast_fusion.9), channel_id=1, source_target_pairs={{0,16},{16,0},{1,17},{17,1},{2,18},{18,2},{3,19},{19,3},{4,20},{20... | collective-permute-start | bytes 98312 | tf_op jit(solution)/shard_map/ppermute | solution.py:89
  278.0 4.9 %collective-permute-start.44 = (bf16[64,256]{1,0:T(8,128)(2,1)S(1)}, bf16[64,256]{1,0:T(8,128)(2,1)S(1)}, u32[]{:S(2)}, u32[]{:S(2)}) collective-permute-start(bf16[64,256]{1,0:T(8,128)(2,1)S(1)} %dynamic-slice_bitcast_fusion.11), channel_id=1, source_target_pairs={{0,16},{16,0},{1,17},{17,1},{2,18},{18,2},{3,19},{19,3},{4,20},{20... | collective-permute-start | bytes 98312 | tf_op jit(solution)/shard_map/ppermute | solution.py:89
  280.7 4.9 %collective-permute-start.49 = (bf16[64,256]{1,0:T(8,128)(2,1)S(1)}, bf16[64,256]{1,0:T(8,128)(2,1)S(1)}, u32[]{:S(2)}, u32[]{:S(2)}) collective-permute-start(bf16[64,256]{1,0:T(8,128)(2,1)S(1)} %dynamic-slice_bitcast_fusion.10), channel_id=1, source_target_pairs={{0,16},{16,0},{1,17},{17,1},{2,18},{18,2},{3,19},{19,3},{4,20},{20... | collective-permute-start | bytes 98312 | tf_op jit(solution)/shard_map/ppermute | solution.py:89
  312.9 18.0 %collective-permute-start.55 = (bf16[16,96,768]{2,1,0:T(8,128)(2,1)}, bf16[16,96,768]{2,1,0:T(8,128)(2,1)}, u32[]{:S(2)}, u32[]{:S(2)}) collective-permute-start(bf16[16,96,768]{2,1,0:T(8,128)(2,1)} %get-tuple-element.33), channel_id=1, source_target_pairs={{0,2},{2,0},{1,3},{3,1},{4,6},{6,4},{5,7},{7,5},{8,10},{10,8},{9,1... | collective-permute-start | bytes 7077896 | tf_op jit(solution)/shard_map/ppermute | solution.py:89
  313.4 22.5 %collective-permute-start.60 = (bf16[16,96,768]{2,1,0:T(8,128)(2,1)}, bf16[16,96,768]{2,1,0:T(8,128)(2,1)}, u32[]{:S(2)}, u32[]{:S(2)}) collective-permute-start(bf16[16,96,768]{2,1,0:T(8,128)(2,1)} %get-tuple-element.35), channel_id=1, source_target_pairs={{0,2},{2,0},{1,3},{3,1},{4,6},{6,4},{5,7},{7,5},{8,10},{10,8},{9,1... | collective-permute-start | bytes 7077896 | tf_op jit(solution)/shard_map/ppermute | solution.py:89
  313.5 27.2 %collective-permute-start.65 = (bf16[16,96,768]{2,1,0:T(8,128)(2,1)}, bf16[16,96,768]{2,1,0:T(8,128)(2,1)}, u32[]{:S(2)}, u32[]{:S(2)}) collective-permute-start(bf16[16,96,768]{2,1,0:T(8,128)(2,1)} %get-tuple-element.37), channel_id=1, source_target_pairs={{0,2},{2,0},{1,3},{3,1},{4,6},{6,4},{5,7},{7,5},{8,10},{10,8},{9,1... | collective-permute-start | bytes 7077896 | tf_op jit(solution)/shard_map/ppermute | solution.py:89
  314.2 9.9 %collective-permute-start.71 = (f32[2,2,2,288]{3,2,1,0:T(2,128)S(1)}, f32[2,2,2,288]{3,2,1,0:T(2,128)S(1)}, u32[]{:S(2)}, u32[]{:S(2)}) collective-permute-start(f32[2,2,2,288]{3,2,1,0:T(2,128)S(1)} %dynamic-slice_bitcast_fusion.13), channel_id=1, source_target_pairs={{0,8},{8,0},{1,9},{9,1},{2,10},{10,2},{3,11},{11,3},{4,12},{12,4},... | collective-permute-start | bytes 27656 | tf_op jit(solution)/shard_map/ppermute | solution.py:89
  324.2 5.8 %collective-permute-start.72 = (f32[2,2,288]{2,1,0:T(2,128)S(1)}, f32[2,2,288]{2,1,0:T(2,128)S(1)}, u32[]{:S(2)}, u32[]{:S(2)}) collective-permute-start(f32[2,2,288]{2,1,0:T(2,128)S(1)} %fusion.54), channel_id=1, source_target_pairs={{0,4},{4,0},{1,5},{5,1},{2,6},{6,2},{3,7},{7,3},{8,12},{12,8},{9,1... | collective-permute-start | bytes 13832 | tf_op jit(solution)/shard_map/ppermute | solution.py:89
  330.0 19.0 %collective-permute-start.73 = (f32[2,288]{1,0:T(2,128)S(1)}, f32[2,288]{1,0:T(2,128)S(1)}, u32[]{:S(2)}, u32[]{:S(2)}) collective-permute-start(f32[2,288]{1,0:T(2,128)S(1)} %bitcast.262), channel_id=1, source_target_pairs={{0,1},{1,0},{2,3},{3,2},{4,5},{5,4},{6,7},{7,6},{8,9},{9,8},{10,11... | collective-permute-start | bytes 6920 | tf_op jit(solution)/shard_map/ppermute | solution.py:89
  335.1 29.3 %collective-permute-start.56 = (bf16[8,96,768]{2,1,0:T(8,128)(2,1)}, bf16[8,96,768]{2,1,0:T(8,128)(2,1)}, u32[]{:S(2)}, u32[]{:S(2)}) collective-permute-start(bf16[8,96,768]{2,1,0:T(8,128)(2,1)} %get-tuple-element.46), channel_id=1, source_target_pairs={{0,8},{8,0},{1,9},{9,1},{2,10},{10,2},{3,11},{11,3},{4,12},{12,4},... | collective-permute-start | bytes 3538952 | tf_op jit(solution)/shard_map/ppermute | solution.py:89
  339.4 48.4 %collective-permute-start.61 = (bf16[8,96,768]{2,1,0:T(8,128)(2,1)}, bf16[8,96,768]{2,1,0:T(8,128)(2,1)S(1)}, u32[]{:S(2)}, u32[]{:S(2)}) collective-permute-start(bf16[8,96,768]{2,1,0:T(8,128)(2,1)} %get-tuple-element.48), channel_id=1, source_target_pairs={{0,8},{8,0},{1,9},{9,1},{2,10},{10,2},{3,11},{11,3},{4,12},{12,4},... | collective-permute-start | bytes 3538952 | tf_op jit(solution)/shard_map/ppermute | solution.py:89
  343.2 46.2 %collective-permute-start.66 = (bf16[8,96,768]{2,1,0:T(8,128)(2,1)S(1)}, bf16[8,96,768]{2,1,0:T(8,128)(2,1)S(1)}, u32[]{:S(2)}, u32[]{:S(2)}) collective-permute-start(bf16[8,96,768]{2,1,0:T(8,128)(2,1)S(1)} %get-tuple-element.50), channel_id=1, source_target_pairs={{0,1},{1,0},{2,3},{3,2},{4,5},{5,4},{6,7},{7,6},{8,9},{9,8},{10,11... | collective-permute-start | bytes 3538952 | tf_op jit(solution)/shard_map/ppermute | solution.py:89
  349.0 42.3 %collective-permute-start.74 = (f32[288]{0:T(512)S(1)}, f32[288]{0:T(512)S(1)}, u32[]{:S(2)}, u32[]{:S(2)}) collective-permute-start(f32[288]{0:T(512)S(1)} %get-tuple-element.39), channel_id=1, source_target_pairs={{0,16},{16,0},{1,17},{17,1},{2,18},{18,2},{3,19},{19,3},{4,20},{20... | collective-permute-start | bytes 3464 | tf_op jit(solution)/shard_map/ppermute | solution.py:89
  365.9 26.1 %collective-permute-start.57 = (bf16[4,96,768]{2,1,0:T(8,128)(2,1)S(1)}, bf16[4,96,768]{2,1,0:T(8,128)(2,1)S(1)}, u32[]{:S(2)}, u32[]{:S(2)}) collective-permute-start(bf16[4,96,768]{2,1,0:T(8,128)(2,1)S(1)} %get-tuple-element.55), channel_id=1, source_target_pairs={{0,4},{4,0},{1,5},{5,1},{2,6},{6,2},{3,7},{7,3},{8,12},{12,8},{9,1... | collective-permute-start | bytes 1769480 | tf_op jit(solution)/shard_map/ppermute | solution.py:89
  388.2 16.3 %collective-permute-start.62 = (bf16[4,96,768]{2,1,0:T(8,128)(2,1)S(1)}, bf16[4,96,768]{2,1,0:T(8,128)(2,1)S(1)}, u32[]{:S(2)}, u32[]{:S(2)}) collective-permute-start(bf16[4,96,768]{2,1,0:T(8,128)(2,1)S(1)} %get-tuple-element.57), channel_id=1, source_target_pairs={{0,1},{1,0},{2,3},{3,2},{4,5},{5,4},{6,7},{7,6},{8,9},{9,8},{10,11... | collective-permute-start | bytes 1769480 | tf_op jit(solution)/shard_map/ppermute | solution.py:89
  389.8 16.1 %collective-permute-start.67 = (bf16[4,96,768]{2,1,0:T(8,128)(2,1)S(1)}, bf16[4,96,768]{2,1,0:T(8,128)(2,1)S(1)}, u32[]{:S(2)}, u32[]{:S(2)}) collective-permute-start(bf16[4,96,768]{2,1,0:T(8,128)(2,1)S(1)} %get-tuple-element.59), channel_id=1, source_target_pairs={{0,8},{8,0},{1,9},{9,1},{2,10},{10,2},{3,11},{11,3},{4,12},{12,4},... | collective-permute-start | bytes 1769480 | tf_op jit(solution)/shard_map/ppermute | solution.py:89
  392.2 16.1 %collective-permute-start.58 = (bf16[2,96,768]{2,1,0:T(8,128)(2,1)S(1)}, bf16[2,96,768]{2,1,0:T(8,128)(2,1)S(1)}, u32[]{:S(2)}, u32[]{:S(2)}) collective-permute-start(bf16[2,96,768]{2,1,0:T(8,128)(2,1)S(1)} %get-tuple-element.63), channel_id=1, source_target_pairs={{0,1},{1,0},{2,3},{3,2},{4,5},{5,4},{6,7},{7,6},{8,9},{9,8},{10,11... | collective-permute-start | bytes 884744 | tf_op jit(solution)/shard_map/ppermute | solution.py:89
  404.7 7.0 %collective-permute-start.63 = (bf16[2,96,768]{2,1,0:T(8,128)(2,1)S(1)}, bf16[2,96,768]{2,1,0:T(8,128)(2,1)S(1)}, u32[]{:S(2)}, u32[]{:S(2)}) collective-permute-start(bf16[2,96,768]{2,1,0:T(8,128)(2,1)S(1)} %get-tuple-element.65), channel_id=1, source_target_pairs={{0,4},{4,0},{1,5},{5,1},{2,6},{6,2},{3,7},{7,3},{8,12},{12,8},{9,1... | collective-permute-start | bytes 884744 | tf_op jit(solution)/shard_map/ppermute | solution.py:89
  406.0 8.8 %collective-permute-start.68 = (bf16[2,96,768]{2,1,0:T(8,128)(2,1)S(1)}, bf16[2,96,768]{2,1,0:T(8,128)(2,1)S(1)}, u32[]{:S(2)}, u32[]{:S(2)}) collective-permute-start(bf16[2,96,768]{2,1,0:T(8,128)(2,1)S(1)} %get-tuple-element.67), channel_id=1, source_target_pairs={{0,4},{4,0},{1,5},{5,1},{2,6},{6,2},{3,7},{7,3},{8,12},{12,8},{9,1... | collective-permute-start | bytes 884744 | tf_op jit(solution)/shard_map/ppermute | solution.py:89
  408.3 14.8 %collective-permute-start.59 = (bf16[1,96,768]{2,1,0:T(8,128)(2,1)S(1)}, bf16[1,96,768]{2,1,0:T(8,128)(2,1)S(1)}, u32[]{:S(2)}, u32[]{:S(2)}) collective-permute-start(bf16[1,96,768]{2,1,0:T(8,128)(2,1)S(1)} %add_convert_fusion.22), channel_id=1, source_target_pairs={{0,16},{16,0},{1,17},{17,1},{2,18},{18,2},{3,19},{19,3},{4,20},{20... | collective-permute-start | bytes 442376 | tf_op jit(solution)/shard_map/ppermute | solution.py:89
  411.7 14.5 %collective-permute-start.64 = (bf16[1,96,768]{2,1,0:T(8,128)(2,1)S(1)}, bf16[1,96,768]{2,1,0:T(8,128)(2,1)S(1)}, u32[]{:S(2)}, u32[]{:S(2)}) collective-permute-start(bf16[1,96,768]{2,1,0:T(8,128)(2,1)S(1)} %add_convert_fusion.20), channel_id=1, source_target_pairs={{0,16},{16,0},{1,17},{17,1},{2,18},{18,2},{3,19},{19,3},{4,20},{20... | collective-permute-start | bytes 442376 | tf_op jit(solution)/shard_map/ppermute | solution.py:89
  414.9 13.4 %collective-permute-start.69 = (bf16[1,96,768]{2,1,0:T(8,128)(2,1)S(1)}, bf16[1,96,768]{2,1,0:T(8,128)(2,1)S(1)}, u32[]{:S(2)}, u32[]{:S(2)}) collective-permute-start(bf16[1,96,768]{2,1,0:T(8,128)(2,1)S(1)} %add_convert_fusion.18), channel_id=1, source_target_pairs={{0,16},{16,0},{1,17},{17,1},{2,18},{18,2},{3,19},{19,3},{4,20},{20... | collective-permute-start | bytes 442376 | tf_op jit(solution)/shard_map/ppermute | solution.py:89
  (49 other events, 530.5 us)

commit v3 on v2

--- a/solution.py
+++ b/solution.py
@@ -119,7 +119,7 @@
     outer = [name for name in names if name != core]
     count = len(outer)
     if count == 4:
-        picks = ((0, 3, 2, 1), (0, 2, 3, 1), (0, 2, 1, 3))
+        picks = ((0, 3, 2, 1), (0, 2, 1, 3), (0, 1, 3, 2))
         return [[outer[k] for k in pick] + [core] for pick in picks]
     step = max(1, count // 3)
     return [outer[step * k :] + outer[: step * k] + [core] for k in range(3)]
@@ -129,29 +129,52 @@
     return 1 << (len(names) - 1 - names.index(name))
 
 
-def gather_relative(shard, order, names):
-    grown, masks = shard[None], [0]
-    for name in order[:-2]:
-        grown = jnp.concatenate([grown, flip(grown, name)])
-        masks = masks + [mask | device_mask(name, names) for mask in masks]
-    pieces = [(grown, masks)]
-    for name in order[-2:]:
-        bit = device_mask(name, names)
-        pieces = pieces + [(flip(piece, name), [mask | bit for mask in own]) for piece, own in pieces]
-    return pieces
-
-
-def reduce_relative(keep, send, order):
-    for name in order:
-        other = flip(send, name)
-        half = keep.shape[0] // 2
-        total = [
-            keep[part].astype(jnp.float32) + other[part].astype(jnp.float32)
-            for part in ((slice(half, None), slice(0, half)) if half else (slice(0, None),))
+def gather_relative(shards, orders, names, early=(), work=None):
+    held = []
+    for shard, order in zip(shards, orders):
+        grown, masks = shard[None], [0]
+        for name in order[:-2]:
+            grown = jnp.concatenate([grown, flip(grown, name)])
+            masks = masks + [mask | device_mask(name, names) for mask in masks]
+        held.append((grown, masks))
+    grown_all = [grown for grown, _ in held]
+    others = [flip(grown, order[-2]) for grown, order in zip(grown_all, orders)]
+    if work is not None:
+        grown_late, early = lax.optimization_barrier((grown_all, early))
+        grown_all, early = lax.optimization_barrier((grown_late, work(*early)))
+    gathered = []
+    for grown, other, (_, masks), order in zip(grown_all, others, held, orders):
+        bit = device_mask(order[-2], names)
+        pieces = [(grown, masks), (other, [mask | bit for mask in masks])]
+        bit = device_mask(order[-1], names)
+        pieces = pieces + [
+            (flip(piece, order[-1]), [mask | bit for mask in own]) for piece, own in pieces
         ]
-        if half:
-            send, keep = (value.astype(keep.dtype) for value in total)
-    return total[0][0]
+        gathered.append(pieces)
+    return gathered, early
+
+
+def add_terms(terms):
+    total = terms[0].astype(jnp.float32)
+    for term in terms[1:]:
+        total = total + term.astype(jnp.float32)
+    return total
+
+
+def reduce_relative(keeps, sends, orders, late):
+    terms_all = [[keep] for keep in keeps]
+    sends = list(sends)
+    for step in range(len(orders[0])):
+        for k, order in enumerate(orders):
+            terms = terms_all[k] + [flip(sends[k], order[step])]
+            half = terms[0].shape[0] // 2
+            if half:
+                sends[k] = add_terms([term[half:] for term in terms]).astype(terms[0].dtype)
+                terms = [term[:half] for term in terms]
+            terms_all[k] = terms
+        if step == 0 and late:
+            sends[-1], late = lax.optimization_barrier((sends[-1], late))
+    return [add_terms(terms)[0] for terms in terms_all], late
 
 
 def dot_nn(left, right):
@@ -327,10 +350,8 @@
         for u in range(first // unit, last // unit):
             part = u % 3
             relative = (u // 3) ^ me
-            spot = jnp.int32(0)
             bits, core_bit = plan[part]
-            for k, bit in enumerate(bits):
-                spot = spot + jnp.where((relative & bit) != 0, 1 << (len(bits) - 1 - k), 0)
+            spot = sink_spot(relative, bits)
             across = (relative & core_bit) != 0
             source = grads.at[u * unit : (u + 1) * unit]
 
@@ -513,6 +534,223 @@
     )(me, lengths, places, rows, vecs, top, *saved)
 
 
+def turn_lanes(shift, width):
+    source = lax.broadcasted_iota(jnp.int32, (width, width), 0) + shift
+    source = jnp.where(source >= width, source - width, source)
+    return (source == lax.broadcasted_iota(jnp.int32, (width, width), 1)).astype(jnp.bfloat16)
+
+
+def table_kernel(embed_here, shift_ref, rows_ref, ends_ref, table_ref, owned_ref, tall):
+    count, width = table_ref.shape
+    here = rows_ref.shape[0]
+    shift = shift_ref[0]
+    tall[here:, :] = jnp.zeros((tall.shape[0] - here, width), jnp.float32)
+    tall[8 : 8 + here, :] = rows_ref[...].astype(jnp.float32)
+    tall[7:8, :] = ends_ref[0:1, :]
+    tall[7 + here : 8 + here, :] = tall[7 + here : 8 + here, :] + ends_ref[1:2, :]
+    tall[8 + here : 9 + here, :] = ends_ref[2:3, :]
+    lane = lax.broadcasted_iota(jnp.int32, (count, width), 1)
+    rolled = jnp.where(lane < width - shift, tall[8 : 8 + count, :], tall[7 : 7 + count, :])
+    table = dot_nn(rolled.astype(jnp.bfloat16), turn_lanes(shift, width))
+    start = lax.broadcasted_iota(jnp.int32, (count, 1), 0) * width - shift
+    owned = (start >= 0) & (start < embed_here)
+    table_ref[...] = table.astype(jnp.bfloat16)
+    owned_ref[...] = jnp.where(owned, table, 0.0).astype(jnp.bfloat16)
+
+
+def call_table(shift, rows, ends, count, embed_here):
+    width = rows.shape[1]
+    vmem = pl.BlockSpec(memory_space=pltpu.VMEM)
+    smem = pl.BlockSpec(memory_space=pltpu.SMEM)
+    return pl.pallas_call(
+        functools.partial(table_kernel, embed_here),
+        out_shape=[jax.ShapeDtypeStruct((count, width), jnp.bfloat16)] * 2,
+        in_specs=[smem, vmem, vmem],
+        out_specs=[vmem] * 2,
+        scratch_shapes=[pltpu.VMEM((count + 16, width), jnp.float32)],
+        compiler_params=pltpu.CompilerParams(vmem_limit_bytes=32 * 2**20),
+        cost_estimate=pl.CostEstimate(
+            flops=32 * count * width * width, bytes_accessed=40 * 2**20, transcendentals=0
+        ),
+    )(shift, rows, ends)
+
+
+def logits_kernel(plan, embed_here, picks, span, *refs):
+    me_ref, shift_ref, table_ref = refs[:3]
+    blocks = refs[3 : 3 + len(plan)]
+    picked, first, expo_ref, stat_ref, in_sem = refs[3 + len(plan) :]
+    count, width = table_ref.shape
+    me, shift = me_ref[0], shift_ref[0]
+    extra = first.shape[1]
+    for (part, masks), block in zip(plan, blocks):
+        cut = block.shape[2]
+        cols = pl.ds(part * cut, cut)
+        for place, mask in enumerate(masks):
+            device = me ^ mask
+            row = pl.multiple_of(device * picks, 16)
+            pltpu.make_async_copy(
+                block.at[place, pl.ds(0, picks)], picked.at[pl.ds(row, picks), cols], in_sem.at[0]
+            ).start()
+            pltpu.make_async_copy(
+                block.at[place, pl.ds(picks, extra)], first.at[device, :, cols], in_sem.at[1]
+            ).start()
+    start = lax.broadcasted_iota(jnp.int32, (count, 1), 0) * width - shift
+    owned = (start >= 0) & (start < embed_here)
+    touched = (start > -width) & (start < embed_here)
+    pltpu.make_async_copy(first, first, in_sem.at[1]).wait()
+    pltpu.make_async_copy(picked, picked, in_sem.at[0]).wait()
+    chunks = picked.shape[0] // span
+    for k in range(chunks):
+        here = slice(k * span, (k + 1) * span)
+        logits = jnp.where(touched, contract_cols(table_ref[...], picked[here, :]), -1e30)
+        top = jnp.max(logits, axis=0, keepdims=True)
+        expo = jnp.where(touched, jnp.exp(logits - top), 0.0)
+        total = jnp.sum(jnp.where(owned, expo, 0.0), axis=0, keepdims=True)
+        expo_ref[:, here] = expo
+        copies = stat_ref.shape[0]
+        stat_ref[:, k : k + 1, :] = jnp.broadcast_to(top[None], (copies, 1, span))
+        stat_ref[:, chunks + k : chunks + k + 1, :] = jnp.broadcast_to(
+            total[None], (copies, 1, span)
+        )
+
+
+def call_logits(me, shift, table, gathered, picks, embed_here, devices):
+    count, width = table.shape
+    pieces = [(part, piece, masks) for part, own in enumerate(gathered) for piece, masks in own]
+    plan = tuple((part, tuple(masks)) for part, _, masks in pieces)
+    extra = pieces[0][1].shape[1] - picks
+    rows = devices * picks
+    span = rows // 4
+    vmem = pl.BlockSpec(memory_space=pltpu.VMEM)
+    smem = pl.BlockSpec(memory_space=pltpu.SMEM)
+    hbm = pl.BlockSpec(memory_space=pl.ANY)
+    low, full = jnp.bfloat16, jnp.float32
+    return pl.pallas_call(
+        functools.partial(logits_kernel, plan, embed_here, picks, span),
+        out_shape=[
+            jax.ShapeDtypeStruct((rows, width), low),
+            jax.ShapeDtypeStruct((devices, extra, width), low),
+            jax.ShapeDtypeStruct((count, rows), full),
+            jax.ShapeDtypeStruct((devices, 8, span), full),
+        ],
+        in_specs=[smem, smem, vmem] + [hbm] * len(pieces),
+        out_specs=[vmem] * 4,
+        scratch_shapes=[pltpu.SemaphoreType.DMA((2,))],
+        compiler_params=pltpu.CompilerParams(vmem_limit_bytes=48 * 2**20),
+        cost_estimate=pl.CostEstimate(
+            flops=2 * rows * count * width, bytes_accessed=16 * 2**20, transcendentals=0
+        ),
+    )(me, shift, table, *[piece for _, piece, _ in pieces])
+
+
+def sink_spot(relative, bits):
+    spot = jnp.int32(0)
+    for k, bit in enumerate(bits):
+        spot = spot + jnp.where((relative & bit) != 0, 1 << (len(bits) - 1 - k), 0)
+    return spot
+
+
+def picked_kernel(plan, embed_here, picks, *refs):
+    me_ref, shift_ref, stat_ref, expo_ref, label_ref, owned_ref, dlog_ref = refs[:7]
+    sinks = refs[7:13]
+    terms, out_sem = refs[13:]
+    count, width = owned_ref.shape
+    me, shift = me_ref[0], shift_ref[0]
+    span = stat_ref.shape[2]
+    chunks = expo_ref.shape[1] // span
+    start = lax.broadcasted_iota(jnp.int32, (count, 1), 0) * width - shift
+    touched = (start > -width) & (start < embed_here)
+    row = lax.broadcasted_iota(jnp.int32, (count, span), 0)
+    mine = stat_ref[pl.ds(me, 1)]
+    for k in range(chunks):
+        here = slice(k * span, (k + 1) * span)
+        tops = stat_ref[:, k : k + 1, :]
+        top = jnp.max(tops, axis=0)
+        total = jnp.sum(
+            stat_ref[:, chunks + k : chunks + k + 1, :] * jnp.exp(tops - top[None]), axis=0
+        )
+        scale = jnp.exp(mine[0, k : k + 1, :] - top) / total
+        hot = (row == label_ref[0:1, here]) & touched
+        used = label_ref[1:2, here] > 0
+        probs = expo_ref[:, here] * scale
+        d_logits = jnp.where(used, jnp.where(hot, probs - 1.0, probs), 0.0).astype(jnp.bfloat16)
+        dlog_ref[:, here] = d_logits
+        terms[here, :] = contract_rows(d_logits, owned_ref[...]).astype(jnp.bfloat16)
+        for b in range(span // picks):
+            device = k * (span // picks) + b
+            for part, (bits, core_bit) in enumerate(plan):
+                relative = device ^ me
+                spot = sink_spot(relative, bits)
+                across = (relative & core_bit) != 0
+                cut = width // len(plan)
+                source = terms.at[
+                    device * picks : (device + 1) * picks, part * cut : (part + 1) * cut
+                ]
+
+                @pl.when(across)
+                def _(part=part, source=source, spot=spot):
+                    pltpu.make_async_copy(
+                        source, sinks[2 * part + 1].at[spot], out_sem.at[2 * part + 1]
+                    ).start()
+
+                @pl.when(jnp.logical_not(across))
+                def _(part=part, source=source, spot=spot):
+                    pltpu.make_async_copy(
+                        source, sinks[2 * part].at[spot], out_sem.at[2 * part]
+                    ).start()
+
+    for k, sink in enumerate(sinks):
+        pltpu.make_async_copy(sink, sink, out_sem.at[k]).wait()
+
+
+def call_picked(me, shift, stats, expo, labels, owned, plan, picks, embed_here):
+    count, width = owned.shape
+    devices, rows = stats.shape[0], expo.shape[1]
+    vmem = pl.BlockSpec(memory_space=pltpu.VMEM)
+    smem = pl.BlockSpec(memory_space=pltpu.SMEM)
+    hbm = pl.BlockSpec(memory_space=pl.ANY)
+    low = jnp.bfloat16
+    return pl.pallas_call(
+        functools.partial(picked_kernel, plan, embed_here, picks),
+        out_shape=[jax.ShapeDtypeStruct((count, rows), low)]
+        + [jax.ShapeDtypeStruct((devices // 2, picks, width // 3), low)] * 6,
+        in_specs=[smem, smem, vmem, vmem, vmem, vmem],
+        out_specs=[vmem] + [hbm] * 6,
+        scratch_shapes=[pltpu.VMEM((rows, width), low), pltpu.SemaphoreType.DMA((6,))],
+        compiler_params=pltpu.CompilerParams(vmem_limit_bytes=48 * 2**20),
+        cost_estimate=pl.CostEstimate(
+            flops=2 * rows * count * width, bytes_accessed=16 * 2**20, transcendentals=0
+        ),
+    )(me, shift, stats, expo, labels, owned)
+
+
+def embed_kernel(shift_ref, dlog_ref, picked_ref, out_ref, wide):
+    here, width = out_ref.shape
+    shift = shift_ref[0]
+    turned = contract_cols(picked_ref[...], turn_lanes(shift, width)).astype(jnp.bfloat16)
+    wide[...] = dot_nn(dlog_ref[...], turned)
+    lane = lax.broadcasted_iota(jnp.int32, (here, width), 1)
+    out_ref[...] = jnp.where(lane < width - shift, wide[:here, :], wide[1 : here + 1, :])
+
+
+def call_embed(shift, dlog, picked, here):
+    count, rows = dlog.shape
+    width = picked.shape[1]
+    vmem = pl.BlockSpec(memory_space=pltpu.VMEM)
+    smem = pl.BlockSpec(memory_space=pltpu.SMEM)
+    return pl.pallas_call(
+        embed_kernel,
+        out_shape=jax.ShapeDtypeStruct((here, width), jnp.float32),
+        in_specs=[smem, vmem, vmem],
+        out_specs=vmem,
+        scratch_shapes=[pltpu.VMEM((count, width), jnp.float32)],
+        compiler_params=pltpu.CompilerParams(vmem_limit_bytes=40 * 2**20),
+        cost_estimate=pl.CostEstimate(
+            flops=16 * rows * count * width, bytes_accessed=64 * 2**20, transcendentals=0
+        ),
+    )(shift, dlog, picked)
+
+
 def plain_forward(mats_all, vecs_all, block_input, span_lengths):
     seq_here, length, width = block_input.shape
     rows_here = seq_here * length
@@ -684,15 +922,24 @@
             pad_row(labels_flat // 256),
             pad_row(labels_flat % 256),
             pad_row(jnp.concatenate([span_pairs // 256, span_pairs % 256, span_lengths // 4])),
-            jnp.zeros((4, width), low),
+            embedding[-width:].astype(low)[None],
+            embedding[:width].astype(low)[None],
+            jnp.zeros((2, width), low),
         ]
     )
-    small_all = gather_bits(small, orders[0], names)
-    if by_kernel:
-        gathered = [gather_relative(mats_low[k], orders[k], names) for k in range(3)]
-    else:
-        gathered = [gather_bits(mats_low[k], orders[k], names) for k in range(3)]
-    vecs_all = small_all[:, 0, :vec_here].reshape(-1)
+    small_all = lax.all_to_all(
+        jnp.broadcast_to(small, (devices,) + small.shape), names, 0, 0, tiled=True
+    )
+    embed_here = embedding.shape[0]
+    shifted_rows = -(-embed_here // width)
+    over = shifted_rows * width - embed_here
+    shift = (me * (embed_here % width)) % width
+    first_row = me * (embed_here // width) + (me * (embed_here % width)) // width
+    shifted = jnp.pad(embedding.astype(low), (0, over)).reshape(shifted_rows, width)
+    from_left = lax.dynamic_index_in_dim(small_all[:, 4], (me + devices - 1) % devices, 0, False)
+    from_right = lax.dynamic_index_in_dim(small_all[:, 5], (me + 1) % devices, 0, False)
+    right_rows = jnp.pad(from_right, (width - over, over)).reshape(2, width)
+    vec_rows = small_all[:, 0, :vec_here].reshape(-1).astype(jnp.float32).reshape(-1, width)
     labels_all = (
         small_all[:, 1, :picks_here].astype(jnp.int32) * 256
         + small_all[:, 2, :picks_here].astype(jnp.int32)
@@ -700,131 +947,129 @@
     ints_all = small_all[:, 3, : 3 * seq_here].astype(jnp.int32)
     pairs_all = (ints_all[:, :seq_here] * 256 + ints_all[:, seq_here : 2 * seq_here]).reshape(-1)
     quarter_all = ints_all[:, 2 * seq_here :].reshape(-1)
-
-    embed_here = embedding.shape[0]
-    shifted_rows = -(-embed_here // width)
-    shift = (me * (embed_here % width)) % width
-    first_row = me * (embed_here // width) + (me * (embed_here % width)) // width
-    embed_low = embedding.astype(low)
-    ring = range(devices)
-    from_left = lax.ppermute(embed_low[-width:], names, [(k, (k + 1) % devices) for k in ring])
-    from_right = lax.ppermute(embed_low[:width], names, [((k + 1) % devices, k) for k in ring])
-    shifted = jnp.concatenate(
-        [
-            from_left,
-            embed_low,
-            from_right,
-            jnp.zeros((shifted_rows * width - embed_here,), low),
-        ]
-    ).reshape(shifted_rows + 2, width)
-    lanes = jnp.arange(width)
-    same_row = (lanes < width - shift)[None, :]
-    rolled = jnp.where(same_row, shifted[1:], shifted[:-1])
-    turn = ((lanes[:, None] + shift) % width == lanes[None, :]).astype(low)
-    table = jnp.dot(rolled, turn, preferred_element_type=jnp.float32).astype(low)
-    row_start = jnp.arange(shifted_rows + 1) * width - shift
-    owned = (row_start >= 0) & (row_start < embed_here)
-    touched = (row_start + width > 0) & (row_start < embed_here)
-    table_owned = jnp.where(owned[:, None], table, 0)
-
-    heads_pad = -(picks_here + seq_here) % 8
+    row_of = labels_all - first_row
+    used = (jnp.arange(slots)[None, :] < quarter_all[:, None]).reshape(-1)
     seq_start = jnp.arange(seq_here, dtype=jnp.int32) * length
+
+    def span_terms(cls_all):
+        span_scale = 2.0 / math.sqrt(width)
+        columns = jnp.arange(cls_all.shape[0])
+        sims = contract_cols(cls_all, cls_all) * span_scale
+        sims = jnp.where(columns[None, :] == columns[:, None], -1e30, sims)
+        partner_hot = (columns[None, :] == pairs_all[:, None]).astype(jnp.float32)
+        d_sims = (jax.nn.softmax(sims, axis=-1) - partner_hot).astype(low)
+        mine = me * seq_here
+        d_sims_rows = lax.dynamic_slice_in_dim(d_sims, mine, seq_here, 0)
+        d_sims_cols = lax.dynamic_slice_in_dim(d_sims, mine, seq_here, 1)
+        return (
+            jnp.dot(d_sims_rows, cls_all, preferred_element_type=jnp.float32)
+            + contract_rows(d_sims_cols, cls_all)
+        ) * span_scale
+
+    step_float = float(ADAM_STEP)
+    cut = width // 3
+    columns = [slice(k * cut, (k + 1) * cut) for k in range(3)]
+    back_orders = [order[::-1] for order in orders]
     if by_kernel:
         lone = me.astype(jnp.int32).reshape(1)
+        lone_shift = shift.astype(jnp.int32).reshape(1)
         tok_rows = block_input.reshape(rows_here, width)
-        vec_rows = vecs_all.astype(jnp.float32).reshape(-1, width)
+        head_rows = picks_here + 16
         places = jnp.concatenate(
             [
                 (mlm_positions + seq_start[:, None]).reshape(-1),
                 seq_start,
-                jnp.full((heads_pad,), -1, jnp.int32),
+                jnp.full((16 - seq_here,), -1, jnp.int32),
             ]
         )
-        heads_rows, *saved = call_forward(
+        ends = jnp.pad(
+            jnp.concatenate([from_left[None], right_rows]).astype(jnp.float32), ((0, 5), (0, 0))
+        )
+        table_rows = -(-(shifted_rows + 1) // 16) * 16
+        labels = jnp.pad(
+            jnp.stack([row_of, used.astype(jnp.int32)]).astype(jnp.int32), ((0, 6), (0, 0))
+        )
+
+        def prepare(shifted, ends, vec_rows, labels):
+            table, owned = call_table(lone_shift, shifted, ends, table_rows, embed_here)
+            return table, owned, vec_rows, labels
+
+        gathered, (table, owned, vec_rows, labels) = gather_relative(
+            mats_low, orders, names, (shifted, ends, vec_rows, labels), prepare
+        )
+        heads, *saved = call_forward(
             lone, span_lengths, places[:, None], tok_rows, vec_rows, gathered, seq_here
         )
+        heads_all, _ = gather_relative([heads[:, c] for c in columns], orders, names)
+        picked, cls_rows, expo, stats = call_logits(
+            lone, lone_shift, table, heads_all, picks_here, embed_here, devices
+        )
+        stats = lax.all_to_all(stats, names, 0, 0, tiled=True)
+        plan = tuple(
+            (tuple(device_mask(name, names) for name in order[1:]), device_mask(order[0], names))
+            for order in back_orders
+        )
+        d_logits, *sinks = call_picked(
+            lone, lone_shift, stats, expo, labels, owned, plan, picks_here, embed_here
+        )
+        d_cls = span_terms(cls_rows[:, :seq_here].reshape(-1, width))
+        d_parts, _ = reduce_relative(sinks[0::2], sinks[1::2], back_orders, ())
+        top = jnp.concatenate(
+            [jnp.concatenate(d_parts, axis=1), jnp.pad(d_cls, ((0, 16 - seq_here), (0, 0)))]
+        )
+        grad_input, d_vecs, *sinks = call_backward(
+            lone, span_lengths, places[None], tok_rows, vec_rows, top, saved, plan, third, seq_here
+        )
+        grad_input = grad_input.reshape(seq_here, length, width)
+        summed, (d_logits, picked, d_vecs) = reduce_relative(
+            sinks[0::2], sinks[1::2], back_orders, (d_logits, picked, d_vecs)
+        )
+        grad_embed = call_embed(lone_shift, d_logits, picked, shifted_rows)
     else:
+        same_row = (jnp.arange(width) < width - shift)[None, :]
+        tall = jnp.concatenate([from_left[None], shifted, jnp.zeros((1, width), low)])
+        tall = tall.at[shifted_rows : shifted_rows + 2].add(right_rows)
+        lanes = jnp.arange(width)
+        turn = ((lanes[:, None] + shift) % width == lanes[None, :]).astype(low)
+        rolled = jnp.where(same_row, tall[1:], tall[:-1])
+        table = jnp.dot(rolled, turn, preferred_element_type=jnp.float32).astype(low)
+        row_start = jnp.arange(shifted_rows + 1) * width - shift
+        owned = (row_start >= 0) & (row_start < embed_here)
+        touched = (row_start + width > 0) & (row_start < embed_here)
+        gathered = [gather_bits(mats_low[k], orders[k], names) for k in range(3)]
         mats_all = jnp.stack(gathered, axis=1).reshape(-1)
-        output, plain_backward = plain_forward(mats_all, vecs_all, block_input, span_lengths)
+        output, plain_backward = plain_forward(
+            mats_all, vec_rows.reshape(-1), block_input, span_lengths
+        )
         output_seq = output.reshape(seq_here, length, width)
         picked_here = jnp.take_along_axis(output_seq, mlm_positions[:, :, None], axis=1)
-        heads_rows = jnp.concatenate(
+        heads = jnp.concatenate([picked_here.reshape(-1, width), output_seq[:, 0, :]]).astype(low)
+        heads_all = jnp.concatenate(
+            [gather_bits(heads[:, c], order, names) for c, order in zip(columns, orders)], axis=2
+        )
+        picked = heads_all[:, :picks_here, :].reshape(-1, width)
+        logits = contract_cols(picked, table)
+        masked = jnp.where(owned[None, :], logits, -jnp.inf)
+        part_max = jnp.max(masked, axis=-1)
+        part_sum = jnp.sum(jnp.exp(masked - part_max[:, None]), axis=-1)
+        full_max = lax.pmax(part_max, names)
+        full_sum = lax.psum(part_sum * jnp.exp(part_max - full_max), names)
+        hot = row_of[:, None] == jnp.arange(shifted_rows + 1)[None, :]
+        probs = jnp.exp(logits - full_max[:, None]) / full_sum[:, None]
+        d_logits = jnp.where(
+            used[:, None] & touched[None, :], probs - hot.astype(jnp.float32), 0.0
+        ).astype(low)
+        d_picked = jnp.dot(
+            d_logits, jnp.where(owned[:, None], table, 0), preferred_element_type=jnp.float32
+        )
+        blocks = d_picked.astype(low).reshape(devices, picks_here, width)
+        d_picked = jnp.concatenate(
             [
-                picked_here.reshape(-1, width),
-                output_seq[:, 0, :],
-                jnp.zeros((heads_pad, width), jnp.float32),
-            ]
-        ).astype(low)
-
-    cut = width // 3
-    heads_all = jnp.concatenate(
-        [
-            gather_bits(heads_rows[:, k * cut : (k + 1) * cut], orders[k], names)
-            for k in range(3)
-        ],
-        axis=2,
-    )
-    picked = heads_all[:, :picks_here, :].reshape(-1, width)
-    cls_all = heads_all[:, picks_here : picks_here + seq_here, :].reshape(-1, width)
-
-    logits = contract_cols(picked, table)
-    masked = jnp.where(owned[None, :], logits, -jnp.inf)
-    part_max = jnp.max(masked, axis=-1)
-    part_sum = jnp.sum(jnp.exp(masked - part_max[:, None]), axis=-1)
-    stats = jnp.stack([part_max, part_sum]).reshape(1, -1, 128)
-    stats_all = lax.all_to_all(
-        jnp.broadcast_to(stats, (devices,) + stats.shape[1:]), names, 0, 0, tiled=True
-    ).reshape(devices, 2, -1)
-    full_max = jnp.max(stats_all[:, 0], axis=0)
-    full_sum = jnp.sum(stats_all[:, 1] * jnp.exp(stats_all[:, 0] - full_max), axis=0)
-    row_of = labels_all - first_row
-    hot = row_of[:, None] == jnp.arange(shifted_rows + 1)[None, :]
-    used = (jnp.arange(slots)[None, :] < quarter_all[:, None]).reshape(-1, 1)
-    probs = jnp.exp(logits - full_max[:, None]) / full_sum[:, None]
-    d_logits = jnp.where(
-        used & touched[None, :], probs - hot.astype(jnp.float32), 0.0
-    ).astype(low)
-    d_picked_part = jnp.dot(d_logits, table_owned, preferred_element_type=jnp.float32).astype(low)
-    blocks = d_picked_part.reshape(devices, picks_here, width)
-    d_picked = jnp.concatenate(
-        [
-            reduce_bits(blocks[:, :, k * cut : (k + 1) * cut], orders[k][::-1], names)
-            for k in range(3)
-        ],
-        axis=1,
-    ).astype(jnp.float32)
-
-    span_scale = 2.0 / math.sqrt(width)
-    columns = jnp.arange(cls_all.shape[0])
-    sims = contract_cols(cls_all, cls_all) * span_scale
-    sims = jnp.where(columns[None, :] == columns[:, None], -1e30, sims)
-    partner_hot = (columns[None, :] == pairs_all[:, None]).astype(jnp.float32)
-    d_sims = (jax.nn.softmax(sims, axis=-1) - partner_hot).astype(low)
-    mine = me * seq_here
-    d_sims_rows = lax.dynamic_slice_in_dim(d_sims, mine, seq_here, 0)
-    d_sims_cols = lax.dynamic_slice_in_dim(d_sims, mine, seq_here, 1)
-    d_cls = (
-        jnp.dot(d_sims_rows, cls_all, preferred_element_type=jnp.float32)
-        + contract_rows(d_sims_cols, cls_all)
-    ) * span_scale
-    if by_kernel:
-        top = jnp.concatenate([d_picked, d_cls, jnp.zeros((heads_pad, width), jnp.float32)])
-        back_orders = [order[::-1] for order in orders]
-        plan = tuple(
-            (
-                tuple(device_mask(name, names) for name in order[1:]),
-                device_mask(order[0], names),
-            )
-            for order in back_orders
-        )
-        grad_input, d_vecs, *sinks = call_backward(
-            lone, span_lengths, places[None], tok_rows, vec_rows, top, saved, plan, third, seq_here
-        )
-        grad_input = grad_input.reshape(seq_here, length, width)
-        summed = [
-            reduce_relative(sinks[2 * k], sinks[2 * k + 1], back_orders[k]) for k in range(3)
-        ]
-    else:
+                reduce_bits(blocks[:, :, c], order, names)
+                for c, order in zip(columns, back_orders)
+            ],
+            axis=1,
+        ).astype(jnp.float32)
         select = (mlm_positions[:, :, None] == jnp.arange(length)[None, None, :]).astype(
             jnp.float32
         )
@@ -834,23 +1079,25 @@
             d_picked.reshape(seq_here, slots, width),
             precision=lax.Precision.HIGHEST,
         )
+        d_cls = span_terms(heads_all[:, picks_here:, :].reshape(-1, width))
         d_output_seq = d_output_seq.at[:, 0, :].add(d_cls)
         valid = jnp.arange(length)[None, :] < span_lengths[:, None]
         d_output = d_output_seq.reshape(rows_here, width) * valid.reshape(rows_here, 1)
         grad_input, d_mats, d_vecs = plain_backward(d_output)
         d_mats = d_mats.reshape(devices, 3, third, width)
         summed = [
-            reduce_bits(d_mats[:, k], orders[k][::-1], names).astype(jnp.float32)
-            for k in range(3)
+            reduce_bits(d_mats[:, k], back_orders[k], names).astype(jnp.float32) for k in range(3)
         ]
+        picked_turned = jnp.dot(picked, turn.T, preferred_element_type=jnp.float32).astype(low)
+        d_rolled = contract_rows(d_logits, picked_turned)
+        grad_embed = jnp.where(same_row, d_rolled[:-1], d_rolled[1:])
+    grad_embed = grad_embed.reshape(-1)[:embed_here]
     grad_mats = jnp.concatenate(summed).reshape(-1)
-    grad_vecs = reduce_bits(d_vecs.reshape(devices, vec_here), orders[0][::-1], names)
-
-    picked_turned = jnp.dot(picked, turn.T, preferred_element_type=jnp.float32).astype(low)
-    d_rolled = contract_rows(d_logits, picked_turned)
-    grad_embed = jnp.where(same_row, d_rolled[:-1], d_rolled[1:]).reshape(-1)[:embed_here]
-
-    step_float = float(ADAM_STEP)
+    vec_terms = jnp.pad(d_vecs.reshape(devices, vec_here), ((0, 0), (0, -vec_here % 128)))
+    vec_terms = lax.all_to_all(
+        vec_terms.reshape(devices, -1, 128), names, 0, 0, tiled=True
+    ).reshape(devices, -1)
+    grad_vecs = jnp.sum(vec_terms, axis=0)[:vec_here]
     step_mats = adam_step(layer_mats, grad_mats, mom1_mats, mom2_mats, step_float, decay_rate)
     step_vecs = adam_step(vectors, grad_vecs, mom1_vecs, mom2_vecs, step_float, 0.0)
     step_embed = adam_step(embedding, grad_embed, mom1_embed, mom2_embed, step_float, decay_rate)

time: 438 us -> 352 us (0.80)
  waiting for transfers between devices: 190 us -> 98.6 us
  Pallas kernels: 43.7 us -> 77.2 us
  matrix products: 21.3 us -> 0.56 us
  local copies, waits for them, and re-layouts: 48.2 us -> 36.3 us
  starting transfers between devices: 75.7 us -> 85.2 us
    ppermute x73 -> x66, waiting for transfers between devices: 174 us -> 84.2 us  [flip(): return lax.ppermute(value, name, [(0, 1), (1, 0)])]
    pallas_call x0 -> x4, Pallas kernels: none -> 33 us  [the longest x1 13 us: call_picked(): pl.pallas_call(functools.partial(picked_kernel, plan, embed_here, picks),...]
    concatenate x3 -> x0, local copies, waits for them, and re-layouts: 15.2 us -> none  [the longest x2 14.5 us: on_device(): jnp.concatenate([from_left, embed_low, from_right, jnp.zeros((shifted_row...]
    unnamed x84 -> x59, local copies, waits for them, and re-layouts: 7.3 us -> 17.3 us
    ppermute x2 -> x0, waiting for transfers between devices: 9.41 us -> none  [the longest x1 6.09 us: on_device(): lax.ppermute(embed_low[-width:], names, [(k, (k + 1) % devices) for k in...]
    dot_general x2 -> x1, matrix products: 9.04 us -> 0.13 us  [contract_rows(): lax.dot_general(left, right, (((0,), (0,)), ((), ())), preferred_element_...]
    dot_general x3 -> x1, matrix products: 8.82 us -> 0.25 us  [span_terms(): jnp.dot(d_sims_rows, cls_all, preferred_element_type=jnp.float32)]
    all_to_all x1 -> x3, starting transfers between devices: 3.33 us -> 11.8 us  [the longest x1 4.83 us: on_device(): stats = lax.all_to_all(stats, names, 0, 0, tiled=True)]
  transfers between devices with their start and end apart: 76 -> 69, of which waited for: 42 -> 37; matrix products, arithmetic and copies ran while one was open for 20% -> 20% of each run, Pallas kernels for 0% -> 2%
where the time goes in v3:
time: 352 us; the launch traced here: 348 us
  waiting for transfers between devices  98.6 us (28%)
  starting transfers between devices  85.2 us (24%)
  Pallas kernels  77.2 us (22%)
  other arithmetic  48.6 us (14%)
  local copies, waits for them, and re-layouts  36.3 us (10%)
    ppermute x66, waiting for transfers between devices, flip(): return lax.ppermute(value, name, [(0, 1), (1, 0)])  84.2 us
    ppermute x66, starting transfers between devices, flip(): return lax.ppermute(value, name, [(0, 1), (1, 0)])  73.4 us
    pallas_call x1, Pallas kernels, call_backward(): pl.pallas_call(functools.partial(backward_kernel, plan, unit, seq_here),...  25.5 us
    convert_element_type x24, other arithmetic, reduce_relative(): sends[k] = add_terms([term[half:] for term in terms]).astype(terms[0].dtype)  18.8 us
    pallas_call x1, Pallas kernels, call_forward(): pl.pallas_call(functools.partial(forward_kernel, plan, seq_here), out_sha...  18.7 us
    unnamed x59, local copies, waits for them, and re-layouts  17.3 us
    all_to_all x1, waiting for transfers between devices, on_device(): stats = lax.all_to_all(stats, names, 0, 0, tiled=True)  14 us
    pallas_call x1, Pallas kernels, call_picked(): pl.pallas_call(functools.partial(picked_kernel, plan, embed_here, picks),...  13 us
  transfers between devices with their start and end apart: 69, of which 37 were waited for; matrix products, arithmetic and copies ran while one was open for 20% of the time, Pallas kernels for 2%

profile of v3, /device:TPU:0, one launch (start us, length us, event | category | flops | bytes accessed | tf_op | source)
XLA Modules:
  0.0 348.0 jit_solution(15730161284293797544)
XLA Ops:
  2.9 4.1 %collective-permute-start = (bf16[1,96,768]{2,1,0:T(8,128)(2,1)S(1)}, bf16[1,96,768]{2,1,0:T(8,128)(2,1)}, u32[]{:S(2)}, u32[]{:S(2)}) collective-permute-start(bf16[1,96,768]{2,1,0:T(8,128)(2,1)S(1)} %unstack.16), channel_id=1, source_target_pairs={{0,16},{16,0},{1,17},{17,1},{2,18},{18,2},{3,19},{19,3},{4,20},{20... | collective-permute-start | bytes 442376 | tf_op jit(solution)/shard_map/ppermute | solution.py:89
  8.3 3.0 collective-permute-start.6
  13.8 3.9 %all-to-all-start = ((bf16[32,8,768]{2,1,0:T(8,128)(2,1)}), bf16[32,8,768]{2,1,0:T(8,128)(2,1)}, u32[]{:S(2)}, u32[]{:S(2)}) async-start(bf16[32,8,768]{2,1,0:T(8,128)(2,1)} %broadcast_in_dim.59), calls=%async_computation | async-start | bytes 786432 | tf_op jit(solution)/shard_map/all_to_all | solution.py:930
  20.9 3.1 reshape.168.rows_ref
  25.0 1.8 collective-permute-start.1
  26.8 1.5 collective-permute-done.3
  29.2 2.3 collective-permute-start.4
  32.9 1.6 constant_dynamic-update-slice_fusion.2
  34.4 1.6 constant_dynamic-update-slice_fusion.6
  36.0 1.6 constant_dynamic-update-slice_fusion.10
  38.6 1.9 collective-permute-start.2
  40.5 1.8 pad_maximum_fusion.2
  42.3 2.0 collective-permute-start.5
  44.3 1.8 pad_maximum_fusion.3
  55.4 3.2 collective-permute-done.8
  58.6 2.0 constant_dynamic-update-slice_fusion.8.refs_13_
  61.4 1.9 constant_dynamic-update-slice_fusion.4.refs_9_
  65.4 1.6 collective-permute-start.9
  66.9 1.6 shard_map.189
  70.2 14.7 %collective-permute-done.15.refs_14_ = bf16[8,96,768]{2,1,0:T(8,128)(2,1)} collective-permute-done((bf16[8,96,768]{2,1,0:T(8,128)(2,1)}, bf16[8,96,768]{2,1,0:T(8,128)(2,1)}, u32[]{:S(2)}, u32[]{:S(2)}) %collective-permute-start.15) | collective-permute-done | bytes 1179680 | tf_op jit(solution)/shard_map/ppermute | solution.py:89
  84.9 3.0 collective-permute-done.12.refs_10_
  87.9 2.6 collective-permute-done.9.refs_6_
  91.9 1.7 collective-permute-done.14.refs_12_
  93.7 1.7 collective-permute-done.11.refs_8_
  95.3 18.7 %shard_map.190 = (bf16[80,768]{1,0:T(8,128)(2,1)}, bf16[9216,768]{1,0:T(8,128)(2,1)}, bf16[256,2304]{1,0:T(8,128)(2,1)}, bf16[256,768]{1,0:T(8,128)(2,1)}, f32[2...) custom-call(s32[1]{0:T(128)} %bitcast.refs_0_, s32[2]{0:T(128)} %refs_1_.3, ...), custom_call_target="tpu_custom_call" | custom-call | flops 3623878656 | bytes 50331648 | tf_op jit(solution)/shard_map/pallas_call | solution.py:478
  114.9 4.1 %collective-permute-start.30 = (bf16[1,80,256]{2,1,0:T(8,128)(2,1)S(1)}, bf16[1,80,256]{2,1,0:T(8,128)(2,1)S(1)}, u32[]{:S(2)}, u32[]{:S(2)}) collective-permute-start(bf16[1,80,256]{2,1,0:T(8,128)(2,1)S(1)} %get-tuple-element.112), channel_id=1, source_target_pairs={{0,16},{16,0},{1,17},{17,1},{2,18},{18,2},{3,19},{19,3},{4,20},{20... | collective-permute-start | bytes 122888 | tf_op jit(solution)/shard_map/ppermute | solution.py:89
  119.1 2.8 collective-permute-start.18
  122.0 1.7 collective-permute-start.31
  123.7 2.5 collective-permute-done.18
  127.4 1.6 collective-permute-start.25
  129.0 1.8 collective-permute-done.19
  130.7 1.6 collective-permute-start.20
  133.7 2.5 collective-permute-done.20
  139.0 1.6 collective-permute-start.33
  141.1 5.3 %collective-permute-done.21.refs_4_ = bf16[8,80,256]{2,1,0:T(8,128)(2,1)S(1)} collective-permute-done((bf16[8,80,256]{2,1,0:T(8,128)(2,1)S(1)}, bf16[8,80,256]{2,1,0:T(8,128)(2,1)S(1)}, u32[]{:S(2)}, u32[]{:S(2)}) %collective-permute-start.21) | collective-permute-done | bytes 327712 | tf_op jit(solution)/shard_map/ppermute | solution.py:89
  149.0 12.6 %shard_map.191 = (bf16[2048,768]{1,0:T(8,128)(2,1)}, bf16[32,16,768]{2,1,0:T(8,128)(2,1)S(1)}, f32[960,2048]{1,0:T(8,128)}, f32[32,8,512]{2,1,0:T(8,128)}) custom-call(s32[1]{0:T(128)} %bitcast.refs_0_, s32[1]{0:T(128)} %bitcast.5.shift_ref.refs_1_, bf16[960,768]{1,0:T(8,128)(2,1)} %copy-done.2, bf16[8,80,256]{2,1,0:T(8,128)(2,1)S(1)} %pad_maximum_fusion.4.refs_3_, ...), custom_call_target="tpu_custom_call" | custom-call | flops 3019898880 | bytes 16777216 | tf_op jit(solution)/shard_map/pallas_call | solution.py:628
  161.6 4.8 %all-to-all-start.1 = ((f32[32,8,512]{2,1,0:T(8,128)}), f32[32,8,512]{2,1,0:T(8,128)S(1)}, u32[]{:S(2)}, u32[]{:S(2)}) async-start(f32[32,8,512]{2,1,0:T(8,128)} %get-tuple-element.69), calls=%async_computation.1 | async-start | bytes 1048576 | tf_op jit(solution)/shard_map/all_to_all | solution.py:1007
  167.5 14.0 %all-to-all-done.1.refs_2_ = f32[32,8,512]{2,1,0:T(8,128)S(1)} async-done(((f32[32,8,512]{2,1,0:T(8,128)}), f32[32,8,512]{2,1,0:T(8,128)S(1)}, u32[]{:S(2)}, u32[]{:S(2)}) %all-to-all-start.1) | async-done | bytes 524320 | tf_op jit(solution)/shard_map/all_to_all | solution.py:1007
  181.4 13.0 %shard_map.192 = (bf16[960,2048]{1,0:T(8,128)(2,1)}, bf16[16,64,256]{2,1,0:T(8,128)(2,1)S(1)}, bf16[16,64,256]{2,1,0:T(8,128)(2,1)S(1)}, bf16[16,64,256]{2,1,0:T...) custom-call(s32[1]{0:T(128)} %bitcast.refs_0_, ...), custom_call_target="tpu_custom_call" | custom-call | flops 3019898880 | bytes 16777216 | tf_op jit(solution)/shard_map/pallas_call | solution.py:713
  200.5 5.4 %collective-permute-done.37 = bf16[8,64,256]{2,1,0:T(8,128)(2,1)S(1)} collective-permute-done((bf16[8,64,256]{2,1,0:T(8,128)(2,1)S(1)}, bf16[8,64,256]{2,1,0:T(8,128)(2,1)S(1)}, u32[]{:S(2)}, u32[]{:S(2)}) %collective-permute-start.37) | collective-permute-done | bytes 262176 | tf_op jit(solution)/shard_map/ppermute | solution.py:89
  208.9 2.1 collective-permute-done.38
  216.7 1.7 collective-permute-start.45
  224.1 25.5 %shard_map.193 = (f32[256,768]{1,0:T(8,128)}, f32[12,768]{1,0:T(8,128)}, bf16[16,96,768]{2,1,0:T(8,128)(2,1)}, bf16[16,96,768]{2,1,0:T(8,128)(2,1)}, bf16[16,96,...) custom-call(s32[1]{0:T(128)} %bitcast.refs_0_, ...), custom_call_target="tpu_custom_call" | custom-call | flops 7247757312 | bytes 50331648 | tf_op jit(solution)/shard_map/pallas_call | solution.py:513
  250.3 4.2 %collective-permute-done.51 = bf16[16,96,768]{2,1,0:T(8,128)(2,1)S(1)} collective-permute-done((bf16[16,96,768]{2,1,0:T(8,128)(2,1)}, bf16[16,96,768]{2,1,0:T(8,128)(2,1)S(1)}, u32[]{:S(2)}, u32[]{:S(2)}) %collective-permute-start.51) | collective-permute-done | bytes 2359328 | tf_op jit(solution)/shard_map/ppermute | solution.py:89
  254.5 3.6 %add_convert_fusion.2 = bf16[8,96,768]{2,1,0:T(8,128)(2,1)} fusion(bf16[16,96,768]{2,1,0:T(8,128)(2,1)S(1)} %collective-permute-done.51, bf16[16,96,768]{2,1,0:T(8,128)(2,1)} %get-tuple-element.88), kind=kLoop, calls=%fused_computation.9 | loop fusion | flops 2359296 | bytes 3538944 | tf_op jit(solution)/shard_map/convert_element_type | solution.py:172
  262.2 1.6 add_convert_fusion
  264.6 3.0 all-to-all-start.2
  267.6 1.9 collective-permute-start.62
  269.6 2.1 copy-done
  271.7 1.9 copy-done.1
  273.6 5.7 %shard_map.194 = f32[954,768]{1,0:T(8,128)S(1)} custom-call(s32[1]{0:T(128)} %bitcast.5.shift_ref.refs_1_, bf16[960,2048]{1,0:T(8,128)(2,1)S(1)} %copy-done, bf16[2048,768]{1,0:T(8,128)(2,1)S(1)} %copy-done.1), custom_call_target="tpu_custom_call" | custom-call | flops 24159191040 | bytes 67108864 | tf_op jit(solution)/shard_map/pallas_call | solution.py:741
  279.3 1.8 reshape.177
  281.1 8.9 %fusion.5 = (f32[732528]{0:T(1024)}, f32[732528]{0:T(1024)}) fusion(f32[732528]{0:T(1024)} %param.21, f32[732528]{0:T(1024)} %param.27, f32[732528]{0:T(1024)} %param.26, f32[732672]{0:T(1024)} %reshape.177), kind=kLoop, calls=%fused_computation.6 | loop fusion | flops 9522864 | bytes 17580672 | tf_op jit(solution)/shard_map/add | solution.py:85
  290.4 1.8 add_convert_fusion.5
  295.6 1.8 collective-permute-done.62
  298.9 2.0 collective-permute-start.63
  301.4 8.0 %collective-permute-done.53 = bf16[4,96,768]{2,1,0:T(8,128)(2,1)S(1)} collective-permute-done((bf16[4,96,768]{2,1,0:T(8,128)(2,1)S(1)}, bf16[4,96,768]{2,1,0:T(8,128)(2,1)S(1)}, u32[]{:S(2)}, u32[]{:S(2)}) %collective-permute-start.53) | collective-permute-done | bytes 589856 | tf_op jit(solution)/shard_map/ppermute | solution.py:89
  310.7 1.7 collective-permute-start.54
  317.8 1.8 collective-permute-done.54
  320.7 2.4 collective-permute-start.55
  327.0 2.1 collective-permute-start.65
  329.0 8.1 %collective-permute-done.55 = bf16[1,96,768]{2,1,0:T(8,128)(2,1)S(1)} collective-permute-done((bf16[1,96,768]{2,1,0:T(8,128)(2,1)S(1)}, bf16[1,96,768]{2,1,0:T(8,128)(2,1)S(1)}, u32[]{:S(2)}, u32[]{:S(2)}) %collective-permute-start.55) | collective-permute-done | bytes 147488 | tf_op jit(solution)/shard_map/ppermute | solution.py:89
  338.3 2.0 collective-permute-done.60
  344.7 3.0 fusion.13
  (257 shorter events, 87.8 us)
Async XLA Ops:
  2.9 21.2 %collective-permute-start = (bf16[1,96,768]{2,1,0:T(8,128)(2,1)S(1)}, bf16[1,96,768]{2,1,0:T(8,128)(2,1)}, u32[]{:S(2)}, u32[]{:S(2)}) collective-permute-start(bf16[1,96,768]{2,1,0:T(8,128)(2,1)S(1)} %unstack.16), channel_id=1, source_target_pairs={{0,16},{16,0},{1,17},{17,1},{2,18},{18,2},{3,19},{19,3},{4,20},{20... | collective-permute-start | bytes 442376 | tf_op jit(solution)/shard_map/ppermute | solution.py:89
  7.1 21.1 %collective-permute-start.3 = (bf16[1,96,768]{2,1,0:T(8,128)(2,1)S(1)}, bf16[1,96,768]{2,1,0:T(8,128)(2,1)}, u32[]{:S(2)}, u32[]{:S(2)}) collective-permute-start(bf16[1,96,768]{2,1,0:T(8,128)(2,1)S(1)} %unstack.18), channel_id=1, source_target_pairs={{0,16},{16,0},{1,17},{17,1},{2,18},{18,2},{3,19},{19,3},{4,20},{20... | collective-permute-start | bytes 442376 | tf_op jit(solution)/shard_map/ppermute | solution.py:89
  8.3 23.5 %collective-permute-start.6 = (bf16[1,96,768]{2,1,0:T(8,128)(2,1)S(1)}, bf16[1,96,768]{2,1,0:T(8,128)(2,1)}, u32[]{:S(2)}, u32[]{:S(2)}) collective-permute-start(bf16[1,96,768]{2,1,0:T(8,128)(2,1)S(1)} %unstack.20), channel_id=1, source_target_pairs={{0,16},{16,0},{1,17},{17,1},{2,18},{18,2},{3,19},{19,3},{4,20},{20... | collective-permute-start | bytes 442376 | tf_op jit(solution)/shard_map/ppermute | solution.py:89
  13.8 36.0 %all-to-all-start = ((bf16[32,8,768]{2,1,0:T(8,128)(2,1)}), bf16[32,8,768]{2,1,0:T(8,128)(2,1)}, u32[]{:S(2)}, u32[]{:S(2)}) async-start(bf16[32,8,768]{2,1,0:T(8,128)(2,1)} %broadcast_in_dim.59), calls=%async_computation | async-start | bytes 786432 | tf_op jit(solution)/shard_map/all_to_all | solution.py:930
  25.0 12.6 %collective-permute-start.1 = (bf16[2,96,768]{2,1,0:T(8,128)(2,1)S(1)}, bf16[2,96,768]{2,1,0:T(8,128)(2,1)S(1)}, u32[]{:S(2)}, u32[]{:S(2)}) collective-permute-start(bf16[2,96,768]{2,1,0:T(8,128)(2,1)S(1)} %pad_maximum_fusion.7), channel_id=1, source_target_pairs={{0,1},{1,0},{2,3},{3,2},{4,5},{5,4},{6,7},{7,6},{8,9},{9,8},{10,11... | collective-permute-start | bytes 884744 | tf_op jit(solution)/shard_map/ppermute | solution.py:89
  29.2 11.3 %collective-permute-start.4 = (bf16[2,96,768]{2,1,0:T(8,128)(2,1)S(1)}, bf16[2,96,768]{2,1,0:T(8,128)(2,1)S(1)}, u32[]{:S(2)}, u32[]{:S(2)}) collective-permute-start(bf16[2,96,768]{2,1,0:T(8,128)(2,1)S(1)} %pad_maximum_fusion.8), channel_id=1, source_target_pairs={{0,4},{4,0},{1,5},{5,1},{2,6},{6,2},{3,7},{7,3},{8,12},{12,8},{9,1... | collective-permute-start | bytes 884744 | tf_op jit(solution)/shard_map/ppermute | solution.py:89
  32.8 11.5 %collective-permute-start.7 = (bf16[2,96,768]{2,1,0:T(8,128)(2,1)S(1)}, bf16[2,96,768]{2,1,0:T(8,128)(2,1)S(1)}, u32[]{:S(2)}, u32[]{:S(2)}) collective-permute-start(bf16[2,96,768]{2,1,0:T(8,128)(2,1)S(1)} %pad_maximum_fusion.9), channel_id=1, source_target_pairs={{0,8},{8,0},{1,9},{9,1},{2,10},{10,2},{3,11},{11,3},{4,12},{12,4},... | collective-permute-start | bytes 884744 | tf_op jit(solution)/shard_map/ppermute | solution.py:89
  38.6 26.0 %collective-permute-start.2 = (bf16[4,96,768]{2,1,0:T(8,128)(2,1)S(1)}, bf16[4,96,768]{2,1,0:T(8,128)(2,1)S(1)}, u32[]{:S(2)}, u32[]{:S(2)}) collective-permute-start(bf16[4,96,768]{2,1,0:T(8,128)(2,1)S(1)} %pad_maximum_fusion.1), channel_id=1, source_target_pairs={{0,4},{4,0},{1,5},{5,1},{2,6},{6,2},{3,7},{7,3},{8,12},{12,8},{9,1... | collective-permute-start | bytes 1769480 | tf_op jit(solution)/shard_map/ppermute | solution.py:89
  42.3 19.1 %collective-permute-start.5 = (bf16[4,96,768]{2,1,0:T(8,128)(2,1)}, bf16[4,96,768]{2,1,0:T(8,128)(2,1)}, u32[]{:S(2)}, u32[]{:S(2)}) collective-permute-start(bf16[4,96,768]{2,1,0:T(8,128)(2,1)} %pad_maximum_fusion.2), channel_id=1, source_target_pairs={{0,8},{8,0},{1,9},{9,1},{2,10},{10,2},{3,11},{11,3},{4,12},{12,4},... | collective-permute-start | bytes 1769480 | tf_op jit(solution)/shard_map/ppermute | solution.py:89
  46.1 12.6 %collective-permute-start.8 = (bf16[4,96,768]{2,1,0:T(8,128)(2,1)}, bf16[4,96,768]{2,1,0:T(8,128)(2,1)}, u32[]{:S(2)}, u32[]{:S(2)}) collective-permute-start(bf16[4,96,768]{2,1,0:T(8,128)(2,1)} %pad_maximum_fusion.3), channel_id=1, source_target_pairs={{0,1},{1,0},{2,3},{3,2},{4,5},{5,4},{6,7},{7,6},{8,9},{9,8},{10,11... | collective-permute-start | bytes 1769480 | tf_op jit(solution)/shard_map/ppermute | solution.py:89
  60.6 24.3 %collective-permute-start.15 = (bf16[8,96,768]{2,1,0:T(8,128)(2,1)}, bf16[8,96,768]{2,1,0:T(8,128)(2,1)}, u32[]{:S(2)}, u32[]{:S(2)}) collective-permute-start(bf16[8,96,768]{2,1,0:T(8,128)(2,1)} %constant_dynamic-update-slice_fusion.8.refs_13_), channel_id=1, source_target_pairs={{0,4},{4,0},{1,5},{5,1},{2,6},{6,2},{3,7},{7,3},{8,12},{12,8},{9,1... | collective-permute-start | bytes 3538952 | tf_op jit(solution)/shard_map/ppermute | solution.py:89
  63.3 24.6 %collective-permute-start.12 = (bf16[8,96,768]{2,1,0:T(8,128)(2,1)}, bf16[8,96,768]{2,1,0:T(8,128)(2,1)}, u32[]{:S(2)}, u32[]{:S(2)}) collective-permute-start(bf16[8,96,768]{2,1,0:T(8,128)(2,1)} %constant_dynamic-update-slice_fusion.4.refs_9_), channel_id=1, source_target_pairs={{0,1},{1,0},{2,3},{3,2},{4,5},{5,4},{6,7},{7,6},{8,9},{9,8},{10,11... | collective-permute-start | bytes 3538952 | tf_op jit(solution)/shard_map/ppermute | solution.py:89
  65.4 25.1 %collective-permute-start.9 = (bf16[8,96,768]{2,1,0:T(8,128)(2,1)}, bf16[8,96,768]{2,1,0:T(8,128)(2,1)}, u32[]{:S(2)}, u32[]{:S(2)}) collective-permute-start(bf16[8,96,768]{2,1,0:T(8,128)(2,1)} %constant_dynamic-update-slice_fusion.refs_5_), channel_id=1, source_target_pairs={{0,8},{8,0},{1,9},{9,1},{2,10},{10,2},{3,11},{11,3},{4,12},{12,4},... | collective-permute-start | bytes 3538952 | tf_op jit(solution)/shard_map/ppermute | solution.py:89
  69.7 20.8 %collective-permute-start.10 = (bf16[8,96,768]{2,1,0:T(8,128)(2,1)}, bf16[8,96,768]{2,1,0:T(8,128)(2,1)S(1)}, u32[]{:S(2)}, u32[]{:S(2)}) collective-permute-start(bf16[8,96,768]{2,1,0:T(8,128)(2,1)} %constant_dynamic-update-slice_fusion.refs_5_), channel_id=1, source_target_pairs={{0,2},{2,0},{1,3},{3,1},{4,6},{6,4},{5,7},{7,5},{8,10},{10,8},{9,1... | collective-permute-start | bytes 3538952 | tf_op jit(solution)/shard_map/ppermute | solution.py:89
  69.7 22.2 %collective-permute-start.13 = (bf16[8,96,768]{2,1,0:T(8,128)(2,1)}, bf16[8,96,768]{2,1,0:T(8,128)(2,1)}, u32[]{:S(2)}, u32[]{:S(2)}) collective-permute-start(bf16[8,96,768]{2,1,0:T(8,128)(2,1)} %constant_dynamic-update-slice_fusion.4.refs_9_), channel_id=1, source_target_pairs={{0,2},{2,0},{1,3},{3,1},{4,6},{6,4},{5,7},{7,5},{8,10},{10,8},{9,1... | collective-permute-start | bytes 3538952 | tf_op jit(solution)/shard_map/ppermute | solution.py:89
  84.9 7.1 %collective-permute-start.16 = (bf16[8,96,768]{2,1,0:T(8,128)(2,1)}, bf16[8,96,768]{2,1,0:T(8,128)(2,1)}, u32[]{:S(2)}, u32[]{:S(2)}) collective-permute-start(bf16[8,96,768]{2,1,0:T(8,128)(2,1)} %constant_dynamic-update-slice_fusion.8.refs_13_), channel_id=1, source_target_pairs={{0,2},{2,0},{1,3},{3,1},{4,6},{6,4},{5,7},{7,5},{8,10},{10,8},{9,1... | collective-permute-start | bytes 3538952 | tf_op jit(solution)/shard_map/ppermute | solution.py:89
  87.9 4.1 %collective-permute-start.17 = (bf16[8,96,768]{2,1,0:T(8,128)(2,1)}, bf16[8,96,768]{2,1,0:T(8,128)(2,1)}, u32[]{:S(2)}, u32[]{:S(2)}) collective-permute-start(bf16[8,96,768]{2,1,0:T(8,128)(2,1)} %collective-permute-done.15.refs_14_), channel_id=1, source_target_pairs={{0,2},{2,0},{1,3},{3,1},{4,6},{6,4},{5,7},{7,5},{8,10},{10,8},{9,1... | collective-permute-start | bytes 3538952 | tf_op jit(solution)/shard_map/ppermute | solution.py:89
  90.5 3.2 collective-permute-start.14
  90.5 4.9 %collective-permute-start.11 = (bf16[8,96,768]{2,1,0:T(8,128)(2,1)}, bf16[8,96,768]{2,1,0:T(8,128)(2,1)}, u32[]{:S(2)}, u32[]{:S(2)}) collective-permute-start(bf16[8,96,768]{2,1,0:T(8,128)(2,1)} %collective-permute-done.9.refs_6_), channel_id=1, source_target_pairs={{0,2},{2,0},{1,3},{3,1},{4,6},{6,4},{5,7},{7,5},{8,10},{10,8},{9,1... | collective-permute-start | bytes 3538952 | tf_op jit(solution)/shard_map/ppermute | solution.py:89
  114.9 7.1 %collective-permute-start.30 = (bf16[1,80,256]{2,1,0:T(8,128)(2,1)S(1)}, bf16[1,80,256]{2,1,0:T(8,128)(2,1)S(1)}, u32[]{:S(2)}, u32[]{:S(2)}) collective-permute-start(bf16[1,80,256]{2,1,0:T(8,128)(2,1)S(1)} %get-tuple-element.112), channel_id=1, source_target_pairs={{0,16},{16,0},{1,17},{17,1},{2,18},{18,2},{3,19},{19,3},{4,20},{20... | collective-permute-start | bytes 122888 | tf_op jit(solution)/shard_map/ppermute | solution.py:89
  119.0 8.3 %collective-permute-start.24 = (bf16[1,80,256]{2,1,0:T(8,128)(2,1)S(1)}, bf16[1,80,256]{2,1,0:T(8,128)(2,1)S(1)}, u32[]{:S(2)}, u32[]{:S(2)}) collective-permute-start(bf16[1,80,256]{2,1,0:T(8,128)(2,1)S(1)} %get-tuple-element.113), channel_id=1, source_target_pairs={{0,16},{16,0},{1,17},{17,1},{2,18},{18,2},{3,19},{19,3},{4,20},{20... | collective-permute-start | bytes 122888 | tf_op jit(solution)/shard_map/ppermute | solution.py:89
  119.1 7.1 %collective-permute-start.18 = (bf16[1,80,256]{2,1,0:T(8,128)(2,1)S(1)}, bf16[1,80,256]{2,1,0:T(8,128)(2,1)S(1)}, u32[]{:S(2)}, u32[]{:S(2)}) collective-permute-start(bf16[1,80,256]{2,1,0:T(8,128)(2,1)S(1)} %get-tuple-element.114), channel_id=1, source_target_pairs={{0,16},{16,0},{1,17},{17,1},{2,18},{18,2},{3,19},{19,3},{4,20},{20... | collective-permute-start | bytes 122888 | tf_op jit(solution)/shard_map/ppermute | solution.py:89
  122.0 10.5 %collective-permute-start.31 = (bf16[2,80,256]{2,1,0:T(8,128)(2,1)S(1)}, bf16[2,80,256]{2,1,0:T(8,128)(2,1)S(1)}, u32[]{:S(2)}, u32[]{:S(2)}) collective-permute-start(bf16[2,80,256]{2,1,0:T(8,128)(2,1)S(1)} %pad_maximum_fusion.15), channel_id=1, source_target_pairs={{0,8},{8,0},{1,9},{9,1},{2,10},{10,2},{3,11},{11,3},{4,12},{12,4},... | collective-permute-start | bytes 245768 | tf_op jit(solution)/shard_map/ppermute | solution.py:89
  126.2 4.5 %collective-permute-start.19 = (bf16[2,80,256]{2,1,0:T(8,128)(2,1)S(1)}, bf16[2,80,256]{2,1,0:T(8,128)(2,1)S(1)}, u32[]{:S(2)}, u32[]{:S(2)}) collective-permute-start(bf16[2,80,256]{2,1,0:T(8,128)(2,1)S(1)} %pad_maximum_fusion.13), channel_id=1, source_target_pairs={{0,1},{1,0},{2,3},{3,2},{4,5},{5,4},{6,7},{7,6},{8,9},{9,8},{10,11... | collective-permute-start | bytes 245768 | tf_op jit(solution)/shard_map/ppermute | solution.py:89
  127.4 4.9 %collective-permute-start.25 = (bf16[2,80,256]{2,1,0:T(8,128)(2,1)S(1)}, bf16[2,80,256]{2,1,0:T(8,128)(2,1)S(1)}, u32[]{:S(2)}, u32[]{:S(2)}) collective-permute-start(bf16[2,80,256]{2,1,0:T(8,128)(2,1)S(1)} %pad_maximum_fusion.14), channel_id=1, source_target_pairs={{0,4},{4,0},{1,5},{5,1},{2,6},{6,2},{3,7},{7,3},{8,12},{12,8},{9,1... | collective-permute-start | bytes 245768 | tf_op jit(solution)/shard_map/ppermute | solution.py:89
  130.7 5.4 %collective-permute-start.20 = (bf16[4,80,256]{2,1,0:T(8,128)(2,1)S(1)}, bf16[4,80,256]{2,1,0:T(8,128)(2,1)S(1)}, u32[]{:S(2)}, u32[]{:S(2)}) collective-permute-start(bf16[4,80,256]{2,1,0:T(8,128)(2,1)S(1)} %pad_maximum_fusion.10), channel_id=1, source_target_pairs={{0,4},{4,0},{1,5},{5,1},{2,6},{6,2},{3,7},{7,3},{8,12},{12,8},{9,1... | collective-permute-start | bytes 491528 | tf_op jit(solution)/shard_map/ppermute | solution.py:89
  132.3 5.4 %collective-permute-start.26 = (bf16[4,80,256]{2,1,0:T(8,128)(2,1)S(1)}, bf16[4,80,256]{2,1,0:T(8,128)(2,1)S(1)}, u32[]{:S(2)}, u32[]{:S(2)}) collective-permute-start(bf16[4,80,256]{2,1,0:T(8,128)(2,1)S(1)} %pad_maximum_fusion.11), channel_id=1, source_target_pairs={{0,8},{8,0},{1,9},{9,1},{2,10},{10,2},{3,11},{11,3},{4,12},{12,4},... | collective-permute-start | bytes 491528 | tf_op jit(solution)/shard_map/ppermute | solution.py:89
  132.5 6.4 %collective-permute-start.32 = (bf16[4,80,256]{2,1,0:T(8,128)(2,1)S(1)}, bf16[4,80,256]{2,1,0:T(8,128)(2,1)S(1)}, u32[]{:S(2)}, u32[]{:S(2)}) collective-permute-start(bf16[4,80,256]{2,1,0:T(8,128)(2,1)S(1)} %pad_maximum_fusion.12), channel_id=1, source_target_pairs={{0,1},{1,0},{2,3},{3,2},{4,5},{5,4},{6,7},{7,6},{8,9},{9,8},{10,11... | collective-permute-start | bytes 491528 | tf_op jit(solution)/shard_map/ppermute | solution.py:89
  136.2 4.4 %collective-permute-start.22 = (bf16[8,80,256]{2,1,0:T(8,128)(2,1)S(1)}, bf16[8,80,256]{2,1,0:T(8,128)(2,1)S(1)}, u32[]{:S(2)}, u32[]{:S(2)}) collective-permute-start(bf16[8,80,256]{2,1,0:T(8,128)(2,1)S(1)} %pad_maximum_fusion.4.refs_3_), channel_id=1, source_target_pairs={{0,2},{2,0},{1,3},{3,1},{4,6},{6,4},{5,7},{7,5},{8,10},{10,8},{9,1... | collective-permute-start | bytes 983048 | tf_op jit(solution)/shard_map/ppermute | solution.py:89
  136.2 10.1 %collective-permute-start.21 = (bf16[8,80,256]{2,1,0:T(8,128)(2,1)S(1)}, bf16[8,80,256]{2,1,0:T(8,128)(2,1)S(1)}, u32[]{:S(2)}, u32[]{:S(2)}) collective-permute-start(bf16[8,80,256]{2,1,0:T(8,128)(2,1)S(1)} %pad_maximum_fusion.4.refs_3_), channel_id=1, source_target_pairs={{0,8},{8,0},{1,9},{9,1},{2,10},{10,2},{3,11},{11,3},{4,12},{12,4},... | collective-permute-start | bytes 983048 | tf_op jit(solution)/shard_map/ppermute | solution.py:89
  137.7 8.7 %collective-permute-start.27 = (bf16[8,80,256]{2,1,0:T(8,128)(2,1)S(1)}, bf16[8,80,256]{2,1,0:T(8,128)(2,1)S(1)}, u32[]{:S(2)}, u32[]{:S(2)}) collective-permute-start(bf16[8,80,256]{2,1,0:T(8,128)(2,1)S(1)} %pad_maximum_fusion.5.refs_7_), channel_id=1, source_target_pairs={{0,1},{1,0},{2,3},{3,2},{4,5},{5,4},{6,7},{7,6},{8,9},{9,8},{10,11... | collective-permute-start | bytes 983048 | tf_op jit(solution)/shard_map/ppermute | solution.py:89
  139.0 8.4 %collective-permute-start.33 = (bf16[8,80,256]{2,1,0:T(8,128)(2,1)S(1)}, bf16[8,80,256]{2,1,0:T(8,128)(2,1)S(1)}, u32[]{:S(2)}, u32[]{:S(2)}) collective-permute-start(bf16[8,80,256]{2,1,0:T(8,128)(2,1)S(1)} %pad_maximum_fusion.6.refs_11_), channel_id=1, source_target_pairs={{0,4},{4,0},{1,5},{5,1},{2,6},{6,2},{3,7},{7,3},{8,12},{12,8},{9,1... | collective-permute-start | bytes 983048 | tf_op jit(solution)/shard_map/ppermute | solution.py:89
  140.5 6.9 %collective-permute-start.28 = (bf16[8,80,256]{2,1,0:T(8,128)(2,1)S(1)}, bf16[8,80,256]{2,1,0:T(8,128)(2,1)S(1)}, u32[]{:S(2)}, u32[]{:S(2)}) collective-permute-start(bf16[8,80,256]{2,1,0:T(8,128)(2,1)S(1)} %pad_maximum_fusion.5.refs_7_), channel_id=1, source_target_pairs={{0,2},{2,0},{1,3},{3,1},{4,6},{6,4},{5,7},{7,5},{8,10},{10,8},{9,1... | collective-permute-start | bytes 983048 | tf_op jit(solution)/shard_map/ppermute | solution.py:89
  140.5 6.9 %collective-permute-start.34 = (bf16[8,80,256]{2,1,0:T(8,128)(2,1)S(1)}, bf16[8,80,256]{2,1,0:T(8,128)(2,1)S(1)}, u32[]{:S(2)}, u32[]{:S(2)}) collective-permute-start(bf16[8,80,256]{2,1,0:T(8,128)(2,1)S(1)} %pad_maximum_fusion.6.refs_11_), channel_id=1, source_target_pairs={{0,2},{2,0},{1,3},{3,1},{4,6},{6,4},{5,7},{7,5},{8,10},{10,8},{9,1... | collective-permute-start | bytes 983048 | tf_op jit(solution)/shard_map/ppermute | solution.py:89
  161.6 19.8 %all-to-all-start.1 = ((f32[32,8,512]{2,1,0:T(8,128)}), f32[32,8,512]{2,1,0:T(8,128)S(1)}, u32[]{:S(2)}, u32[]{:S(2)}) async-start(f32[32,8,512]{2,1,0:T(8,128)} %get-tuple-element.69), calls=%async_computation.1 | async-start | bytes 1048576 | tf_op jit(solution)/shard_map/all_to_all | solution.py:1007
  195.9 3.6 %collective-permute-start.46 = (bf16[16,64,256]{2,1,0:T(8,128)(2,1)S(1)}, bf16[16,64,256]{2,1,0:T(8,128)(2,1)S(1)}, u32[]{:S(2)}, u32[]{:S(2)}) collective-permute-start(bf16[16,64,256]{2,1,0:T(8,128)(2,1)S(1)} %get-tuple-element.78), channel_id=1, source_target_pairs={{0,2},{2,0},{1,3},{3,1},{4,6},{6,4},{5,7},{7,5},{8,10},{10,8},{9,1... | collective-permute-start | bytes 1572872 | tf_op jit(solution)/shard_map/ppermute | solution.py:89
  197.2 8.7 %collective-permute-start.37 = (bf16[8,64,256]{2,1,0:T(8,128)(2,1)S(1)}, bf16[8,64,256]{2,1,0:T(8,128)(2,1)S(1)}, u32[]{:S(2)}, u32[]{:S(2)}) collective-permute-start(bf16[8,64,256]{2,1,0:T(8,128)(2,1)S(1)} %add_convert_fusion.11), channel_id=1, source_target_pairs={{0,8},{8,0},{1,9},{9,1},{2,10},{10,2},{3,11},{11,3},{4,12},{12,4},... | collective-permute-start | bytes 786440 | tf_op jit(solution)/shard_map/ppermute | solution.py:89
  198.4 8.6 %collective-permute-start.42 = (bf16[8,64,256]{2,1,0:T(8,128)(2,1)S(1)}, bf16[8,64,256]{2,1,0:T(8,128)(2,1)S(1)}, u32[]{:S(2)}, u32[]{:S(2)}) collective-permute-start(bf16[8,64,256]{2,1,0:T(8,128)(2,1)S(1)} %add_convert_fusion.10), channel_id=1, source_target_pairs={{0,1},{1,0},{2,3},{3,2},{4,5},{5,4},{6,7},{7,6},{8,9},{9,8},{10,11... | collective-permute-start | bytes 786440 | tf_op jit(solution)/shard_map/ppermute | solution.py:89
  199.6 8.3 %collective-permute-start.47 = (bf16[8,64,256]{2,1,0:T(8,128)(2,1)S(1)}, bf16[8,64,256]{2,1,0:T(8,128)(2,1)S(1)}, u32[]{:S(2)}, u32[]{:S(2)}) collective-permute-start(bf16[8,64,256]{2,1,0:T(8,128)(2,1)S(1)} %add_convert_fusion.9), channel_id=1, source_target_pairs={{0,4},{4,0},{1,5},{5,1},{2,6},{6,2},{3,7},{7,3},{8,12},{12,8},{9,1... | collective-permute-start | bytes 786440 | tf_op jit(solution)/shard_map/ppermute | solution.py:89
  205.9 5.0 %collective-permute-start.38 = (bf16[4,64,256]{2,1,0:T(8,128)(2,1)S(1)}, bf16[4,64,256]{2,1,0:T(8,128)(2,1)S(1)}, u32[]{:S(2)}, u32[]{:S(2)}) collective-permute-start(bf16[4,64,256]{2,1,0:T(8,128)(2,1)S(1)} %add_convert_fusion.17), channel_id=1, source_target_pairs={{0,4},{4,0},{1,5},{5,1},{2,6},{6,2},{3,7},{7,3},{8,12},{12,8},{9,1... | collective-permute-start | bytes 393224 | tf_op jit(solution)/shard_map/ppermute | solution.py:89
  207.1 5.0 %collective-permute-start.43 = (bf16[4,64,256]{2,1,0:T(8,128)(2,1)S(1)}, bf16[4,64,256]{2,1,0:T(8,128)(2,1)S(1)}, u32[]{:S(2)}, u32[]{:S(2)}) collective-permute-start(bf16[4,64,256]{2,1,0:T(8,128)(2,1)S(1)} %add_convert_fusion.16), channel_id=1, source_target_pairs={{0,8},{8,0},{1,9},{9,1},{2,10},{10,2},{3,11},{11,3},{4,12},{12,4},... | collective-permute-start | bytes 393224 | tf_op jit(solution)/shard_map/ppermute | solution.py:89
  207.9 5.7 %collective-permute-start.48 = (bf16[4,64,256]{2,1,0:T(8,128)(2,1)S(1)}, bf16[4,64,256]{2,1,0:T(8,128)(2,1)S(1)}, u32[]{:S(2)}, u32[]{:S(2)}) collective-permute-start(bf16[4,64,256]{2,1,0:T(8,128)(2,1)S(1)} %add_convert_fusion.15), channel_id=1, source_target_pairs={{0,1},{1,0},{2,3},{3,2},{4,5},{5,4},{6,7},{7,6},{8,9},{9,8},{10,11... | collective-permute-start | bytes 393224 | tf_op jit(solution)/shard_map/ppermute | solution.py:89
  211.0 4.3 %collective-permute-start.39 = (bf16[2,64,256]{2,1,0:T(8,128)(2,1)S(1)}, bf16[2,64,256]{2,1,0:T(8,128)(2,1)S(1)}, u32[]{:S(2)}, u32[]{:S(2)}) collective-permute-start(bf16[2,64,256]{2,1,0:T(8,128)(2,1)S(1)} %add_convert_fusion.20), channel_id=1, source_target_pairs={{0,1},{1,0},{2,3},{3,2},{4,5},{5,4},{6,7},{7,6},{8,9},{9,8},{10,11... | collective-permute-start | bytes 196616 | tf_op jit(solution)/shard_map/ppermute | solution.py:89
  212.1 4.5 %collective-permute-start.44 = (bf16[2,64,256]{2,1,0:T(8,128)(2,1)S(1)}, bf16[2,64,256]{2,1,0:T(8,128)(2,1)S(1)}, u32[]{:S(2)}, u32[]{:S(2)}) collective-permute-start(bf16[2,64,256]{2,1,0:T(8,128)(2,1)S(1)} %add_convert_fusion.19), channel_id=1, source_target_pairs={{0,4},{4,0},{1,5},{5,1},{2,6},{6,2},{3,7},{7,3},{8,12},{12,8},{9,1... | collective-permute-start | bytes 196616 | tf_op jit(solution)/shard_map/ppermute | solution.py:89
  213.7 4.8 %collective-permute-start.49 = (bf16[2,64,256]{2,1,0:T(8,128)(2,1)S(1)}, bf16[2,64,256]{2,1,0:T(8,128)(2,1)S(1)}, u32[]{:S(2)}, u32[]{:S(2)}) collective-permute-start(bf16[2,64,256]{2,1,0:T(8,128)(2,1)S(1)} %add_convert_fusion.18), channel_id=1, source_target_pairs={{0,8},{8,0},{1,9},{9,1},{2,10},{10,2},{3,11},{11,3},{4,12},{12,4},... | collective-permute-start | bytes 196616 | tf_op jit(solution)/shard_map/ppermute | solution.py:89
  215.4 5.7 %collective-permute-start.40 = (bf16[1,64,256]{2,1,0:T(8,128)(2,1)S(1)}, bf16[1,64,256]{2,1,0:T(8,128)(2,1)S(1)}, u32[]{:S(2)}, u32[]{:S(2)}) collective-permute-start(bf16[1,64,256]{2,1,0:T(8,128)(2,1)S(1)} %add_convert_fusion.23), channel_id=1, source_target_pairs={{0,16},{16,0},{1,17},{17,1},{2,18},{18,2},{3,19},{19,3},{4,20},{20... | collective-permute-start | bytes 98312 | tf_op jit(solution)/shard_map/ppermute | solution.py:89
  216.7 5.2 %collective-permute-start.45 = (bf16[1,64,256]{2,1,0:T(8,128)(2,1)S(1)}, bf16[1,64,256]{2,1,0:T(8,128)(2,1)S(1)}, u32[]{:S(2)}, u32[]{:S(2)}) collective-permute-start(bf16[1,64,256]{2,1,0:T(8,128)(2,1)S(1)} %add_convert_fusion.22), channel_id=1, source_target_pairs={{0,16},{16,0},{1,17},{17,1},{2,18},{18,2},{3,19},{19,3},{4,20},{20... | collective-permute-start | bytes 98312 | tf_op jit(solution)/shard_map/ppermute | solution.py:89
  218.5 4.9 %collective-permute-start.50 = (bf16[1,64,256]{2,1,0:T(8,128)(2,1)S(1)}, bf16[1,64,256]{2,1,0:T(8,128)(2,1)S(1)}, u32[]{:S(2)}, u32[]{:S(2)}) collective-permute-start(bf16[1,64,256]{2,1,0:T(8,128)(2,1)S(1)} %add_convert_fusion.21), channel_id=1, source_target_pairs={{0,16},{16,0},{1,17},{17,1},{2,18},{18,2},{3,19},{19,3},{4,20},{20... | collective-permute-start | bytes 98312 | tf_op jit(solution)/shard_map/ppermute | solution.py:89
  249.7 4.8 %collective-permute-start.51 = (bf16[16,96,768]{2,1,0:T(8,128)(2,1)}, bf16[16,96,768]{2,1,0:T(8,128)(2,1)S(1)}, u32[]{:S(2)}, u32[]{:S(2)}) collective-permute-start(bf16[16,96,768]{2,1,0:T(8,128)(2,1)} %get-tuple-element.89), channel_id=1, source_target_pairs={{0,2},{2,0},{1,3},{3,1},{4,6},{6,4},{5,7},{7,5},{8,10},{10,8},{9,1... | collective-permute-start | bytes 7077896 | tf_op jit(solution)/shard_map/ppermute | solution.py:89
  249.8 9.5 %collective-permute-start.56 = (bf16[16,96,768]{2,1,0:T(8,128)(2,1)}, bf16[16,96,768]{2,1,0:T(8,128)(2,1)S(1)}, u32[]{:S(2)}, u32[]{:S(2)}) collective-permute-start(bf16[16,96,768]{2,1,0:T(8,128)(2,1)} %get-tuple-element.91), channel_id=1, source_target_pairs={{0,2},{2,0},{1,3},{3,1},{4,6},{6,4},{5,7},{7,5},{8,10},{10,8},{9,1... | collective-permute-start | bytes 7077896 | tf_op jit(solution)/shard_map/ppermute | solution.py:89
  250.3 11.7 %collective-permute-start.61 = (bf16[16,96,768]{2,1,0:T(8,128)(2,1)}, bf16[16,96,768]{2,1,0:T(8,128)(2,1)S(1)}, u32[]{:S(2)}, u32[]{:S(2)}) collective-permute-start(bf16[16,96,768]{2,1,0:T(8,128)(2,1)} %get-tuple-element.93), channel_id=1, source_target_pairs={{0,2},{2,0},{1,3},{3,1},{4,6},{6,4},{5,7},{7,5},{8,10},{10,8},{9,1... | collective-permute-start | bytes 7077896 | tf_op jit(solution)/shard_map/ppermute | solution.py:89
  258.1 32.3 %collective-permute-start.52 = (bf16[8,96,768]{2,1,0:T(8,128)(2,1)}, bf16[8,96,768]{2,1,0:T(8,128)(2,1)}, u32[]{:S(2)}, u32[]{:S(2)}) collective-permute-start(bf16[8,96,768]{2,1,0:T(8,128)(2,1)} %add_convert_fusion.2), channel_id=1, source_target_pairs={{0,8},{8,0},{1,9},{9,1},{2,10},{10,2},{3,11},{11,3},{4,12},{12,4},... | collective-permute-start | bytes 3538952 | tf_op jit(solution)/shard_map/ppermute | solution.py:89
  261.1 31.9 %collective-permute-start.57 = (bf16[8,96,768]{2,1,0:T(8,128)(2,1)}, bf16[8,96,768]{2,1,0:T(8,128)(2,1)}, u32[]{:S(2)}, u32[]{:S(2)}) collective-permute-start(bf16[8,96,768]{2,1,0:T(8,128)(2,1)} %add_convert_fusion.1), channel_id=1, source_target_pairs={{0,1},{1,0},{2,3},{3,2},{4,5},{5,4},{6,7},{7,6},{8,9},{9,8},{10,11... | collective-permute-start | bytes 3538952 | tf_op jit(solution)/shard_map/ppermute | solution.py:89
  264.6 25.7 %all-to-all-start.2 = ((f32[32,3,128]{2,1,0:T(4,128)}), f32[32,3,128]{2,1,0:T(4,128)S(1)}, u32[]{:S(2)}, u32[]{:S(2)}) async-start(f32[32,3,128]{2,1,0:T(4,128)} %reshape.176), calls=%async_computation.2 | async-start | bytes 131072 | tf_op jit(solution)/shard_map/all_to_all | solution.py:1097
  267.6 29.8 %collective-permute-start.62 = (bf16[8,96,768]{2,1,0:T(8,128)(2,1)}, bf16[8,96,768]{2,1,0:T(8,128)(2,1)}, u32[]{:S(2)}, u32[]{:S(2)}) collective-permute-start(bf16[8,96,768]{2,1,0:T(8,128)(2,1)} %add_convert_fusion), channel_id=1, source_target_pairs={{0,4},{4,0},{1,5},{5,1},{2,6},{6,2},{3,7},{7,3},{8,12},{12,8},{9,1... | collective-permute-start | bytes 3538952 | tf_op jit(solution)/shard_map/ppermute | solution.py:89
  292.2 17.2 %collective-permute-start.53 = (bf16[4,96,768]{2,1,0:T(8,128)(2,1)S(1)}, bf16[4,96,768]{2,1,0:T(8,128)(2,1)S(1)}, u32[]{:S(2)}, u32[]{:S(2)}) collective-permute-start(bf16[4,96,768]{2,1,0:T(8,128)(2,1)S(1)} %add_convert_fusion.5), channel_id=1, source_target_pairs={{0,4},{4,0},{1,5},{5,1},{2,6},{6,2},{3,7},{7,3},{8,12},{12,8},{9,1... | collective-permute-start | bytes 1769480 | tf_op jit(solution)/shard_map/ppermute | solution.py:89
  294.6 17.9 %collective-permute-start.58 = (bf16[4,96,768]{2,1,0:T(8,128)(2,1)S(1)}, bf16[4,96,768]{2,1,0:T(8,128)(2,1)S(1)}, u32[]{:S(2)}, u32[]{:S(2)}) collective-permute-start(bf16[4,96,768]{2,1,0:T(8,128)(2,1)S(1)} %add_convert_fusion.4), channel_id=1, source_target_pairs={{0,8},{8,0},{1,9},{9,1},{2,10},{10,2},{3,11},{11,3},{4,12},{12,4},... | collective-permute-start | bytes 1769480 | tf_op jit(solution)/shard_map/ppermute | solution.py:89
  298.9 16.3 %collective-permute-start.63 = (bf16[4,96,768]{2,1,0:T(8,128)(2,1)S(1)}, bf16[4,96,768]{2,1,0:T(8,128)(2,1)S(1)}, u32[]{:S(2)}, u32[]{:S(2)}) collective-permute-start(bf16[4,96,768]{2,1,0:T(8,128)(2,1)S(1)} %add_convert_fusion.3), channel_id=1, source_target_pairs={{0,1},{1,0},{2,3},{3,2},{4,5},{5,4},{6,7},{7,6},{8,9},{9,8},{10,11... | collective-permute-start | bytes 1769480 | tf_op jit(solution)/shard_map/ppermute | solution.py:89
  310.7 8.8 %collective-permute-start.54 = (bf16[2,96,768]{2,1,0:T(8,128)(2,1)S(1)}, bf16[2,96,768]{2,1,0:T(8,128)(2,1)S(1)}, u32[]{:S(2)}, u32[]{:S(2)}) collective-permute-start(bf16[2,96,768]{2,1,0:T(8,128)(2,1)S(1)} %add_convert_fusion.8), channel_id=1, source_target_pairs={{0,1},{1,0},{2,3},{3,2},{4,5},{5,4},{6,7},{7,6},{8,9},{9,8},{10,11... | collective-permute-start | bytes 884744 | tf_op jit(solution)/shard_map/ppermute | solution.py:89
  313.6 9.5 %collective-permute-start.59 = (bf16[2,96,768]{2,1,0:T(8,128)(2,1)S(1)}, bf16[2,96,768]{2,1,0:T(8,128)(2,1)S(1)}, u32[]{:S(2)}, u32[]{:S(2)}) collective-permute-start(bf16[2,96,768]{2,1,0:T(8,128)(2,1)S(1)} %add_convert_fusion.7), channel_id=1, source_target_pairs={{0,4},{4,0},{1,5},{5,1},{2,6},{6,2},{3,7},{7,3},{8,12},{12,8},{9,1... | collective-permute-start | bytes 884744 | tf_op jit(solution)/shard_map/ppermute | solution.py:89
  316.3 9.6 %collective-permute-start.64 = (bf16[2,96,768]{2,1,0:T(8,128)(2,1)S(1)}, bf16[2,96,768]{2,1,0:T(8,128)(2,1)S(1)}, u32[]{:S(2)}, u32[]{:S(2)}) collective-permute-start(bf16[2,96,768]{2,1,0:T(8,128)(2,1)S(1)} %add_convert_fusion.6), channel_id=1, source_target_pairs={{0,8},{8,0},{1,9},{9,1},{2,10},{10,2},{3,11},{11,3},{4,12},{12,4},... | collective-permute-start | bytes 884744 | tf_op jit(solution)/shard_map/ppermute | solution.py:89
  320.7 16.4 %collective-permute-start.55 = (bf16[1,96,768]{2,1,0:T(8,128)(2,1)S(1)}, bf16[1,96,768]{2,1,0:T(8,128)(2,1)S(1)}, u32[]{:S(2)}, u32[]{:S(2)}) collective-permute-start(bf16[1,96,768]{2,1,0:T(8,128)(2,1)S(1)} %add_convert_fusion.14), channel_id=1, source_target_pairs={{0,16},{16,0},{1,17},{17,1},{2,18},{18,2},{3,19},{19,3},{4,20},{20... | collective-permute-start | bytes 442376 | tf_op jit(solution)/shard_map/ppermute | solution.py:89
  324.2 16.1 %collective-permute-start.60 = (bf16[1,96,768]{2,1,0:T(8,128)(2,1)S(1)}, bf16[1,96,768]{2,1,0:T(8,128)(2,1)S(1)}, u32[]{:S(2)}, u32[]{:S(2)}) collective-permute-start(bf16[1,96,768]{2,1,0:T(8,128)(2,1)S(1)} %add_convert_fusion.13), channel_id=1, source_target_pairs={{0,16},{16,0},{1,17},{17,1},{2,18},{18,2},{3,19},{19,3},{4,20},{20... | collective-permute-start | bytes 442376 | tf_op jit(solution)/shard_map/ppermute | solution.py:89
  327.0 15.2 %collective-permute-start.65 = (bf16[1,96,768]{2,1,0:T(8,128)(2,1)S(1)}, bf16[1,96,768]{2,1,0:T(8,128)(2,1)S(1)}, u32[]{:S(2)}, u32[]{:S(2)}) collective-permute-start(bf16[1,96,768]{2,1,0:T(8,128)(2,1)S(1)} %add_convert_fusion.12), channel_id=1, source_target_pairs={{0,16},{16,0},{1,17},{17,1},{2,18},{18,2},{3,19},{19,3},{4,20},{20... | collective-permute-start | bytes 442376 | tf_op jit(solution)/shard_map/ppermute | solution.py:89
  (30 other events, 149.5 us)

commit v4 on v3

--- a/solution.py
+++ b/solution.py
@@ -134,14 +134,14 @@
     for shard, order in zip(shards, orders):
         grown, masks = shard[None], [0]
         for name in order[:-2]:
-            grown = jnp.concatenate([grown, flip(grown, name)])
+            grown = lax.optimization_barrier(jnp.concatenate([grown, flip(grown, name)]))
             masks = masks + [mask | device_mask(name, names) for mask in masks]
         held.append((grown, masks))
     grown_all = [grown for grown, _ in held]
     others = [flip(grown, order[-2]) for grown, order in zip(grown_all, orders)]
     if work is not None:
-        grown_late, early = lax.optimization_barrier((grown_all, early))
-        grown_all, early = lax.optimization_barrier((grown_late, work(*early)))
+        late, early = lax.optimization_barrier((grown_all, early))
+        grown_all, early = lax.optimization_barrier((late, work(*early)))
     gathered = []
     for grown, other, (_, masks), order in zip(grown_all, others, held, orders):
         bit = device_mask(order[-2], names)
@@ -161,20 +161,28 @@
     return total
 
 
-def reduce_relative(keeps, sends, orders, late):
+def reduce_relative(keeps, sends, orders, state=None, works=()):
+    works = dict(works)
+    sends = list(sends)
     terms_all = [[keep] for keep in keeps]
-    sends = list(sends)
     for step in range(len(orders[0])):
         for k, order in enumerate(orders):
-            terms = terms_all[k] + [flip(sends[k], order[step])]
-            half = terms[0].shape[0] // 2
+            half = terms_all[k][0].shape[0] // 2
+            if step == 0:
+                urgent, rest = (flip(send, order[step]) for send in sends[k])
+            else:
+                other = flip(sends[k], order[step])
+                urgent, rest = other[half:], other[:half]
             if half:
-                sends[k] = add_terms([term[half:] for term in terms]).astype(terms[0].dtype)
-                terms = [term[:half] for term in terms]
-            terms_all[k] = terms
-        if step == 0 and late:
-            sends[-1], late = lax.optimization_barrier((sends[-1], late))
-    return [add_terms(terms)[0] for terms in terms_all], late
+                upper = [term[half:] for term in terms_all[k]] + [urgent]
+                sends[k] = add_terms(upper).astype(urgent.dtype)
+                terms_all[k] = [term[:half] for term in terms_all[k]] + [rest]
+            else:
+                terms_all[k] = terms_all[k] + [urgent]
+        if step in works:
+            sends[-1], state = lax.optimization_barrier((sends[-1], state))
+            state = works[step](state)
+    return [add_terms(terms)[0] for terms in terms_all], state
 
 
 def dot_nn(left, right):
@@ -188,6 +196,13 @@
     to = lax.broadcasted_iota(jnp.int32, (rows, rows), 0)
     source = lax.broadcasted_iota(jnp.int32, (rows, rows), 1)
     return (source == count * lax.rem(to, span) + lax.div(to, span)).astype(jnp.bfloat16)
+
+
+def deinterleave(count, rows):
+    span = rows // count
+    source = lax.broadcasted_iota(jnp.int32, (rows, rows), 1)
+    to = lax.broadcasted_iota(jnp.int32, (rows, rows), 0)
+    return (to == count * lax.rem(source, span) + lax.div(source, span)).astype(jnp.bfloat16)
 
 
 def valid_rows(len_ref, rows, seq_here):
@@ -229,57 +244,57 @@
     return 0.5 * (1.0 + lax.erf(value * 0.7071067811865476))
 
 
-def forward_kernel(plan, seq_here, *refs):
+def forward_kernel(plan, planes, seq_here, *refs):
     me_ref, len_ref, place_ref, x_ref, vec_ref = refs[:5]
     blocks = refs[5 : 5 + len(plan)]
     heads_ref, wall_ref, qkv_ref, att_ref, n1_ref, pre_ref, n2_ref, stat_ref = refs[
         5 + len(plan) : 13 + len(plan)
     ]
-    raw, turned, in_sem, out_sem = refs[13 + len(plan) :]
+    raw, turned, qkv, att, n1, pre_all, in_sem, out_sem = refs[13 + len(plan) :]
     rows, width = x_ref.shape
     length = rows // seq_here
     pairs = width // (2 * HEAD_DIM)
+    up = 4 * width
     me = me_ref[0]
-    for (part, unit, masks), block in zip(plan, blocks):
-        for place, mask in enumerate(masks):
-            row = pl.multiple_of((3 * (me ^ mask) + part) * unit, 16)
-            pltpu.make_async_copy(block.at[place], raw.at[pl.ds(row, unit)], in_sem).start()
+    for first in (True, False):
+        for (part, unit, masks), block in zip(plan, blocks):
+            for place, mask in enumerate(masks):
+                device = me ^ mask
+                early = device < planes
+
+                @pl.when(early if first else jnp.logical_not(early))
+                def _(device=device, part=part, unit=unit, block=block, place=place, first=first):
+                    row = pl.multiple_of((3 * device + part) * unit, 16)
+                    pltpu.make_async_copy(
+                        block.at[place], raw.at[pl.ds(row, unit)], in_sem.at[0 if first else 1]
+                    ).start()
+
+    copies = []
+
+    def save(source, target):
+        copy = pltpu.make_async_copy(source, target, out_sem.at[len(copies)])
+        copy.start()
+        copies.append(copy)
+
     valid = valid_rows(len_ref, rows, seq_here)
     x = (x_ref[...].astype(jnp.float32) * valid).astype(jnp.bfloat16)
-    pltpu.make_async_copy(raw, raw, in_sem).wait()
-
     split3, split4 = interleave(3, 384), interleave(4, 256)
+    arrived = raw.at[0 : 3 * width]
+    pltpu.make_async_copy(arrived, arrived, in_sem.at[0]).wait()
+
     for b in range(width // 128):
         block = dot_nn(split3, raw[384 * b : 384 * b + 384, :]).astype(jnp.bfloat16)
         for p in range(3):
             turned[width * p + 128 * b : width * p + 128 * b + 128, :] = block[
                 128 * p : 128 * p + 128
             ]
-    up = 4 * width
-    for b in range(width // 64):
-        block = dot_nn(split4, raw[up + 256 * b : up + 256 * b + 256, :]).astype(jnp.bfloat16)
-        for p in range(4):
-            row = width * (3 + p) + 64 * b
-            turned[row : row + 64, :] = block[64 * p : 64 * p + 64]
-    saves = [
-        pltpu.make_async_copy(source, target, out_sem.at[k])
-        for k, (source, target) in enumerate(
-            (
-                (turned.at[0 : 3 * width], wall_ref.at[0 : 3 * width]),
-                (raw.at[3 * width : up], wall_ref.at[3 * width : up]),
-                (turned.at[3 * width : 7 * width], wall_ref.at[up : 2 * up]),
-                (raw.at[2 * up : 3 * up], wall_ref.at[2 * up : 3 * up]),
-            )
-        )
-    ]
-    for save in saves:
-        save.start()
-
+    save(turned.at[0 : 3 * width], wall_ref.at[0 : 3 * width])
     for p, bias in ((0, 0), (1, None), (2, 1)):
         value = dot_nn(x, turned[width * p : width * (p + 1), :])
         if bias is not None:
             value = value + vec_ref[bias : bias + 1, :]
-        qkv_ref[:, width * p : width * (p + 1)] = value.astype(jnp.bfloat16)
+        qkv[:, width * p : width * (p + 1)] = value.astype(jnp.bfloat16)
+    save(qkv, qkv_ref)
 
     stats = jnp.zeros((2 * length, 128), jnp.float32)
     lane = lax.broadcasted_iota(jnp.int32, stats.shape, 1)
@@ -287,20 +302,32 @@
         here = slice(seq * length, (seq + 1) * length)
         for g in range(pairs):
             cols = [slice(width * p + 128 * g, width * p + 128 * g + 128) for p in range(3)]
-            query, key, value = (qkv_ref[here, c] for c in cols)
+            query, key, value = (qkv[here, c] for c in cols)
             scores = pair_scores(stack_pair(query), key, len_ref[seq])
             top = jnp.max(scores, axis=-1, keepdims=True)
             expo = jnp.exp(scores - top)
             total = jnp.sum(expo, axis=-1, keepdims=True)
             stats = jnp.where(lane == seq * pairs + g, top + jnp.log(total), stats)
             probs = (expo / total).astype(jnp.bfloat16)
-            att_ref[here, 128 * g : 128 * g + 128] = join_pair(dot_nn(probs, value)).astype(
+            att[here, 128 * g : 128 * g + 128] = join_pair(dot_nn(probs, value)).astype(
                 jnp.bfloat16
             )
-
-    branch = dot_nn(att_ref[...], raw[3 * width : up, :]) + vec_ref[2:3, :]
+    save(att, att_ref)
+    arrived = raw.at[3 * width : 3 * up]
+    pltpu.make_async_copy(arrived, arrived, in_sem.at[1]).wait()
+    save(raw.at[3 * width : up], wall_ref.at[3 * width : up])
+    save(raw.at[2 * up : 3 * up], wall_ref.at[2 * up : 3 * up])
+
+    branch = dot_nn(att[...], raw[3 * width : up, :]) + vec_ref[2:3, :]
+    for b in range(width // 64):
+        block = dot_nn(split4, raw[up + 256 * b : up + 256 * b + 256, :]).astype(jnp.bfloat16)
+        for p in range(4):
+            row = width * (3 + p) + 64 * b
+            turned[row : row + 64, :] = block[64 * p : 64 * p + 64]
+    save(turned.at[3 * width : 7 * width], wall_ref.at[up : 2 * up])
     normed, inverse = center_rows(x.astype(jnp.float32) + branch)
-    n1_ref[...] = normed
+    n1[...] = normed
+    save(n1, n1_ref)
     stat_one = seq_here * pairs
     hidden = normed * vec_ref[3:4, :] + vec_ref[4:5, :]
     hidden_low = hidden.astype(jnp.bfloat16)
@@ -308,7 +335,8 @@
     for p in range(4):
         pre = dot_nn(hidden_low, turned[width * (3 + p) : width * (4 + p), :])
         pre = pre + vec_ref[5 + p : 6 + p, :]
-        pre_ref[:, width * p : width * (p + 1)] = pre
+        pre_all[p] = pre
+        save(pre_all.at[p], pre_ref.at[p])
         act = (pre * gelu_phi(pre)).astype(jnp.bfloat16)
         total = total + dot_nn(act, raw[2 * up + width * p : 2 * up + width * (p + 1), :])
     normed, inverse_two = center_rows(total)
@@ -323,49 +351,72 @@
     spot = lax.broadcasted_iota(jnp.int32, (place_ref.shape[0], rows), 1)
     choose = (spot == place_ref[...]).astype(jnp.bfloat16)
     heads_ref[...] = dot_nn(choose, output).astype(jnp.bfloat16)
-    for save in saves:
-        save.wait()
-
-
-def backward_kernel(plan, unit, seq_here, *refs):
-    me_ref, len_ref, place_ref, x_ref, vec_ref, top_ref = refs[:6]
+    for copy in copies:
+        copy.wait()
+
+
+def send_block(source, sinks, spots, device, part, out_sem):
+    spot = spots[3 * device + part]
+    half = sinks[0].shape[0]
+
+    def copy(sink, place):
+        pltpu.make_async_copy(source, sink.at[place], out_sem).start()
+
+    keep, urgent, rest = sinks[3 * part : 3 * part + 3]
+    pl.when(spot < half)(functools.partial(copy, keep, spot))
+    pl.when((spot >= half) & (spot < half + half // 2))(
+        functools.partial(copy, rest, spot - half)
+    )
+    pl.when(spot >= half + half // 2)(functools.partial(copy, urgent, spot - half - half // 2))
+
+
+def sink_shapes(devices, block, dtype):
+    half = devices // 2
+    return [
+        jax.ShapeDtypeStruct((count,) + block, dtype)
+        for _ in range(3)
+        for count in (half, half // 2, half // 2)
+    ]
+
+
+def wait_sinks(sinks, out_sem):
+    for sink in sinks:
+        pltpu.make_async_copy(sink, sink, out_sem).wait()
+
+
+def backward_kernel(unit, seq_here, *refs):
+    len_ref, spots, place_ref, x_ref, vec_ref, top_ref = refs[:6]
     wall_ref, qkv_ref, att_ref, n1_ref, pre_ref, n2_ref, stat_ref = refs[6:13]
     gin_ref, dvec_ref = refs[13:15]
-    sinks = refs[15:21]
-    wall, grads, parts, dqkv, in_sem, out_sem = refs[21:]
+    sinks = refs[15:24]
+    wall, grads, parts, dqkv, qkv, att, n1, pre_all, in_sem, out_sem = refs[24:]
     rows, width = x_ref.shape
     length = rows // seq_here
     pairs = width // (2 * HEAD_DIM)
     low = jnp.bfloat16
-    me = me_ref[0]
     up = 4 * width
     loads = [
-        pltpu.make_async_copy(wall_ref.at[a:b], wall.at[a:b], in_sem.at[k])
-        for k, (a, b) in enumerate(((2 * up, 3 * up), (up, 2 * up), (0, up)))
+        pltpu.make_async_copy(source, target, in_sem.at[k])
+        for k, (source, target) in enumerate(
+            (
+                (pre_ref, pre_all),
+                (wall_ref.at[2 * up : 3 * up], wall.at[2 * up : 3 * up]),
+                (n1_ref, n1),
+                (wall_ref.at[up : 2 * up], wall.at[up : 2 * up]),
+                (att_ref, att),
+                (wall_ref.at[3 * width : up], wall.at[3 * width : up]),
+                (qkv_ref, qkv),
+                (wall_ref.at[0 : 3 * width], wall.at[0 : 3 * width]),
+            )
+        )
     ]
     for load in loads:
         load.start()
 
     def emit(first, last):
         for u in range(first // unit, last // unit):
-            part = u % 3
-            relative = (u // 3) ^ me
-            bits, core_bit = plan[part]
-            spot = sink_spot(relative, bits)
-            across = (relative & core_bit) != 0
-            source = grads.at[u * unit : (u + 1) * unit]
-
-            @pl.when(across)
-            def _(part=part, source=source, spot=spot):
-                pltpu.make_async_copy(
-                    source, sinks[2 * part + 1].at[spot], out_sem.at[2 * part + 1]
-                ).start()
-
-            @pl.when(jnp.logical_not(across))
-            def _(part=part, source=source, spot=spot):
-                pltpu.make_async_copy(
-                    source, sinks[2 * part].at[spot], out_sem.at[2 * part]
-                ).start()
+            block = grads.at[u * unit : (u + 1) * unit]
+            send_block(block, sinks, spots, u // 3, u % 3, out_sem)
 
     valid = valid_rows(len_ref, rows, seq_here)
     x = (x_ref[...].astype(jnp.float32) * valid).astype(low)
@@ -394,38 +445,41 @@
     d_resid = norm_back(d_output * vec_ref[10:11, :], normed, inverse_two)
     d_ffn = d_resid.astype(low)
     sums(9, d_ffn.astype(jnp.float32))
-    normed = n1_ref[...]
+    d_hidden = d_resid
+    for load in loads[:4]:
+        load.wait()
+    normed = n1[...]
     hidden_low = (normed * vec_ref[3:4, :] + vec_ref[4:5, :]).astype(low)
-    d_hidden = d_resid
-    for load in loads[:2]:
-        load.wait()
     for p in range(4):
-        pre = pre_ref[:, width * p : width * (p + 1)]
+        pre = pre_all[p]
         phi = gelu_phi(pre)
         act = (pre * phi).astype(low)
         down = slice(2 * up + width * p, 2 * up + width * (p + 1))
         grads[down, :] = contract_rows(act, d_ffn).astype(low)
+        emit(down.start, down.stop)
         slope = phi + pre * jnp.exp(-0.5 * pre * pre) * 0.3989422804014327
         d_pre = (contract_cols(d_ffn, wall[down, :]) * slope).astype(low)
         sums(5 + p, d_pre.astype(jnp.float32))
         parts[width * p : width * (p + 1), :] = contract_rows(hidden_low, d_pre).astype(low)
         d_hidden = d_hidden + contract_cols(d_pre, wall[up + width * p : up + width * (p + 1), :])
-    emit(2 * up, 3 * up)
-    split4 = interleave(4, 256)
+    merge4 = deinterleave(4, 256)
     for b in range(width // 64):
         block = jnp.concatenate(
             [parts[width * p + 64 * b : width * p + 64 * b + 64, :] for p in range(4)], axis=0
         )
-        grads[up + 256 * b : up + 256 * b + 256, :] = contract_rows(split4, block).astype(low)
-    emit(up, 2 * up)
+        grads[up + 256 * b : up + 256 * b + 256, :] = dot_nn(merge4, block).astype(low)
+        if b % 3 == 2:
+            emit(up + 256 * (b - 2), up + 256 * (b + 1))
 
     sums(3, d_hidden * normed)
     sums(4, d_hidden)
     d_resid = norm_back(d_hidden * vec_ref[3:4, :], normed, inverse_one)
     d_branch = d_resid.astype(low)
     sums(2, d_branch.astype(jnp.float32))
-    grads[3 * width : up, :] = contract_rows(att_ref[...], d_branch).astype(low)
-    loads[2].wait()
+    for load in loads[4:]:
+        load.wait()
+    grads[3 * width : up, :] = contract_rows(att[...], d_branch).astype(low)
+    emit(3 * width, up)
     d_att = contract_cols(d_branch, wall[3 * width : up, :]).astype(low)
     lane = lax.broadcasted_iota(jnp.int32, (2 * length, 128), 1)
     stats = stat_ref[0]
@@ -433,7 +487,7 @@
         here = slice(seq * length, (seq + 1) * length)
         for g in range(pairs):
             cols = [slice(width * p + 128 * g, width * p + 128 * g + 128) for p in range(3)]
-            query, key, value = (qkv_ref[here, c] for c in cols)
+            query, key, value = (qkv[here, c] for c in cols)
             query = stack_pair(query)
             log_sum = jnp.sum(
                 jnp.where(lane == seq * pairs + g, stats, 0.0), axis=-1, keepdims=True
@@ -449,24 +503,26 @@
             dqkv[here, cols[1]] = (contract_rows(d_scores, query) * scale).astype(low)
     sums(0, dqkv[:, :width].astype(jnp.float32))
     sums(1, dqkv[:, 2 * width :].astype(jnp.float32))
+    for p in range(3):
+        d_part = dqkv[:, width * p : width * (p + 1)]
+        parts[width * p : width * (p + 1), :] = contract_rows(x, d_part).astype(low)
+    merge3 = deinterleave(3, 384)
+    for b in range(width // 128):
+        block = jnp.concatenate(
+            [parts[width * p + 128 * b : width * p + 128 * b + 128, :] for p in range(3)], axis=0
+        )
+        grads[384 * b : 384 * b + 384, :] = dot_nn(merge3, block).astype(low)
+        if b % 2 == 1:
+            emit(384 * (b - 1), 384 * (b + 1))
     total = d_resid
     for p in range(3):
         d_part = dqkv[:, width * p : width * (p + 1)]
-        parts[width * p : width * (p + 1), :] = contract_rows(x, d_part).astype(low)
         total = total + contract_cols(d_part, wall[width * p : width * (p + 1), :])
-    split3 = interleave(3, 384)
-    for b in range(width // 128):
-        block = jnp.concatenate(
-            [parts[width * p + 128 * b : width * p + 128 * b + 128, :] for p in range(3)], axis=0
-        )
-        grads[384 * b : 384 * b + 384, :] = contract_rows(split3, block).astype(low)
-    emit(0, up)
     gin_ref[...] = total * valid
-    for k, sink in enumerate(sinks):
-        pltpu.make_async_copy(sink, sink, out_sem.at[k]).wait()
-
-
-def call_forward(me, lengths, places, rows, vecs, gathered, seq_here):
+    wait_sinks(sinks, out_sem)
+
+
+def call_forward(me, lengths, places, rows, vecs, gathered, devices, seq_here):
     count, width = rows.shape
     pieces = [(part, piece, masks) for part, own in enumerate(gathered) for piece, masks in own]
     plan = tuple((part, piece.shape[1], tuple(masks)) for part, piece, masks in pieces)
@@ -476,62 +532,69 @@
     hbm = pl.BlockSpec(memory_space=pl.ANY)
     low, full = jnp.bfloat16, jnp.float32
     return pl.pallas_call(
-        functools.partial(forward_kernel, plan, seq_here),
+        functools.partial(forward_kernel, plan, devices // 4, seq_here),
         out_shape=[
             jax.ShapeDtypeStruct((places.shape[0], width), low),
             jax.ShapeDtypeStruct((total, width), low),
             jax.ShapeDtypeStruct((count, 3 * width), low),
             jax.ShapeDtypeStruct((count, width), low),
             jax.ShapeDtypeStruct((count, width), full),
-            jax.ShapeDtypeStruct((count, 4 * width), full),
+            jax.ShapeDtypeStruct((4, count, width), full),
             jax.ShapeDtypeStruct((count, width), full),
             jax.ShapeDtypeStruct((2, count, 128), full),
         ],
         in_specs=[smem, smem, vmem, vmem, vmem] + [hbm] * len(pieces),
-        out_specs=[vmem, hbm] + [vmem] * 6,
+        out_specs=[vmem] + [hbm] * 5 + [vmem] * 2,
         scratch_shapes=[
             pltpu.VMEM((total, width), low),
             pltpu.VMEM((7 * width, width), low),
-            pltpu.SemaphoreType.DMA,
-            pltpu.SemaphoreType.DMA((4,)),
+            pltpu.VMEM((count, 3 * width), low),
+            pltpu.VMEM((count, width), low),
+            pltpu.VMEM((count, width), full),
+            pltpu.VMEM((4, count, width), full),
+            pltpu.SemaphoreType.DMA((2,)),
+            pltpu.SemaphoreType.DMA((11,)),
         ],
-        compiler_params=pltpu.CompilerParams(vmem_limit_bytes=56 * 2**20),
+        compiler_params=pltpu.CompilerParams(vmem_limit_bytes=58 * 2**20),
         cost_estimate=pl.CostEstimate(
             flops=2 * count * total * width, bytes_accessed=48 * 2**20, transcendentals=0
         ),
     )(me, lengths, places, rows, vecs, *[piece for _, piece, _ in pieces])
 
 
-def call_backward(me, lengths, places, rows, vecs, top, saved, plan, unit, seq_here):
+def call_backward(lengths, spots, places, rows, vecs, top, saved, unit, seq_here):
     count, width = rows.shape
     total = 12 * width
     vmem = pl.BlockSpec(memory_space=pltpu.VMEM)
     smem = pl.BlockSpec(memory_space=pltpu.SMEM)
     hbm = pl.BlockSpec(memory_space=pl.ANY)
     low, full = jnp.bfloat16, jnp.float32
-    half = total // unit // 6
     return pl.pallas_call(
-        functools.partial(backward_kernel, plan, unit, seq_here),
+        functools.partial(backward_kernel, unit, seq_here),
         out_shape=[
             jax.ShapeDtypeStruct((count, width), full),
             jax.ShapeDtypeStruct((12, width), full),
         ]
-        + [jax.ShapeDtypeStruct((half, unit, width), low)] * 6,
-        in_specs=[smem, smem, vmem, vmem, vmem, vmem, hbm] + [vmem] * 6,
-        out_specs=[vmem, vmem] + [hbm] * 6,
+        + sink_shapes(total // unit // 3, (unit, width), low),
+        in_specs=[smem, smem, vmem, vmem, vmem, vmem] + [hbm] * 5 + [vmem] * 2,
+        out_specs=[vmem, vmem] + [hbm] * 9,
         scratch_shapes=[
             pltpu.VMEM((total, width), low),
             pltpu.VMEM((total, width), low),
             pltpu.VMEM((4 * width, width), low),
             pltpu.VMEM((count, 3 * width), low),
-            pltpu.SemaphoreType.DMA((3,)),
-            pltpu.SemaphoreType.DMA((6,)),
+            pltpu.VMEM((count, 3 * width), low),
+            pltpu.VMEM((count, width), low),
+            pltpu.VMEM((count, width), full),
+            pltpu.VMEM((4, count, width), full),
+            pltpu.SemaphoreType.DMA((8,)),
+            pltpu.SemaphoreType.DMA,
         ],
-        compiler_params=pltpu.CompilerParams(vmem_limit_bytes=60 * 2**20),
+        compiler_params=pltpu.CompilerParams(vmem_limit_bytes=58 * 2**20),
         cost_estimate=pl.CostEstimate(
             flops=4 * count * total * width, bytes_accessed=48 * 2**20, transcendentals=0
         ),
-    )(me, lengths, places, rows, vecs, top, *saved)
+    )(lengths, spots, places, rows, vecs, top, *saved)
 
 
 def turn_lanes(shift, width):
@@ -540,7 +603,14 @@
     return (source == lax.broadcasted_iota(jnp.int32, (width, width), 1)).astype(jnp.bfloat16)
 
 
-def table_kernel(embed_here, shift_ref, rows_ref, ends_ref, table_ref, owned_ref, tall):
+def table_kernel(
+    embed_here, shift_ref, rows_ref, ends_ref, label_ref, table_ref, owned_ref, columns_ref, tall
+):
+    eye = eye_mask()
+    narrow = lax.broadcasted_iota(jnp.int32, (128, 2), 1)
+    for k in range(0, columns_ref.shape[0], 128):
+        label, used = (to_column(label_ref[row : row + 1, k : k + 128], eye) for row in (0, 1))
+        columns_ref[k : k + 128, :] = jnp.where(narrow == 0, label, used)
     count, width = table_ref.shape
     here = rows_ref.shape[0]
     shift = shift_ref[0]
@@ -558,27 +628,54 @@
     owned_ref[...] = jnp.where(owned, table, 0.0).astype(jnp.bfloat16)
 
 
-def call_table(shift, rows, ends, count, embed_here):
+def call_table(shift, rows, ends, labels, count, embed_here):
     width = rows.shape[1]
     vmem = pl.BlockSpec(memory_space=pltpu.VMEM)
     smem = pl.BlockSpec(memory_space=pltpu.SMEM)
     return pl.pallas_call(
         functools.partial(table_kernel, embed_here),
-        out_shape=[jax.ShapeDtypeStruct((count, width), jnp.bfloat16)] * 2,
-        in_specs=[smem, vmem, vmem],
-        out_specs=[vmem] * 2,
+        out_shape=[jax.ShapeDtypeStruct((count, width), jnp.bfloat16)] * 2
+        + [jax.ShapeDtypeStruct((labels.shape[1], 2), jnp.float32)],
+        in_specs=[smem, vmem, vmem, vmem],
+        out_specs=[vmem] * 3,
         scratch_shapes=[pltpu.VMEM((count + 16, width), jnp.float32)],
-        compiler_params=pltpu.CompilerParams(vmem_limit_bytes=32 * 2**20),
+        compiler_params=pltpu.CompilerParams(vmem_limit_bytes=22 * 2**20),
         cost_estimate=pl.CostEstimate(
             flops=32 * count * width * width, bytes_accessed=40 * 2**20, transcendentals=0
         ),
-    )(shift, rows, ends)
+    )(shift, rows, ends, labels)
+
+
+def eye_mask():
+    return lax.broadcasted_iota(jnp.int32, (128, 128), 0) == lax.broadcasted_iota(
+        jnp.int32, (128, 128), 1
+    )
+
+
+def to_row(column, eye):
+    return jnp.concatenate(
+        [
+            jnp.sum(jnp.where(eye, column[k : k + 128], 0.0), axis=0, keepdims=True)
+            for k in range(0, column.shape[0], 128)
+        ],
+        axis=1,
+    )
+
+
+def to_column(row, eye):
+    return jnp.concatenate(
+        [
+            jnp.sum(jnp.where(eye, row[:, k : k + 128], 0.0), axis=1, keepdims=True)
+            for k in range(0, row.shape[1], 128)
+        ],
+        axis=0,
+    )
 
 
 def logits_kernel(plan, embed_here, picks, span, *refs):
     me_ref, shift_ref, table_ref = refs[:3]
     blocks = refs[3 : 3 + len(plan)]
-    picked, first, expo_ref, stat_ref, in_sem = refs[3 + len(plan) :]
+    picked_ref, first, expo_ref, stat_ref, picked, expo_all, in_sem, out_sem = refs[3 + len(plan) :]
     count, width = table_ref.shape
     me, shift = me_ref[0], shift_ref[0]
     extra = first.shape[1]
@@ -594,24 +691,47 @@
             pltpu.make_async_copy(
                 block.at[place, pl.ds(picks, extra)], first.at[device, :, cols], in_sem.at[1]
             ).start()
-    start = lax.broadcasted_iota(jnp.int32, (count, 1), 0) * width - shift
-    owned = (start >= 0) & (start < embed_here)
-    touched = (start > -width) & (start < embed_here)
+    whole = embed_here // width // 128 * 128
+    eye = eye_mask()
     pltpu.make_async_copy(first, first, in_sem.at[1]).wait()
     pltpu.make_async_copy(picked, picked, in_sem.at[0]).wait()
+    copies = [pltpu.make_async_copy(picked, picked_ref, out_sem.at[0])]
+    copies[0].start()
     chunks = picked.shape[0] // span
-    for k in range(chunks):
-        here = slice(k * span, (k + 1) * span)
-        logits = jnp.where(touched, contract_cols(table_ref[...], picked[here, :]), -1e30)
-        top = jnp.max(logits, axis=0, keepdims=True)
-        expo = jnp.where(touched, jnp.exp(logits - top), 0.0)
-        total = jnp.sum(jnp.where(owned, expo, 0.0), axis=0, keepdims=True)
-        expo_ref[:, here] = expo
-        copies = stat_ref.shape[0]
-        stat_ref[:, k : k + 1, :] = jnp.broadcast_to(top[None], (copies, 1, span))
-        stat_ref[:, chunks + k : chunks + k + 1, :] = jnp.broadcast_to(
-            total[None], (copies, 1, span)
-        )
+    step = span // 2
+    row_start = lax.broadcasted_iota(jnp.int32, (1, count), 1) * width - shift
+    touched = (row_start < embed_here)[:, whole:]
+    owned = (row_start >= 0)[:, :128]
+    tops, totals = [], []
+    for k in range(0, picked.shape[0], step):
+        here = slice(k, k + step)
+        logits = contract_cols(picked[here, :], table_ref[...])
+        logits = jnp.concatenate(
+            [logits[:, :whole], jnp.where(touched, logits[:, whole:], -1e30)], axis=1
+        )
+        top = jnp.max(logits, axis=1, keepdims=True)
+        expo = jnp.exp(logits - top)
+        expo_all[here, :] = expo
+        copies.append(
+            pltpu.make_async_copy(
+                expo_all.at[here], expo_ref.at[here], out_sem.at[1 + k // step]
+            )
+        )
+        copies[-1].start()
+        ends = jnp.where(owned, expo[:, :128], 0.0)
+        total = jnp.sum(jnp.concatenate([ends, expo[:, 128:]], axis=1), axis=1, keepdims=True)
+        tops.append(to_row(top, eye))
+        totals.append(to_row(total, eye))
+    rows = [
+        jnp.concatenate(own[2 * k : 2 * k + 2], axis=1)
+        for own in (tops, totals)
+        for k in range(chunks)
+    ]
+    stats = jnp.concatenate(rows, axis=0)
+    for device in range(stat_ref.shape[0]):
+        stat_ref[device] = stats
+    for copy in copies:
+        copy.wait()
 
 
 def call_logits(me, shift, table, gathered, picks, embed_here, devices):
@@ -630,125 +750,180 @@
         out_shape=[
             jax.ShapeDtypeStruct((rows, width), low),
             jax.ShapeDtypeStruct((devices, extra, width), low),
-            jax.ShapeDtypeStruct((count, rows), full),
+            jax.ShapeDtypeStruct((rows, count), full),
             jax.ShapeDtypeStruct((devices, 8, span), full),
         ],
         in_specs=[smem, smem, vmem] + [hbm] * len(pieces),
-        out_specs=[vmem] * 4,
-        scratch_shapes=[pltpu.SemaphoreType.DMA((2,))],
-        compiler_params=pltpu.CompilerParams(vmem_limit_bytes=48 * 2**20),
+        out_specs=[hbm, vmem, hbm, vmem],
+        scratch_shapes=[
+            pltpu.VMEM((rows, width), low),
+            pltpu.VMEM((rows, count), full),
+            pltpu.SemaphoreType.DMA((2,)),
+            pltpu.SemaphoreType.DMA((9,)),
+        ],
+        compiler_params=pltpu.CompilerParams(vmem_limit_bytes=58 * 2**20),
         cost_estimate=pl.CostEstimate(
             flops=2 * rows * count * width, bytes_accessed=16 * 2**20, transcendentals=0
         ),
     )(me, shift, table, *[piece for _, piece, _ in pieces])
 
 
-def sink_spot(relative, bits):
-    spot = jnp.int32(0)
-    for k, bit in enumerate(bits):
-        spot = spot + jnp.where((relative & bit) != 0, 1 << (len(bits) - 1 - k), 0)
-    return spot
-
-
-def picked_kernel(plan, embed_here, picks, *refs):
-    me_ref, shift_ref, stat_ref, expo_ref, label_ref, owned_ref, dlog_ref = refs[:7]
-    sinks = refs[7:13]
-    terms, out_sem = refs[13:]
-    count, width = owned_ref.shape
-    me, shift = me_ref[0], shift_ref[0]
-    span = stat_ref.shape[2]
-    chunks = expo_ref.shape[1] // span
-    start = lax.broadcasted_iota(jnp.int32, (count, 1), 0) * width - shift
-    touched = (start > -width) & (start < embed_here)
-    row = lax.broadcasted_iota(jnp.int32, (count, span), 0)
-    mine = stat_ref[pl.ds(me, 1)]
-    for k in range(chunks):
-        here = slice(k * span, (k + 1) * span)
-        tops = stat_ref[:, k : k + 1, :]
-        top = jnp.max(tops, axis=0)
-        total = jnp.sum(
-            stat_ref[:, chunks + k : chunks + k + 1, :] * jnp.exp(tops - top[None]), axis=0
-        )
-        scale = jnp.exp(mine[0, k : k + 1, :] - top) / total
-        hot = (row == label_ref[0:1, here]) & touched
-        used = label_ref[1:2, here] > 0
-        probs = expo_ref[:, here] * scale
-        d_logits = jnp.where(used, jnp.where(hot, probs - 1.0, probs), 0.0).astype(jnp.bfloat16)
-        dlog_ref[:, here] = d_logits
-        terms[here, :] = contract_rows(d_logits, owned_ref[...]).astype(jnp.bfloat16)
-        for b in range(span // picks):
-            device = k * (span // picks) + b
-            for part, (bits, core_bit) in enumerate(plan):
-                relative = device ^ me
-                spot = sink_spot(relative, bits)
-                across = (relative & core_bit) != 0
-                cut = width // len(plan)
-                source = terms.at[
-                    device * picks : (device + 1) * picks, part * cut : (part + 1) * cut
-                ]
-
-                @pl.when(across)
-                def _(part=part, source=source, spot=spot):
-                    pltpu.make_async_copy(
-                        source, sinks[2 * part + 1].at[spot], out_sem.at[2 * part + 1]
-                    ).start()
-
-                @pl.when(jnp.logical_not(across))
-                def _(part=part, source=source, spot=spot):
-                    pltpu.make_async_copy(
-                        source, sinks[2 * part].at[spot], out_sem.at[2 * part]
-                    ).start()
-
-    for k, sink in enumerate(sinks):
-        pltpu.make_async_copy(sink, sink, out_sem.at[k]).wait()
-
-
-def call_picked(me, shift, stats, expo, labels, owned, plan, picks, embed_here):
-    count, width = owned.shape
-    devices, rows = stats.shape[0], expo.shape[1]
-    vmem = pl.BlockSpec(memory_space=pltpu.VMEM)
+def mix_kernel(expo_ref, column_ref, owned_ref, mix_ref, row_ref, own_ref):
+    rows, count = expo_ref.shape
+    step = min(rows, 256)
+    lane = lax.broadcasted_iota(jnp.int32, (step, count), 1)
+    for k in range(0, rows, step):
+        here = slice(k, k + step)
+        expo = expo_ref[here, :]
+        hot = lane == column_ref[here, 0:1].astype(jnp.int32)
+        own_ref[here, :] = jnp.sum(jnp.where(hot, expo, 0.0), axis=1, keepdims=True)
+        others = jnp.where(hot, 0.0, expo).astype(jnp.bfloat16)
+        mix_ref[here, :] = dot_nn(others, owned_ref[...]).astype(jnp.bfloat16)
+        row_ref[here, :] = dot_nn(hot.astype(jnp.bfloat16), owned_ref[...]).astype(jnp.bfloat16)
+
+
+def call_mix(expo, columns, owned):
+    rows, count = expo.shape
+    width = owned.shape[1]
+    low = jnp.bfloat16
+    step = rows // 4
+
+    def tile(lanes):
+        return pl.BlockSpec((step, lanes), lambda k: (k, 0))
+
+    return pl.pallas_call(
+        mix_kernel,
+        grid=(4,),
+        out_shape=[
+            jax.ShapeDtypeStruct((rows, width), low),
+            jax.ShapeDtypeStruct((rows, width), low),
+            jax.ShapeDtypeStruct((rows, 1), jnp.float32),
+        ],
+        in_specs=[tile(count), tile(2), pl.BlockSpec((count, width), lambda k: (0, 0))],
+        out_specs=[tile(width), tile(width), tile(1)],
+        compiler_params=pltpu.CompilerParams(vmem_limit_bytes=48 * 2**20),
+        cost_estimate=pl.CostEstimate(
+            flops=16 * rows * count * width, bytes_accessed=64 * 2**20, transcendentals=0
+        ),
+    )(expo, columns, owned)
+
+
+def terms_kernel(picks, *refs):
+    me_ref, spots, stat_ref, mix_ref, row_ref, own_ref, column_ref, scale_ref = refs[:8]
+    sinks = refs[8:17]
+    terms, out_sem = refs[17:]
+    span, width = mix_ref.shape
+    chunks = terms.shape[0]
+    chunk = pl.program_id(0)
+    mine = stat_ref[pl.ds(me_ref[0], 1), pl.ds(chunk, 1), :][0]
+    tops = stat_ref[:, pl.ds(chunk, 1), :]
+    top = jnp.max(tops, axis=0)
+    totals = stat_ref[:, pl.ds(chunks + chunk, 1), :]
+    total = jnp.sum(totals * jnp.exp(tops - top[None]), axis=0)
+    scale = to_column(jnp.exp(mine - top) / total, eye_mask())
+    scale_ref[...] = scale
+    used = column_ref[:, 1:2]
+    label = (own_ref[...] * scale - 1.0).astype(jnp.bfloat16).astype(jnp.float32)
+    terms[chunk] = (
+        mix_ref[...].astype(jnp.float32) * (scale * used)
+        + row_ref[...].astype(jnp.float32) * (label * used)
+    ).astype(jnp.bfloat16)
+    cut = width // 3
+    for b in range(span // picks):
+        for part in range(3):
+            source = terms.at[
+                chunk, b * picks : (b + 1) * picks, part * cut : (part + 1) * cut
+            ]
+            send_block(source, sinks, spots, chunk * (span // picks) + b, part, out_sem)
+
+    @pl.when(chunk == chunks - 1)
+    def _():
+        wait_sinks(sinks, out_sem)
+
+
+def call_terms(me, spots, stats, mix, label_rows, own, columns, picks):
+    rows, width = mix.shape
+    devices, _, span = stats.shape
     smem = pl.BlockSpec(memory_space=pltpu.SMEM)
     hbm = pl.BlockSpec(memory_space=pl.ANY)
     low = jnp.bfloat16
+
+    def tile(lanes):
+        return pl.BlockSpec((span, lanes), lambda k: (k, 0))
+
     return pl.pallas_call(
-        functools.partial(picked_kernel, plan, embed_here, picks),
-        out_shape=[jax.ShapeDtypeStruct((count, rows), low)]
-        + [jax.ShapeDtypeStruct((devices // 2, picks, width // 3), low)] * 6,
-        in_specs=[smem, smem, vmem, vmem, vmem, vmem],
-        out_specs=[vmem] + [hbm] * 6,
-        scratch_shapes=[pltpu.VMEM((rows, width), low), pltpu.SemaphoreType.DMA((6,))],
+        functools.partial(terms_kernel, picks),
+        grid=(rows // span,),
+        out_shape=[jax.ShapeDtypeStruct((rows, 1), jnp.float32)]
+        + sink_shapes(devices, (picks, width // 3), low),
+        in_specs=[
+            smem,
+            smem,
+            pl.BlockSpec(stats.shape, lambda k: (0, 0, 0)),
+            tile(width),
+            tile(width),
+            tile(1),
+            tile(2),
+        ],
+        out_specs=[tile(1)] + [hbm] * 9,
+        scratch_shapes=[
+            pltpu.VMEM((rows // span, span, width), low),
+            pltpu.SemaphoreType.DMA,
+        ],
         compiler_params=pltpu.CompilerParams(vmem_limit_bytes=48 * 2**20),
         cost_estimate=pl.CostEstimate(
-            flops=2 * rows * count * width, bytes_accessed=16 * 2**20, transcendentals=0
+            flops=8 * rows * width, bytes_accessed=10 * 2**20, transcendentals=0
         ),
-    )(me, shift, stats, expo, labels, owned)
-
-
-def embed_kernel(shift_ref, dlog_ref, picked_ref, out_ref, wide):
+    )(me, spots, stats, mix, label_rows, own, columns)
+
+
+def embed_kernel(shift_ref, expo_ref, scale_ref, column_ref, picked_ref, out_ref, wide):
     here, width = out_ref.shape
+    rows, count = expo_ref.shape
     shift = shift_ref[0]
+    chunk = pl.program_id(0)
+    probs = expo_ref[...] * scale_ref[...]
+    lane = lax.broadcasted_iota(jnp.int32, (rows, count), 1)
+    hot = lane == column_ref[:, 0:1].astype(jnp.int32)
+    terms = (jnp.where(hot, probs - 1.0, probs) * column_ref[:, 1:2]).astype(jnp.bfloat16)
     turned = contract_cols(picked_ref[...], turn_lanes(shift, width)).astype(jnp.bfloat16)
-    wide[...] = dot_nn(dlog_ref[...], turned)
-    lane = lax.broadcasted_iota(jnp.int32, (here, width), 1)
-    out_ref[...] = jnp.where(lane < width - shift, wide[:here, :], wide[1 : here + 1, :])
-
-
-def call_embed(shift, dlog, picked, here):
-    count, rows = dlog.shape
+    total = contract_rows(terms, turned)
+
+    @pl.when(chunk == 0)
+    def _():
+        wide[...] = total
+
+    @pl.when(chunk > 0)
+    def _():
+        wide[...] = wide[...] + total
+
+    @pl.when(chunk == pl.num_programs(0) - 1)
+    def _():
+        lane = lax.broadcasted_iota(jnp.int32, (here, width), 1)
+        out_ref[...] = jnp.where(lane < width - shift, wide[:here, :], wide[1 : here + 1, :])
+
+
+def call_embed(shift, expo, scale, columns, picked, here):
+    rows, count = expo.shape
     width = picked.shape[1]
-    vmem = pl.BlockSpec(memory_space=pltpu.VMEM)
     smem = pl.BlockSpec(memory_space=pltpu.SMEM)
+    step = rows // 8
+
+    def tile(lanes):
+        return pl.BlockSpec((step, lanes), lambda k: (k, 0))
+
     return pl.pallas_call(
         embed_kernel,
+        grid=(8,),
         out_shape=jax.ShapeDtypeStruct((here, width), jnp.float32),
-        in_specs=[smem, vmem, vmem],
-        out_specs=vmem,
+        in_specs=[smem, tile(count), tile(1), tile(2), tile(width)],
+        out_specs=pl.BlockSpec((here, width), lambda k: (0, 0)),
         scratch_shapes=[pltpu.VMEM((count, width), jnp.float32)],
-        compiler_params=pltpu.CompilerParams(vmem_limit_bytes=40 * 2**20),
+        compiler_params=pltpu.CompilerParams(vmem_limit_bytes=20 * 2**20),
         cost_estimate=pl.CostEstimate(
             flops=16 * rows * count * width, bytes_accessed=64 * 2**20, transcendentals=0
         ),
-    )(shift, dlog, picked)
+    )(shift, expo, scale, columns, picked)
 
 
 def plain_forward(mats_all, vecs_all, block_input, span_lengths):
@@ -912,41 +1087,56 @@
     vec_here = vectors.shape[0]
     mats_low = layer_mats.astype(low).reshape(3, third, width)
 
-    def pad_row(row):
-        return jnp.pad(row, (0, width - row.shape[0])).astype(low)[None]
-
     labels_flat = mlm_labels.reshape(-1)
-    small = jnp.concatenate(
+    common = jnp.concatenate(
         [
-            pad_row(vectors.astype(low)),
-            pad_row(labels_flat // 256),
-            pad_row(labels_flat % 256),
-            pad_row(jnp.concatenate([span_pairs // 256, span_pairs % 256, span_lengths // 4])),
-            embedding[-width:].astype(low)[None],
-            embedding[:width].astype(low)[None],
-            jnp.zeros((2, width), low),
+            value.astype(low)
+            for value in (
+                vectors,
+                labels_flat // 256,
+                labels_flat % 256,
+                span_pairs // 256,
+                span_pairs % 256,
+                span_lengths // 4,
+            )
         ]
     )
-    small_all = lax.all_to_all(
-        jnp.broadcast_to(small, (devices,) + small.shape), names, 0, 0, tiled=True
-    )
+    ends = [vec_here, picks_here, picks_here, seq_here, seq_here, seq_here]
+    common = jnp.pad(common, (0, width - common.shape[0]))
+    others = jnp.arange(devices)[:, None]
+    right, left = (me + 1) % devices, (me + devices - 1) % devices
+    border = jnp.where(
+        others == right,
+        embedding[-width:].astype(low),
+        jnp.where(others == left, embedding[:width].astype(low), jnp.zeros((), low)),
+    )
+    small = jnp.stack([jnp.broadcast_to(common, border.shape), border], axis=1)
+    small_all = lax.all_to_all(small, names, 0, 0, tiled=True)
+    starts = [sum(ends[:k]) for k in range(len(ends))]
+    vecs_all, labels_high, labels_low, pairs_high, pairs_low, quarter_all = (
+        small_all[:, 0, start : start + size] for start, size in zip(starts, ends)
+    )
+
     embed_here = embedding.shape[0]
     shifted_rows = -(-embed_here // width)
     over = shifted_rows * width - embed_here
     shift = (me * (embed_here % width)) % width
     first_row = me * (embed_here // width) + (me * (embed_here % width)) // width
-    shifted = jnp.pad(embedding.astype(low), (0, over)).reshape(shifted_rows, width)
-    from_left = lax.dynamic_index_in_dim(small_all[:, 4], (me + devices - 1) % devices, 0, False)
-    from_right = lax.dynamic_index_in_dim(small_all[:, 5], (me + 1) % devices, 0, False)
+
+    def table_shard(embedding):
+        return jnp.pad(embedding.astype(low), (0, over)).reshape(shifted_rows, width)
+
+    from_left = lax.dynamic_index_in_dim(small_all[:, 1], left, 0, False)
+    from_right = lax.dynamic_index_in_dim(small_all[:, 1], right, 0, False)
     right_rows = jnp.pad(from_right, (width - over, over)).reshape(2, width)
-    vec_rows = small_all[:, 0, :vec_here].reshape(-1).astype(jnp.float32).reshape(-1, width)
-    labels_all = (
-        small_all[:, 1, :picks_here].astype(jnp.int32) * 256
-        + small_all[:, 2, :picks_here].astype(jnp.int32)
-    ).reshape(-1)
-    ints_all = small_all[:, 3, : 3 * seq_here].astype(jnp.int32)
-    pairs_all = (ints_all[:, :seq_here] * 256 + ints_all[:, seq_here : 2 * seq_here]).reshape(-1)
-    quarter_all = ints_all[:, 2 * seq_here :].reshape(-1)
+    vec_rows = vecs_all.reshape(-1).astype(jnp.float32).reshape(-1, width)
+
+    def whole(high, small):
+        return (high.astype(jnp.int32) * 256 + small.astype(jnp.int32)).reshape(-1)
+
+    labels_all = whole(labels_high, labels_low)
+    pairs_all = whole(pairs_high, pairs_low)
+    quarter_all = quarter_all.astype(jnp.int32).reshape(-1)
     row_of = labels_all - first_row
     used = (jnp.arange(slots)[None, :] < quarter_all[:, None]).reshape(-1)
     seq_start = jnp.arange(seq_here, dtype=jnp.int32) * length
@@ -967,6 +1157,16 @@
         ) * span_scale
 
     step_float = float(ADAM_STEP)
+
+    def embed_step(grad_rows):
+        grad = grad_rows.reshape(-1)[:embed_here]
+        return grad, adam_step(embedding, grad, mom1_embed, mom2_embed, step_float, decay_rate)
+
+    def sum_vectors(d_vecs):
+        terms = d_vecs.reshape(devices, 1, vec_here)
+        terms = lax.all_to_all(terms, names, 0, 0, tiled=True)
+        return jnp.sum(terms, axis=(0, 1))
+
     cut = width // 3
     columns = [slice(k * cut, (k + 1) * cut) for k in range(3)]
     back_orders = [order[::-1] for order in orders]
@@ -974,7 +1174,18 @@
         lone = me.astype(jnp.int32).reshape(1)
         lone_shift = shift.astype(jnp.int32).reshape(1)
         tok_rows = block_input.reshape(rows_here, width)
-        head_rows = picks_here + 16
+        relative = jnp.arange(devices, dtype=jnp.int32) ^ me.astype(jnp.int32)
+        spots = jnp.stack(
+            [
+                sum(
+                    ((relative & device_mask(name, names)) != 0).astype(jnp.int32)
+                    << (len(names) - 1 - k)
+                    for k, name in enumerate(order)
+                )
+                for order in back_orders
+            ],
+            axis=1,
+        ).reshape(-1)
         places = jnp.concatenate(
             [
                 (mlm_positions + seq_start[:, None]).reshape(-1),
@@ -985,49 +1196,66 @@
         ends = jnp.pad(
             jnp.concatenate([from_left[None], right_rows]).astype(jnp.float32), ((0, 5), (0, 0))
         )
-        table_rows = -(-(shifted_rows + 1) // 16) * 16
+        table_rows = -(-(shifted_rows + 1) // 128) * 128
         labels = jnp.pad(
-            jnp.stack([row_of, used.astype(jnp.int32)]).astype(jnp.int32), ((0, 6), (0, 0))
-        )
-
-        def prepare(shifted, ends, vec_rows, labels):
-            table, owned = call_table(lone_shift, shifted, ends, table_rows, embed_here)
-            return table, owned, vec_rows, labels
-
-        gathered, (table, owned, vec_rows, labels) = gather_relative(
-            mats_low, orders, names, (shifted, ends, vec_rows, labels), prepare
+            jnp.stack([row_of.astype(jnp.float32), used.astype(jnp.float32)]), ((0, 6), (0, 0))
+        )
+
+        def prepare(embedding, ends, labels, *others):
+            shifted = table_shard(embedding)
+            table = call_table(lone_shift, shifted, ends, labels, table_rows, embed_here)
+            return *table, *others
+
+        gathered, (table, owned, columns_all, vec_rows) = gather_relative(
+            mats_low, orders, names, (embedding, ends, labels, vec_rows), prepare
         )
         heads, *saved = call_forward(
-            lone, span_lengths, places[:, None], tok_rows, vec_rows, gathered, seq_here
+            lone, span_lengths, places[:, None], tok_rows, vec_rows, gathered, devices, seq_here
         )
         heads_all, _ = gather_relative([heads[:, c] for c in columns], orders, names)
         picked, cls_rows, expo, stats = call_logits(
             lone, lone_shift, table, heads_all, picks_here, embed_here, devices
         )
         stats = lax.all_to_all(stats, names, 0, 0, tiled=True)
-        plan = tuple(
-            (tuple(device_mask(name, names) for name in order[1:]), device_mask(order[0], names))
-            for order in back_orders
-        )
-        d_logits, *sinks = call_picked(
-            lone, lone_shift, stats, expo, labels, owned, plan, picks_here, embed_here
+        mix, hot_rows, own = call_mix(expo, columns_all, owned)
+        scale, *sinks = call_terms(
+            lone, spots, stats, mix, hot_rows, own, columns_all, picks_here
         )
         d_cls = span_terms(cls_rows[:, :seq_here].reshape(-1, width))
-        d_parts, _ = reduce_relative(sinks[0::2], sinks[1::2], back_orders, ())
+        d_parts, _ = reduce_relative(
+            sinks[0::3], list(zip(sinks[1::3], sinks[2::3])), back_orders
+        )
         top = jnp.concatenate(
             [jnp.concatenate(d_parts, axis=1), jnp.pad(d_cls, ((0, 16 - seq_here), (0, 0)))]
         )
         grad_input, d_vecs, *sinks = call_backward(
-            lone, span_lengths, places[None], tok_rows, vec_rows, top, saved, plan, third, seq_here
+            span_lengths, spots, places[None], tok_rows, vec_rows, top, saved, third, seq_here
         )
         grad_input = grad_input.reshape(seq_here, length, width)
-        summed, (d_logits, picked, d_vecs) = reduce_relative(
-            sinks[0::2], sinks[1::2], back_orders, (d_logits, picked, d_vecs)
-        )
-        grad_embed = call_embed(lone_shift, d_logits, picked, shifted_rows)
+        def table_grad(state):
+            expo, picked, d_vecs = state
+            grad_embed = call_embed(
+                lone_shift, expo, scale, columns_all, picked, shifted_rows
+            )
+            grad_embed, d_vecs = lax.optimization_barrier((grad_embed, d_vecs))
+            return grad_embed, sum_vectors(d_vecs)
+
+        def table_step(state):
+            grad_embed, grad_vecs = state
+            return *embed_step(grad_embed), grad_vecs
+
+        summed, (grad_embed, step_embed, grad_vecs) = reduce_relative(
+            sinks[0::3],
+            list(zip(sinks[1::3], sinks[2::3])),
+            back_orders,
+            (expo, picked, d_vecs),
+            {0: table_grad, len(names) - 2: table_step},
+        )
     else:
         same_row = (jnp.arange(width) < width - shift)[None, :]
-        tall = jnp.concatenate([from_left[None], shifted, jnp.zeros((1, width), low)])
+        tall = jnp.concatenate(
+            [from_left[None], table_shard(embedding), jnp.zeros((1, width), low)]
+        )
         tall = tall.at[shifted_rows : shifted_rows + 2].add(right_rows)
         lanes = jnp.arange(width)
         turn = ((lanes[:, None] + shift) % width == lanes[None, :]).astype(low)
@@ -1090,17 +1318,11 @@
         ]
         picked_turned = jnp.dot(picked, turn.T, preferred_element_type=jnp.float32).astype(low)
         d_rolled = contract_rows(d_logits, picked_turned)
-        grad_embed = jnp.where(same_row, d_rolled[:-1], d_rolled[1:])
-    grad_embed = grad_embed.reshape(-1)[:embed_here]
+        grad_embed, step_embed = embed_step(jnp.where(same_row, d_rolled[:-1], d_rolled[1:]))
+        grad_vecs = sum_vectors(d_vecs)
     grad_mats = jnp.concatenate(summed).reshape(-1)
-    vec_terms = jnp.pad(d_vecs.reshape(devices, vec_here), ((0, 0), (0, -vec_here % 128)))
-    vec_terms = lax.all_to_all(
-        vec_terms.reshape(devices, -1, 128), names, 0, 0, tiled=True
-    ).reshape(devices, -1)
-    grad_vecs = jnp.sum(vec_terms, axis=0)[:vec_here]
     step_mats = adam_step(layer_mats, grad_mats, mom1_mats, mom2_mats, step_float, decay_rate)
     step_vecs = adam_step(vectors, grad_vecs, mom1_vecs, mom2_vecs, step_float, 0.0)
-    step_embed = adam_step(embedding, grad_embed, mom1_embed, mom2_embed, step_float, decay_rate)
     return (grad_input, grad_mats, grad_vecs, grad_embed, step_mats, step_vecs, step_embed)
 
 

time: 352 us -> 332 us (0.943)
  local copies, waits for them, and re-layouts: 36.3 us -> 24.2 us
  waiting for transfers between devices: 98.6 us -> 90.1 us
  starting transfers between devices: 85.2 us -> 78.9 us
  other arithmetic: 48.6 us -> 52.4 us
    all_to_all x1, waiting for transfers between devices: 14 us -> 0.01 us  [on_device(): stats = lax.all_to_all(stats, names, 0, 0, tiled=True)]
    ppermute x66 -> x72, starting transfers between devices: 73.4 us -> 67.2 us  [flip(): return lax.ppermute(value, name, [(0, 1), (1, 0)])]
    ppermute x66 -> x72, waiting for transfers between devices: 84.2 us -> 90.1 us  [flip(): return lax.ppermute(value, name, [(0, 1), (1, 0)])]
    unnamed x59 -> x82, local copies, waits for them, and re-layouts: 17.3 us -> 11.9 us
    concatenate x4 -> x1, local copies, waits for them, and re-layouts: 4.78 us -> 0.1 us  [on_device(): jnp.concatenate([value.astype(low) for value in (vectors, labels_flat //...]
    convert_element_type x29 -> x31, other arithmetic: 20.9 us -> 24.8 us  [the longest x24 24.5 us: reduce_relative(): sends[k] = add_terms(upper).astype(urgent.dtype)]
    pallas_call x4 -> x5, Pallas kernels: 63 us -> 66.9 us  [the longest x1 23.1 us: call_backward(): pl.pallas_call(functools.partial(backward_kernel, unit, seq_here), out_sh...]
    concatenate x16 -> x18, other arithmetic: 7.62 us -> 5.63 us  [gather_relative(): jnp.concatenate([grown, flip(grown, name)])]
  transfers between devices with their start and end apart: 69 -> 75, of which waited for: 37 -> 37; matrix products, arithmetic and copies ran while one was open for 20% -> 17% of each run, Pallas kernels for 2% -> 8%
where the time goes in v4:
time: 332 us; the launch traced here: 326 us
  waiting for transfers between devices  90.1 us (27%)
  starting transfers between devices  78.9 us (24%)
  Pallas kernels  78.2 us (24%)
  other arithmetic  52.4 us (16%)
  local copies, waits for them, and re-layouts  24.2 us (7%)
    ppermute x72, waiting for transfers between devices, flip(): return lax.ppermute(value, name, [(0, 1), (1, 0)])  90.1 us
    ppermute x72, starting transfers between devices, flip(): return lax.ppermute(value, name, [(0, 1), (1, 0)])  67.2 us
    convert_element_type x24, other arithmetic, reduce_relative(): sends[k] = add_terms(upper).astype(urgent.dtype)  24.5 us
    pallas_call x1, Pallas kernels, call_backward(): pl.pallas_call(functools.partial(backward_kernel, unit, seq_here), out_sh...  23.1 us
    pallas_call x1, Pallas kernels, call_forward(): pl.pallas_call(functools.partial(forward_kernel, plan, devices // 4, seq_...  13.8 us
    add x3, other arithmetic, adam_step(): return first_hat / (jnp.sqrt(second_hat) + adam_eps) + decay * weight  12.6 us
    unnamed x82, local copies, waits for them, and re-layouts  11.9 us
    pallas_call x1, Pallas kernels, call_embed(): pl.pallas_call(embed_kernel, grid=(8,), out_shape=jax.ShapeDtypeStruct((h...  11.7 us
  transfers between devices with their start and end apart: 75, of which 37 were waited for; matrix products, arithmetic and copies ran while one was open for 17% of the time, Pallas kernels for 8%

profile of v4, /device:TPU:0, one launch (start us, length us, event | category | flops | bytes accessed | tf_op | source)
XLA Modules:
  0.0 326.4 jit_solution(5615529024870040659)
XLA Ops:
  2.2 4.1 %collective-permute-start = (bf16[1,96,768]{2,1,0:T(8,128)(2,1)S(1)}, bf16[1,96,768]{2,1,0:T(8,128)(2,1)}, u32[]{:S(2)}, u32[]{:S(2)}) collective-permute-start(bf16[1,96,768]{2,1,0:T(8,128)(2,1)S(1)} %unstack.16), channel_id=1, source_target_pairs={{0,16},{16,0},{1,17},{17,1},{2,18},{18,2},{3,19},{19,3},{4,20},{20... | collective-permute-start | bytes 442376 | tf_op jit(solution)/shard_map/ppermute | solution.py:89
  6.7 3.0 collective-permute-start.6
  11.7 3.8 %all-to-all-start = ((bf16[32,2,768]{2,1,0:T(2,128)(2,1)}), bf16[32,2,768]{2,1,0:T(2,128)(2,1)S(1)}, u32[]{:S(2)}, u32[]{:S(2)}) async-start(bf16[32,2,768]{2,1,0:T(2,128)(2,1)} %pad_maximum_fusion.16), calls=%async_computation | async-start | bytes 196608 | tf_op jit(solution)/shard_map/all_to_all | solution.py:1114
  15.6 5.4 %collective-permute-done = bf16[1,96,768]{2,1,0:T(8,128)(2,1)} collective-permute-done((bf16[1,96,768]{2,1,0:T(8,128)(2,1)S(1)}, bf16[1,96,768]{2,1,0:T(8,128)(2,1)}, u32[]{:S(2)}, u32[]{:S(2)}) %collective-permute-start) | collective-permute-done | bytes 147488 | tf_op jit(solution)/shard_map/ppermute | solution.py:89
  22.0 2.9 collective-permute-done.3
  25.8 1.8 collective-permute-done.6
  27.9 1.5 collective-permute-start.4
  29.5 1.5 collective-permute-start.1
  32.7 5.0 %collective-permute-done.1 = bf16[2,96,768]{2,1,0:T(8,128)(2,1)S(1)} collective-permute-done((bf16[2,96,768]{2,1,0:T(8,128)(2,1)S(1)}, bf16[2,96,768]{2,1,0:T(8,128)(2,1)S(1)}, u32[]{:S(2)}, u32[]{:S(2)}) %collective-permute-start.1) | collective-permute-done | bytes 294944 | tf_op jit(solution)/shard_map/ppermute | solution.py:89
  40.5 11.0 %collective-permute-done.2 = bf16[4,96,768]{2,1,0:T(8,128)(2,1)S(1)} collective-permute-done((bf16[4,96,768]{2,1,0:T(8,128)(2,1)S(1)}, bf16[4,96,768]{2,1,0:T(8,128)(2,1)S(1)}, u32[]{:S(2)}, u32[]{:S(2)}) %collective-permute-start.2) | collective-permute-done | bytes 589856 | tf_op jit(solution)/shard_map/ppermute | solution.py:89
  55.7 1.5 collective-permute-start.12
  59.3 3.4 %reshape.399.rows_ref = bf16[954,768]{1,0:T(8,128)(2,1)S(1)} reshape(bf16[732672]{0:T(1024)(128)(2,1)} %pad.32) | data formatting | bytes 2930688 | tf_op jit(solution)/shard_map/reshape | solution.py:1127
  62.7 1.7 shard_map.189
  67.3 13.4 %collective-permute-done.15.refs_14_ = bf16[8,96,768]{2,1,0:T(8,128)(2,1)} collective-permute-done((bf16[8,96,768]{2,1,0:T(8,128)(2,1)}, bf16[8,96,768]{2,1,0:T(8,128)(2,1)}, u32[]{:S(2)}, u32[]{:S(2)}) %collective-permute-start.15) | collective-permute-done | bytes 1179680 | tf_op jit(solution)/shard_map/ppermute | solution.py:89
  83.8 1.7 collective-permute-done.17.refs_16_
  85.5 1.7 collective-permute-done.14.refs_12_
  87.2 1.7 collective-permute-done.11.refs_8_
  88.9 13.8 %shard_map.190 = (bf16[80,768]{1,0:T(8,128)(2,1)}, bf16[9216,768]{1,0:T(8,128)(2,1)}, bf16[256,2304]{1,0:T(8,128)(2,1)}, bf16[256,768]{1,0:T(8,128)(2,1)}, f32[2...) custom-call(s32[1]{0:T(128)} %bitcast.4.refs_0_, s32[2]{0:T(128)} %refs_0_.1, ...), custom_call_target="tpu_custom_call" | custom-call | flops 3623878656 | bytes 50331648 | tf_op jit(solution)/shard_map/pallas_call | solution.py:534
  103.6 3.4 %collective-permute-start.30 = (bf16[1,80,256]{2,1,0:T(8,128)(2,1)S(1)}, bf16[1,80,256]{2,1,0:T(8,128)(2,1)S(1)}, u32[]{:S(2)}, u32[]{:S(2)}) collective-permute-start(bf16[1,80,256]{2,1,0:T(8,128)(2,1)S(1)} %get-tuple-element.140), channel_id=1, source_target_pairs={{0,16},{16,0},{1,17},{17,1},{2,18},{18,2},{3,19},{19,3},{4,20},{20... | collective-permute-start | bytes 122888 | tf_op jit(solution)/shard_map/ppermute | solution.py:89
  107.1 2.8 collective-permute-start.18
  110.0 3.9 %collective-permute-done.18 = bf16[1,80,256]{2,1,0:T(8,128)(2,1)S(1)} collective-permute-done((bf16[1,80,256]{2,1,0:T(8,128)(2,1)S(1)}, bf16[1,80,256]{2,1,0:T(8,128)(2,1)S(1)}, u32[]{:S(2)}, u32[]{:S(2)}) %collective-permute-start.18) | collective-permute-done | bytes 40992 | tf_op jit(solution)/shard_map/ppermute | solution.py:89
  113.9 1.6 collective-permute-start.19
  116.0 2.4 collective-permute-done.19
  119.0 1.5 collective-permute-done.25
  121.1 2.7 collective-permute-done.20
  124.2 1.7 collective-permute-done.26
  126.1 1.9 collective-permute-start.33
  128.6 5.6 %collective-permute-done.21.refs_4_ = bf16[8,80,256]{2,1,0:T(8,128)(2,1)S(1)} collective-permute-done((bf16[8,80,256]{2,1,0:T(8,128)(2,1)S(1)}, bf16[8,80,256]{2,1,0:T(8,128)(2,1)S(1)}, u32[]{:S(2)}, u32[]{:S(2)}) %collective-permute-start.21) | collective-permute-done | bytes 327712 | tf_op jit(solution)/shard_map/ppermute | solution.py:89
  137.5 9.5 %shard_map.191 = (bf16[2048,768]{1,0:T(8,128)(2,1)}, bf16[32,16,768]{2,1,0:T(8,128)(2,1)}, f32[2048,1024]{1,0:T(8,128)}, f32[32,8,512]{2,1,0:T(8,128)}) custom-call(s32[1]{0:T(128)} %bitcast.4.refs_0_, s32[1]{0:T(128)} %bitcast.3.shift_ref.refs_1_, bf16[1024,768]{1,0:T(8,128)(2,1)} %copy-done.7, bf16[8,80,256]{2,1,0:T(8,128)(2,1)} %copy-done.19, ...), custom_call_target="tpu_custom_call" | custom-call | flops 3221225472 | bytes 16777216 | tf_op jit(solution)/shard_map/pallas_call | solution.py:748
  147.0 3.3 %all-to-all-start.1 = ((f32[32,8,512]{2,1,0:T(8,128)}), f32[32,8,512]{2,1,0:T(8,128)S(1)}, u32[]{:S(2)}, u32[]{:S(2)}) async-start(f32[32,8,512]{2,1,0:T(8,128)} %get-tuple-element.85), calls=%async_computation.1 | async-start | bytes 1048576 | tf_op jit(solution)/shard_map/all_to_all | solution.py:1219
  150.3 1.4 copy-done.9
  151.7 11.3 %shard_map.192 = (bf16[2048,768]{1,0:T(8,128)(2,1)}, bf16[2048,768]{1,0:T(8,128)(2,1)}, f32[2048,1]{1,0:T(8,128)S(1)}) custom-call(f32[2048,1024]{1,0:T(8,128)} %get-tuple-element.122.expo_ref, f32[2048,2]{1,0:T(8,128)S(1)} %get-tuple-element.87.column_ref.refs_6_, bf16[1024,768]{1,0:T(8,128)(2,1)S(1)} %copy-done.9), custom_call_target="tpu_custom_call" | custom-call | flops 25769803776 | bytes 67108864 | tf_op jit(solution)/shard_map/pallas_call | solution.py:794
  166.6 7.0 %shard_map.193 = (f32[2048,1]{1,0:T(8,128)S(1)}, bf16[16,64,256]{2,1,0:T(8,128)(2,1)S(1)}, bf16[8,64,256]{2,1,0:T(8,128)(2,1)S(1)}, bf16[8,64,256]{2,1,0:T(8,128...) custom-call(s32[1]{0:T(128)} %bitcast.4.refs_0_, ...), custom_call_target="tpu_custom_call" | custom-call | flops 12582912 | bytes 10485760 | tf_op jit(solution)/shard_map/pallas_call | solution.py:854
  179.2 1.5 collective-permute-start.50
  180.7 4.2 %collective-permute-done.38 = bf16[8,64,256]{2,1,0:T(8,128)(2,1)S(1)} collective-permute-done((bf16[8,64,256]{2,1,0:T(8,128)(2,1)S(1)}, bf16[8,64,256]{2,1,0:T(8,128)(2,1)S(1)}, u32[]{:S(2)}, u32[]{:S(2)}) %collective-permute-start.38) | collective-permute-done | bytes 262176 | tf_op jit(solution)/shard_map/ppermute | solution.py:89
  187.6 1.5 collective-permute-start.51
  193.4 1.9 collective-permute-start.52
  195.3 2.5 collective-permute-start.41
  198.4 2.5 collective-permute-start.53
  201.3 1.7 collective-permute-done.47
  204.2 23.1 %shard_map.194 = (f32[256,768]{1,0:T(8,128)}, f32[12,768]{1,0:T(8,128)}, bf16[16,96,768]{2,1,0:T(8,128)(2,1)}, bf16[8,96,768]{2,1,0:T(8,128)(2,1)}, bf16[8,96,76...) custom-call(s32[2]{0:T(128)} %refs_0_.1, ...), custom_call_target="tpu_custom_call" | custom-call | flops 7247757312 | bytes 50331648 | tf_op jit(solution)/shard_map/pallas_call | solution.py:572
  228.4 2.0 collective-permute-done.55
  230.5 2.7 add_convert_fusion.2
  235.1 2.7 add_convert_fusion.1
  241.6 3.4 %copy-done.5 = f32[2048,1024]{1,0:T(8,128)S(1)} copy-done((f32[2048,1024]{1,0:T(8,128)S(1)}, f32[2048,1024]{1,0:T(8,128)}, u32[]{:S(2)}) %copy-start.5) | copy-done | bytes 8388632
  245.0 11.7 %shard_map.195 = f32[954,768]{1,0:T(8,128)S(1)} custom-call(s32[1]{0:T(128)} %bitcast.3.shift_ref.refs_1_, f32[2048,1024]{1,0:T(8,128)S(1)} %copy-done.5, f32[2048,1]{1,0:T(8,128)S(1)} %get-tuple-element.123.scale_ref, f32[2048,2]{1,0:T(8,128)S(1)} %copy-done.1, bf16[2048,768]{1,0:T(8,128)(2,1)S(1)} %copy-done.6), custom_call_target="tpu_custom_call" | custom-call | flops 25769803776 | bytes 67108864 | tf_op jit(solution)/shard_map/pallas_call | solution.py:915
  257.4 4.7 %all-to-all-start.2 = ((f32[32,1,288]{2,1,0:T(1,128)}), f32[32,1,288]{2,1,0:T(1,128)}, u32[]{:S(2)}, u32[]{:S(2)}) async-start(f32[32,1,288]{2,1,0:T(1,128)} %reshape.410), calls=%async_computation.2 | async-start | bytes 98304 | tf_op jit(solution)/shard_map/all_to_all | solution.py:1167
  262.1 2.4 add_convert_fusion.5
  264.6 1.9 collective-permute-start.57
  266.5 2.4 add_convert_fusion.4
  268.9 1.5 collective-permute-start.63
  270.4 2.4 add_convert_fusion.3
  272.8 1.5 collective-permute-start.69
  275.2 5.9 %collective-permute-done.57 = bf16[4,96,768]{2,1,0:T(8,128)(2,1)S(1)} collective-permute-done((bf16[4,96,768]{2,1,0:T(8,128)(2,1)}, bf16[4,96,768]{2,1,0:T(8,128)(2,1)S(1)}, u32[]{:S(2)}, u32[]{:S(2)}) %collective-permute-start.57) | collective-permute-done | bytes 589856 | tf_op jit(solution)/shard_map/ppermute | solution.py:89
  286.3 3.1 collective-permute-done.69
  291.4 2.8 collective-permute-done.58
  294.2 1.9 add_convert_fusion.14
  296.1 2.4 collective-permute-start.59
  298.6 2.0 add_convert_fusion.13
  301.7 1.9 add_convert_fusion.12
  303.6 2.4 collective-permute-start.71
  306.1 1.8 reshape.405
  307.8 9.0 %fusion.5 = (f32[732528]{0:T(1024)}, f32[732528]{0:T(1024)}) fusion(f32[732528]{0:T(1024)} %param.21, f32[732528]{0:T(1024)} %param.27, f32[732528]{0:T(1024)} %param.26, f32[732672]{0:T(1024)} %reshape.405), kind=kLoop, calls=%fused_computation.6 | loop fusion | flops 9522864 | bytes 17580672 | tf_op jit(solution)/shard_map/add | solution.py:85
  322.9 3.0 fusion.13
  (288 shorter events, 70.8 us)
Async XLA Ops:
  2.2 18.8 %collective-permute-start = (bf16[1,96,768]{2,1,0:T(8,128)(2,1)S(1)}, bf16[1,96,768]{2,1,0:T(8,128)(2,1)}, u32[]{:S(2)}, u32[]{:S(2)}) collective-permute-start(bf16[1,96,768]{2,1,0:T(8,128)(2,1)S(1)} %unstack.16), channel_id=1, source_target_pairs={{0,16},{16,0},{1,17},{17,1},{2,18},{18,2},{3,19},{19,3},{4,20},{20... | collective-permute-start | bytes 442376 | tf_op jit(solution)/shard_map/ppermute | solution.py:89
  6.5 18.4 %collective-permute-start.3 = (bf16[1,96,768]{2,1,0:T(8,128)(2,1)S(1)}, bf16[1,96,768]{2,1,0:T(8,128)(2,1)}, u32[]{:S(2)}, u32[]{:S(2)}) collective-permute-start(bf16[1,96,768]{2,1,0:T(8,128)(2,1)S(1)} %unstack.18), channel_id=1, source_target_pairs={{0,16},{16,0},{1,17},{17,1},{2,18},{18,2},{3,19},{19,3},{4,20},{20... | collective-permute-start | bytes 442376 | tf_op jit(solution)/shard_map/ppermute | solution.py:89
  6.7 20.9 %collective-permute-start.6 = (bf16[1,96,768]{2,1,0:T(8,128)(2,1)S(1)}, bf16[1,96,768]{2,1,0:T(8,128)(2,1)S(1)}, u32[]{:S(2)}, u32[]{:S(2)}) collective-permute-start(bf16[1,96,768]{2,1,0:T(8,128)(2,1)S(1)} %unstack.20), channel_id=1, source_target_pairs={{0,16},{16,0},{1,17},{17,1},{2,18},{18,2},{3,19},{19,3},{4,20},{20... | collective-permute-start | bytes 442376 | tf_op jit(solution)/shard_map/ppermute | solution.py:89
  11.7 19.2 %all-to-all-start = ((bf16[32,2,768]{2,1,0:T(2,128)(2,1)}), bf16[32,2,768]{2,1,0:T(2,128)(2,1)S(1)}, u32[]{:S(2)}, u32[]{:S(2)}) async-start(bf16[32,2,768]{2,1,0:T(2,128)(2,1)} %pad_maximum_fusion.16), calls=%async_computation | async-start | bytes 196608 | tf_op jit(solution)/shard_map/all_to_all | solution.py:1114
  27.6 11.5 %collective-permute-start.7 = (bf16[2,96,768]{2,1,0:T(8,128)(2,1)S(1)}, bf16[2,96,768]{2,1,0:T(8,128)(2,1)S(1)}, u32[]{:S(2)}, u32[]{:S(2)}) collective-permute-start(bf16[2,96,768]{2,1,0:T(8,128)(2,1)S(1)} %pad_maximum_fusion.12), channel_id=1, source_target_pairs={{0,8},{8,0},{1,9},{9,1},{2,10},{10,2},{3,11},{11,3},{4,12},{12,4},... | collective-permute-start | bytes 884744 | tf_op jit(solution)/shard_map/ppermute | solution.py:89
  27.9 10.4 %collective-permute-start.4 = (bf16[2,96,768]{2,1,0:T(8,128)(2,1)S(1)}, bf16[2,96,768]{2,1,0:T(8,128)(2,1)S(1)}, u32[]{:S(2)}, u32[]{:S(2)}) collective-permute-start(bf16[2,96,768]{2,1,0:T(8,128)(2,1)S(1)} %pad_maximum_fusion.11), channel_id=1, source_target_pairs={{0,4},{4,0},{1,5},{5,1},{2,6},{6,2},{3,7},{7,3},{8,12},{12,8},{9,1... | collective-permute-start | bytes 884744 | tf_op jit(solution)/shard_map/ppermute | solution.py:89
  29.5 8.3 %collective-permute-start.1 = (bf16[2,96,768]{2,1,0:T(8,128)(2,1)S(1)}, bf16[2,96,768]{2,1,0:T(8,128)(2,1)S(1)}, u32[]{:S(2)}, u32[]{:S(2)}) collective-permute-start(bf16[2,96,768]{2,1,0:T(8,128)(2,1)S(1)} %pad_maximum_fusion.10), channel_id=1, source_target_pairs={{0,1},{1,0},{2,3},{3,2},{4,5},{5,4},{6,7},{7,6},{8,9},{9,8},{10,11... | collective-permute-start | bytes 884744 | tf_op jit(solution)/shard_map/ppermute | solution.py:89
  37.8 13.7 %collective-permute-start.2 = (bf16[4,96,768]{2,1,0:T(8,128)(2,1)S(1)}, bf16[4,96,768]{2,1,0:T(8,128)(2,1)S(1)}, u32[]{:S(2)}, u32[]{:S(2)}) collective-permute-start(bf16[4,96,768]{2,1,0:T(8,128)(2,1)S(1)} %pad_maximum_fusion.4), channel_id=1, source_target_pairs={{0,4},{4,0},{1,5},{5,1},{2,6},{6,2},{3,7},{7,3},{8,12},{12,8},{9,1... | collective-permute-start | bytes 1769480 | tf_op jit(solution)/shard_map/ppermute | solution.py:89
  38.4 14.2 %collective-permute-start.5 = (bf16[4,96,768]{2,1,0:T(8,128)(2,1)S(1)}, bf16[4,96,768]{2,1,0:T(8,128)(2,1)S(1)}, u32[]{:S(2)}, u32[]{:S(2)}) collective-permute-start(bf16[4,96,768]{2,1,0:T(8,128)(2,1)S(1)} %pad_maximum_fusion.5), channel_id=1, source_target_pairs={{0,8},{8,0},{1,9},{9,1},{2,10},{10,2},{3,11},{11,3},{4,12},{12,4},... | collective-permute-start | bytes 1769480 | tf_op jit(solution)/shard_map/ppermute | solution.py:89
  39.2 14.6 %collective-permute-start.8 = (bf16[4,96,768]{2,1,0:T(8,128)(2,1)S(1)}, bf16[4,96,768]{2,1,0:T(8,128)(2,1)S(1)}, u32[]{:S(2)}, u32[]{:S(2)}) collective-permute-start(bf16[4,96,768]{2,1,0:T(8,128)(2,1)S(1)} %pad_maximum_fusion.6), channel_id=1, source_target_pairs={{0,1},{1,0},{2,3},{3,2},{4,5},{5,4},{6,7},{7,6},{8,9},{9,8},{10,11... | collective-permute-start | bytes 1769480 | tf_op jit(solution)/shard_map/ppermute | solution.py:89
  54.9 25.7 %collective-permute-start.15 = (bf16[8,96,768]{2,1,0:T(8,128)(2,1)}, bf16[8,96,768]{2,1,0:T(8,128)(2,1)}, u32[]{:S(2)}, u32[]{:S(2)}) collective-permute-start(bf16[8,96,768]{2,1,0:T(8,128)(2,1)} %pad_maximum_fusion.2.refs_13_), channel_id=1, source_target_pairs={{0,4},{4,0},{1,5},{5,1},{2,6},{6,2},{3,7},{7,3},{8,12},{12,8},{9,1... | collective-permute-start | bytes 3538952 | tf_op jit(solution)/shard_map/ppermute | solution.py:89
  55.7 25.2 %collective-permute-start.12 = (bf16[8,96,768]{2,1,0:T(8,128)(2,1)}, bf16[8,96,768]{2,1,0:T(8,128)(2,1)}, u32[]{:S(2)}, u32[]{:S(2)}) collective-permute-start(bf16[8,96,768]{2,1,0:T(8,128)(2,1)} %pad_maximum_fusion.1.refs_9_), channel_id=1, source_target_pairs={{0,1},{1,0},{2,3},{3,2},{4,5},{5,4},{6,7},{7,6},{8,9},{9,8},{10,11... | collective-permute-start | bytes 3538952 | tf_op jit(solution)/shard_map/ppermute | solution.py:89
  57.2 24.9 %collective-permute-start.9 = (bf16[8,96,768]{2,1,0:T(8,128)(2,1)}, bf16[8,96,768]{2,1,0:T(8,128)(2,1)}, u32[]{:S(2)}, u32[]{:S(2)}) collective-permute-start(bf16[8,96,768]{2,1,0:T(8,128)(2,1)} %pad_maximum_fusion.refs_5_), channel_id=1, source_target_pairs={{0,8},{8,0},{1,9},{9,1},{2,10},{10,2},{3,11},{11,3},{4,12},{12,4},... | collective-permute-start | bytes 3538952 | tf_op jit(solution)/shard_map/ppermute | solution.py:89
  66.8 15.3 %collective-permute-start.10 = (bf16[8,96,768]{2,1,0:T(8,128)(2,1)}, bf16[8,96,768]{2,1,0:T(8,128)(2,1)S(1)}, u32[]{:S(2)}, u32[]{:S(2)}) collective-permute-start(bf16[8,96,768]{2,1,0:T(8,128)(2,1)} %pad_maximum_fusion.refs_5_), channel_id=1, source_target_pairs={{0,2},{2,0},{1,3},{3,1},{4,6},{6,4},{5,7},{7,5},{8,10},{10,8},{9,1... | collective-permute-start | bytes 3538952 | tf_op jit(solution)/shard_map/ppermute | solution.py:89
  66.8 16.8 %collective-permute-start.13 = (bf16[8,96,768]{2,1,0:T(8,128)(2,1)}, bf16[8,96,768]{2,1,0:T(8,128)(2,1)S(1)}, u32[]{:S(2)}, u32[]{:S(2)}) collective-permute-start(bf16[8,96,768]{2,1,0:T(8,128)(2,1)} %pad_maximum_fusion.1.refs_9_), channel_id=1, source_target_pairs={{0,2},{2,0},{1,3},{3,1},{4,6},{6,4},{5,7},{7,5},{8,10},{10,8},{9,1... | collective-permute-start | bytes 3538952 | tf_op jit(solution)/shard_map/ppermute | solution.py:89
  80.9 4.7 %collective-permute-start.17 = (bf16[8,96,768]{2,1,0:T(8,128)(2,1)}, bf16[8,96,768]{2,1,0:T(8,128)(2,1)}, u32[]{:S(2)}, u32[]{:S(2)}) collective-permute-start(bf16[8,96,768]{2,1,0:T(8,128)(2,1)} %collective-permute-done.15.refs_14_), channel_id=1, source_target_pairs={{0,2},{2,0},{1,3},{3,1},{4,6},{6,4},{5,7},{7,5},{8,10},{10,8},{9,1... | collective-permute-start | bytes 3538952 | tf_op jit(solution)/shard_map/ppermute | solution.py:89
  82.1 5.1 %collective-permute-start.14 = (bf16[8,96,768]{2,1,0:T(8,128)(2,1)}, bf16[8,96,768]{2,1,0:T(8,128)(2,1)}, u32[]{:S(2)}, u32[]{:S(2)}) collective-permute-start(bf16[8,96,768]{2,1,0:T(8,128)(2,1)} %collective-permute-done.12.refs_10_), channel_id=1, source_target_pairs={{0,2},{2,0},{1,3},{3,1},{4,6},{6,4},{5,7},{7,5},{8,10},{10,8},{9,1... | collective-permute-start | bytes 3538952 | tf_op jit(solution)/shard_map/ppermute | solution.py:89
  82.1 6.8 %collective-permute-start.11 = (bf16[8,96,768]{2,1,0:T(8,128)(2,1)}, bf16[8,96,768]{2,1,0:T(8,128)(2,1)}, u32[]{:S(2)}, u32[]{:S(2)}) collective-permute-start(bf16[8,96,768]{2,1,0:T(8,128)(2,1)} %collective-permute-done.9.refs_6_), channel_id=1, source_target_pairs={{0,2},{2,0},{1,3},{3,1},{4,6},{6,4},{5,7},{7,5},{8,10},{10,8},{9,1... | collective-permute-start | bytes 3538952 | tf_op jit(solution)/shard_map/ppermute | solution.py:89
  103.6 6.4 %collective-permute-start.30 = (bf16[1,80,256]{2,1,0:T(8,128)(2,1)S(1)}, bf16[1,80,256]{2,1,0:T(8,128)(2,1)S(1)}, u32[]{:S(2)}, u32[]{:S(2)}) collective-permute-start(bf16[1,80,256]{2,1,0:T(8,128)(2,1)S(1)} %get-tuple-element.140), channel_id=1, source_target_pairs={{0,16},{16,0},{1,17},{17,1},{2,18},{18,2},{3,19},{19,3},{4,20},{20... | collective-permute-start | bytes 122888 | tf_op jit(solution)/shard_map/ppermute | solution.py:89
  107.0 8.4 %collective-permute-start.24 = (bf16[1,80,256]{2,1,0:T(8,128)(2,1)S(1)}, bf16[1,80,256]{2,1,0:T(8,128)(2,1)S(1)}, u32[]{:S(2)}, u32[]{:S(2)}) collective-permute-start(bf16[1,80,256]{2,1,0:T(8,128)(2,1)S(1)} %get-tuple-element.141), channel_id=1, source_target_pairs={{0,16},{16,0},{1,17},{17,1},{2,18},{18,2},{3,19},{19,3},{4,20},{20... | collective-permute-start | bytes 122888 | tf_op jit(solution)/shard_map/ppermute | solution.py:89
  107.1 6.8 %collective-permute-start.18 = (bf16[1,80,256]{2,1,0:T(8,128)(2,1)S(1)}, bf16[1,80,256]{2,1,0:T(8,128)(2,1)S(1)}, u32[]{:S(2)}, u32[]{:S(2)}) collective-permute-start(bf16[1,80,256]{2,1,0:T(8,128)(2,1)S(1)} %get-tuple-element.142), channel_id=1, source_target_pairs={{0,16},{16,0},{1,17},{17,1},{2,18},{18,2},{3,19},{19,3},{4,20},{20... | collective-permute-start | bytes 122888 | tf_op jit(solution)/shard_map/ppermute | solution.py:89
  115.5 5.0 %collective-permute-start.25 = (bf16[2,80,256]{2,1,0:T(8,128)(2,1)S(1)}, bf16[2,80,256]{2,1,0:T(8,128)(2,1)S(1)}, u32[]{:S(2)}, u32[]{:S(2)}) collective-permute-start(bf16[2,80,256]{2,1,0:T(8,128)(2,1)S(1)} %pad_maximum_fusion.18), channel_id=1, source_target_pairs={{0,4},{4,0},{1,5},{5,1},{2,6},{6,2},{3,7},{7,3},{8,12},{12,8},{9,1... | collective-permute-start | bytes 245768 | tf_op jit(solution)/shard_map/ppermute | solution.py:89
  116.0 4.6 %collective-permute-start.31 = (bf16[2,80,256]{2,1,0:T(8,128)(2,1)S(1)}, bf16[2,80,256]{2,1,0:T(8,128)(2,1)S(1)}, u32[]{:S(2)}, u32[]{:S(2)}) collective-permute-start(bf16[2,80,256]{2,1,0:T(8,128)(2,1)S(1)} %pad_maximum_fusion.19), channel_id=1, source_target_pairs={{0,8},{8,0},{1,9},{9,1},{2,10},{10,2},{3,11},{11,3},{4,12},{12,4},... | collective-permute-start | bytes 245768 | tf_op jit(solution)/shard_map/ppermute | solution.py:89
  118.4 5.4 %collective-permute-start.20 = (bf16[4,80,256]{2,1,0:T(8,128)(2,1)S(1)}, bf16[4,80,256]{2,1,0:T(8,128)(2,1)S(1)}, u32[]{:S(2)}, u32[]{:S(2)}) collective-permute-start(bf16[4,80,256]{2,1,0:T(8,128)(2,1)S(1)} %pad_maximum_fusion.13), channel_id=1, source_target_pairs={{0,4},{4,0},{1,5},{5,1},{2,6},{6,2},{3,7},{7,3},{8,12},{12,8},{9,1... | collective-permute-start | bytes 491528 | tf_op jit(solution)/shard_map/ppermute | solution.py:89
  120.5 5.4 %collective-permute-start.26 = (bf16[4,80,256]{2,1,0:T(8,128)(2,1)S(1)}, bf16[4,80,256]{2,1,0:T(8,128)(2,1)S(1)}, u32[]{:S(2)}, u32[]{:S(2)}) collective-permute-start(bf16[4,80,256]{2,1,0:T(8,128)(2,1)S(1)} %pad_maximum_fusion.14), channel_id=1, source_target_pairs={{0,8},{8,0},{1,9},{9,1},{2,10},{10,2},{3,11},{11,3},{4,12},{12,4},... | collective-permute-start | bytes 491528 | tf_op jit(solution)/shard_map/ppermute | solution.py:89
  120.7 5.4 %collective-permute-start.32 = (bf16[4,80,256]{2,1,0:T(8,128)(2,1)S(1)}, bf16[4,80,256]{2,1,0:T(8,128)(2,1)S(1)}, u32[]{:S(2)}, u32[]{:S(2)}) collective-permute-start(bf16[4,80,256]{2,1,0:T(8,128)(2,1)S(1)} %pad_maximum_fusion.15), channel_id=1, source_target_pairs={{0,1},{1,0},{2,3},{3,2},{4,5},{5,4},{6,7},{7,6},{8,9},{9,8},{10,11... | collective-permute-start | bytes 491528 | tf_op jit(solution)/shard_map/ppermute | solution.py:89
  124.1 10.1 %collective-permute-start.21 = (bf16[8,80,256]{2,1,0:T(8,128)(2,1)S(1)}, bf16[8,80,256]{2,1,0:T(8,128)(2,1)S(1)}, u32[]{:S(2)}, u32[]{:S(2)}) collective-permute-start(bf16[8,80,256]{2,1,0:T(8,128)(2,1)S(1)} %pad_maximum_fusion.7.refs_3_), channel_id=1, source_target_pairs={{0,8},{8,0},{1,9},{9,1},{2,10},{10,2},{3,11},{11,3},{4,12},{12,4},... | collective-permute-start | bytes 983048 | tf_op jit(solution)/shard_map/ppermute | solution.py:89
  126.0 8.4 %collective-permute-start.27 = (bf16[8,80,256]{2,1,0:T(8,128)(2,1)S(1)}, bf16[8,80,256]{2,1,0:T(8,128)(2,1)S(1)}, u32[]{:S(2)}, u32[]{:S(2)}) collective-permute-start(bf16[8,80,256]{2,1,0:T(8,128)(2,1)S(1)} %pad_maximum_fusion.8.refs_7_), channel_id=1, source_target_pairs={{0,1},{1,0},{2,3},{3,2},{4,5},{5,4},{6,7},{7,6},{8,9},{9,8},{10,11... | collective-permute-start | bytes 983048 | tf_op jit(solution)/shard_map/ppermute | solution.py:89
  126.1 9.5 %collective-permute-start.33 = (bf16[8,80,256]{2,1,0:T(8,128)(2,1)S(1)}, bf16[8,80,256]{2,1,0:T(8,128)(2,1)S(1)}, u32[]{:S(2)}, u32[]{:S(2)}) collective-permute-start(bf16[8,80,256]{2,1,0:T(8,128)(2,1)S(1)} %pad_maximum_fusion.9.refs_11_), channel_id=1, source_target_pairs={{0,4},{4,0},{1,5},{5,1},{2,6},{6,2},{3,7},{7,3},{8,12},{12,8},{9,1... | collective-permute-start | bytes 983048 | tf_op jit(solution)/shard_map/ppermute | solution.py:89
  128.0 8.7 %collective-permute-start.28 = (bf16[8,80,256]{2,1,0:T(8,128)(2,1)S(1)}, bf16[8,80,256]{2,1,0:T(8,128)(2,1)}, u32[]{:S(2)}, u32[]{:S(2)}) collective-permute-start(bf16[8,80,256]{2,1,0:T(8,128)(2,1)S(1)} %pad_maximum_fusion.8.refs_7_), channel_id=1, source_target_pairs={{0,2},{2,0},{1,3},{3,1},{4,6},{6,4},{5,7},{7,5},{8,10},{10,8},{9,1... | collective-permute-start | bytes 983048 | tf_op jit(solution)/shard_map/ppermute | solution.py:89
  128.1 8.6 %collective-permute-start.34 = (bf16[8,80,256]{2,1,0:T(8,128)(2,1)S(1)}, bf16[8,80,256]{2,1,0:T(8,128)(2,1)}, u32[]{:S(2)}, u32[]{:S(2)}) collective-permute-start(bf16[8,80,256]{2,1,0:T(8,128)(2,1)S(1)} %pad_maximum_fusion.9.refs_11_), channel_id=1, source_target_pairs={{0,2},{2,0},{1,3},{3,1},{4,6},{6,4},{5,7},{7,5},{8,10},{10,8},{9,1... | collective-permute-start | bytes 983048 | tf_op jit(solution)/shard_map/ppermute | solution.py:89
  147.0 18.4 %all-to-all-start.1 = ((f32[32,8,512]{2,1,0:T(8,128)}), f32[32,8,512]{2,1,0:T(8,128)S(1)}, u32[]{:S(2)}, u32[]{:S(2)}) async-start(f32[32,8,512]{2,1,0:T(8,128)} %get-tuple-element.85), calls=%async_computation.1 | async-start | bytes 1048576 | tf_op jit(solution)/shard_map/all_to_all | solution.py:1219
  175.5 10.4 %collective-permute-start.42 = (bf16[8,64,256]{2,1,0:T(8,128)(2,1)S(1)}, bf16[8,64,256]{2,1,0:T(8,128)(2,1)S(1)}, u32[]{:S(2)}, u32[]{:S(2)}) collective-permute-start(bf16[8,64,256]{2,1,0:T(8,128)(2,1)S(1)} %get-tuple-element.96), channel_id=1, source_target_pairs={{0,2},{2,0},{1,3},{3,1},{4,6},{6,4},{5,7},{7,5},{8,10},{10,8},{9,1... | collective-permute-start | bytes 786440 | tf_op jit(solution)/shard_map/ppermute | solution.py:89
  175.6 12.0 %collective-permute-start.48 = (bf16[8,64,256]{2,1,0:T(8,128)(2,1)S(1)}, bf16[8,64,256]{2,1,0:T(8,128)(2,1)S(1)}, u32[]{:S(2)}, u32[]{:S(2)}) collective-permute-start(bf16[8,64,256]{2,1,0:T(8,128)(2,1)S(1)} %get-tuple-element.99), channel_id=1, source_target_pairs={{0,2},{2,0},{1,3},{3,1},{4,6},{6,4},{5,7},{7,5},{8,10},{10,8},{9,1... | collective-permute-start | bytes 786440 | tf_op jit(solution)/shard_map/ppermute | solution.py:89
  176.3 8.7 %collective-permute-start.38 = (bf16[8,64,256]{2,1,0:T(8,128)(2,1)S(1)}, bf16[8,64,256]{2,1,0:T(8,128)(2,1)S(1)}, u32[]{:S(2)}, u32[]{:S(2)}) collective-permute-start(bf16[8,64,256]{2,1,0:T(8,128)(2,1)S(1)} %add_convert_fusion.11), channel_id=1, source_target_pairs={{0,8},{8,0},{1,9},{9,1},{2,10},{10,2},{3,11},{11,3},{4,12},{12,4},... | collective-permute-start | bytes 786440 | tf_op jit(solution)/shard_map/ppermute | solution.py:89
  177.8 8.6 %collective-permute-start.44 = (bf16[8,64,256]{2,1,0:T(8,128)(2,1)S(1)}, bf16[8,64,256]{2,1,0:T(8,128)(2,1)S(1)}, u32[]{:S(2)}, u32[]{:S(2)}) collective-permute-start(bf16[8,64,256]{2,1,0:T(8,128)(2,1)S(1)} %add_convert_fusion.10), channel_id=1, source_target_pairs={{0,1},{1,0},{2,3},{3,2},{4,5},{5,4},{6,7},{7,6},{8,9},{9,8},{10,11... | collective-permute-start | bytes 786440 | tf_op jit(solution)/shard_map/ppermute | solution.py:89
  179.2 8.4 %collective-permute-start.50 = (bf16[8,64,256]{2,1,0:T(8,128)(2,1)S(1)}, bf16[8,64,256]{2,1,0:T(8,128)(2,1)S(1)}, u32[]{:S(2)}, u32[]{:S(2)}) collective-permute-start(bf16[8,64,256]{2,1,0:T(8,128)(2,1)S(1)} %add_convert_fusion.9), channel_id=1, source_target_pairs={{0,4},{4,0},{1,5},{5,1},{2,6},{6,2},{3,7},{7,3},{8,12},{12,8},{9,1... | collective-permute-start | bytes 786440 | tf_op jit(solution)/shard_map/ppermute | solution.py:89
  185.0 5.1 %collective-permute-start.39 = (bf16[4,64,256]{2,1,0:T(8,128)(2,1)S(1)}, bf16[4,64,256]{2,1,0:T(8,128)(2,1)S(1)}, u32[]{:S(2)}, u32[]{:S(2)}) collective-permute-start(bf16[4,64,256]{2,1,0:T(8,128)(2,1)S(1)} %add_convert_fusion.17), channel_id=1, source_target_pairs={{0,4},{4,0},{1,5},{5,1},{2,6},{6,2},{3,7},{7,3},{8,12},{12,8},{9,1... | collective-permute-start | bytes 393224 | tf_op jit(solution)/shard_map/ppermute | solution.py:89
  186.4 5.0 %collective-permute-start.45 = (bf16[4,64,256]{2,1,0:T(8,128)(2,1)S(1)}, bf16[4,64,256]{2,1,0:T(8,128)(2,1)S(1)}, u32[]{:S(2)}, u32[]{:S(2)}) collective-permute-start(bf16[4,64,256]{2,1,0:T(8,128)(2,1)S(1)} %add_convert_fusion.16), channel_id=1, source_target_pairs={{0,8},{8,0},{1,9},{9,1},{2,10},{10,2},{3,11},{11,3},{4,12},{12,4},... | collective-permute-start | bytes 393224 | tf_op jit(solution)/shard_map/ppermute | solution.py:89
  187.6 5.7 %collective-permute-start.51 = (bf16[4,64,256]{2,1,0:T(8,128)(2,1)S(1)}, bf16[4,64,256]{2,1,0:T(8,128)(2,1)S(1)}, u32[]{:S(2)}, u32[]{:S(2)}) collective-permute-start(bf16[4,64,256]{2,1,0:T(8,128)(2,1)S(1)} %add_convert_fusion.15), channel_id=1, source_target_pairs={{0,1},{1,0},{2,3},{3,2},{4,5},{5,4},{6,7},{7,6},{8,9},{9,8},{10,11... | collective-permute-start | bytes 393224 | tf_op jit(solution)/shard_map/ppermute | solution.py:89
  190.1 5.2 %collective-permute-start.40 = (bf16[2,64,256]{2,1,0:T(8,128)(2,1)S(1)}, bf16[2,64,256]{2,1,0:T(8,128)(2,1)S(1)}, u32[]{:S(2)}, u32[]{:S(2)}) collective-permute-start(bf16[2,64,256]{2,1,0:T(8,128)(2,1)S(1)} %add_convert_fusion.20), channel_id=1, source_target_pairs={{0,1},{1,0},{2,3},{3,2},{4,5},{5,4},{6,7},{7,6},{8,9},{9,8},{10,11... | collective-permute-start | bytes 196616 | tf_op jit(solution)/shard_map/ppermute | solution.py:89
  191.5 6.3 %collective-permute-start.46 = (bf16[2,64,256]{2,1,0:T(8,128)(2,1)S(1)}, bf16[2,64,256]{2,1,0:T(8,128)(2,1)S(1)}, u32[]{:S(2)}, u32[]{:S(2)}) collective-permute-start(bf16[2,64,256]{2,1,0:T(8,128)(2,1)S(1)} %add_convert_fusion.19), channel_id=1, source_target_pairs={{0,4},{4,0},{1,5},{5,1},{2,6},{6,2},{3,7},{7,3},{8,12},{12,8},{9,1... | collective-permute-start | bytes 196616 | tf_op jit(solution)/shard_map/ppermute | solution.py:89
  193.4 5.0 %collective-permute-start.52 = (bf16[2,64,256]{2,1,0:T(8,128)(2,1)S(1)}, bf16[2,64,256]{2,1,0:T(8,128)(2,1)S(1)}, u32[]{:S(2)}, u32[]{:S(2)}) collective-permute-start(bf16[2,64,256]{2,1,0:T(8,128)(2,1)S(1)} %add_convert_fusion.18), channel_id=1, source_target_pairs={{0,8},{8,0},{1,9},{9,1},{2,10},{10,2},{3,11},{11,3},{4,12},{12,4},... | collective-permute-start | bytes 196616 | tf_op jit(solution)/shard_map/ppermute | solution.py:89
  195.3 6.0 %collective-permute-start.41 = (bf16[1,64,256]{2,1,0:T(8,128)(2,1)S(1)}, bf16[1,64,256]{2,1,0:T(8,128)(2,1)S(1)}, u32[]{:S(2)}, u32[]{:S(2)}) collective-permute-start(bf16[1,64,256]{2,1,0:T(8,128)(2,1)S(1)} %add_convert_fusion.23), channel_id=1, source_target_pairs={{0,16},{16,0},{1,17},{17,1},{2,18},{18,2},{3,19},{19,3},{4,20},{20... | collective-permute-start | bytes 98312 | tf_op jit(solution)/shard_map/ppermute | solution.py:89
  197.8 5.2 %collective-permute-start.47 = (bf16[1,64,256]{2,1,0:T(8,128)(2,1)S(1)}, bf16[1,64,256]{2,1,0:T(8,128)(2,1)S(1)}, u32[]{:S(2)}, u32[]{:S(2)}) collective-permute-start(bf16[1,64,256]{2,1,0:T(8,128)(2,1)S(1)} %add_convert_fusion.22), channel_id=1, source_target_pairs={{0,16},{16,0},{1,17},{17,1},{2,18},{18,2},{3,19},{19,3},{4,20},{20... | collective-permute-start | bytes 98312 | tf_op jit(solution)/shard_map/ppermute | solution.py:89
  198.4 5.0 %collective-permute-start.53 = (bf16[1,64,256]{2,1,0:T(8,128)(2,1)S(1)}, bf16[1,64,256]{2,1,0:T(8,128)(2,1)S(1)}, u32[]{:S(2)}, u32[]{:S(2)}) collective-permute-start(bf16[1,64,256]{2,1,0:T(8,128)(2,1)S(1)} %add_convert_fusion.21), channel_id=1, source_target_pairs={{0,16},{16,0},{1,17},{17,1},{2,18},{18,2},{3,19},{19,3},{4,20},{20... | collective-permute-start | bytes 98312 | tf_op jit(solution)/shard_map/ppermute | solution.py:89
  227.3 6.4 %collective-permute-start.61 = (bf16[8,96,768]{2,1,0:T(8,128)(2,1)}, bf16[8,96,768]{2,1,0:T(8,128)(2,1)S(1)}, u32[]{:S(2)}, u32[]{:S(2)}) collective-permute-start(bf16[8,96,768]{2,1,0:T(8,128)(2,1)} %get-tuple-element.115), channel_id=1, source_target_pairs={{0,2},{2,0},{1,3},{3,1},{4,6},{6,4},{5,7},{7,5},{8,10},{10,8},{9,1... | collective-permute-start | bytes 3538952 | tf_op jit(solution)/shard_map/ppermute | solution.py:89
  227.8 10.0 %collective-permute-start.67 = (bf16[8,96,768]{2,1,0:T(8,128)(2,1)}, bf16[8,96,768]{2,1,0:T(8,128)(2,1)S(1)}, u32[]{:S(2)}, u32[]{:S(2)}) collective-permute-start(bf16[8,96,768]{2,1,0:T(8,128)(2,1)} %get-tuple-element.118), channel_id=1, source_target_pairs={{0,2},{2,0},{1,3},{3,1},{4,6},{6,4},{5,7},{7,5},{8,10},{10,8},{9,1... | collective-permute-start | bytes 3538952 | tf_op jit(solution)/shard_map/ppermute | solution.py:89
  227.9 12.3 %collective-permute-start.54 = (bf16[8,96,768]{2,1,0:T(8,128)(2,1)}, bf16[8,96,768]{2,1,0:T(8,128)(2,1)S(1)}, u32[]{:S(2)}, u32[]{:S(2)}) collective-permute-start(bf16[8,96,768]{2,1,0:T(8,128)(2,1)} %get-tuple-element.111), channel_id=1, source_target_pairs={{0,2},{2,0},{1,3},{3,1},{4,6},{6,4},{5,7},{7,5},{8,10},{10,8},{9,1... | collective-permute-start | bytes 3538952 | tf_op jit(solution)/shard_map/ppermute | solution.py:89
  228.3 38.1 %collective-permute-start.60 = (bf16[8,96,768]{2,1,0:T(8,128)(2,1)}, bf16[8,96,768]{2,1,0:T(8,128)(2,1)}, u32[]{:S(2)}, u32[]{:S(2)}) collective-permute-start(bf16[8,96,768]{2,1,0:T(8,128)(2,1)} %get-tuple-element.114), channel_id=1, source_target_pairs={{0,2},{2,0},{1,3},{3,1},{4,6},{6,4},{5,7},{7,5},{8,10},{10,8},{9,1... | collective-permute-start | bytes 3538952 | tf_op jit(solution)/shard_map/ppermute | solution.py:89
  230.4 40.0 %collective-permute-start.66 = (bf16[8,96,768]{2,1,0:T(8,128)(2,1)}, bf16[8,96,768]{2,1,0:T(8,128)(2,1)}, u32[]{:S(2)}, u32[]{:S(2)}) collective-permute-start(bf16[8,96,768]{2,1,0:T(8,128)(2,1)} %get-tuple-element.117), channel_id=1, source_target_pairs={{0,2},{2,0},{1,3},{3,1},{4,6},{6,4},{5,7},{7,5},{8,10},{10,8},{9,1... | collective-permute-start | bytes 3538952 | tf_op jit(solution)/shard_map/ppermute | solution.py:89
  233.7 28.4 %collective-permute-start.56 = (bf16[8,96,768]{2,1,0:T(8,128)(2,1)}, bf16[8,96,768]{2,1,0:T(8,128)(2,1)}, u32[]{:S(2)}, u32[]{:S(2)}) collective-permute-start(bf16[8,96,768]{2,1,0:T(8,128)(2,1)} %add_convert_fusion.2), channel_id=1, source_target_pairs={{0,8},{8,0},{1,9},{9,1},{2,10},{10,2},{3,11},{11,3},{4,12},{12,4},... | collective-permute-start | bytes 3538952 | tf_op jit(solution)/shard_map/ppermute | solution.py:89
  237.8 28.6 %collective-permute-start.62 = (bf16[8,96,768]{2,1,0:T(8,128)(2,1)}, bf16[8,96,768]{2,1,0:T(8,128)(2,1)}, u32[]{:S(2)}, u32[]{:S(2)}) collective-permute-start(bf16[8,96,768]{2,1,0:T(8,128)(2,1)} %add_convert_fusion.1), channel_id=1, source_target_pairs={{0,1},{1,0},{2,3},{3,2},{4,5},{5,4},{6,7},{7,6},{8,9},{9,8},{10,11... | collective-permute-start | bytes 3538952 | tf_op jit(solution)/shard_map/ppermute | solution.py:89
  240.2 30.2 %collective-permute-start.68 = (bf16[8,96,768]{2,1,0:T(8,128)(2,1)}, bf16[8,96,768]{2,1,0:T(8,128)(2,1)}, u32[]{:S(2)}, u32[]{:S(2)}) collective-permute-start(bf16[8,96,768]{2,1,0:T(8,128)(2,1)} %add_convert_fusion), channel_id=1, source_target_pairs={{0,4},{4,0},{1,5},{5,1},{2,6},{6,2},{3,7},{7,3},{8,12},{12,8},{9,1... | collective-permute-start | bytes 3538952 | tf_op jit(solution)/shard_map/ppermute | solution.py:89
  257.4 16.9 %all-to-all-start.2 = ((f32[32,1,288]{2,1,0:T(1,128)}), f32[32,1,288]{2,1,0:T(1,128)}, u32[]{:S(2)}, u32[]{:S(2)}) async-start(f32[32,1,288]{2,1,0:T(1,128)} %reshape.410), calls=%async_computation.2 | async-start | bytes 98304 | tf_op jit(solution)/shard_map/all_to_all | solution.py:1167
  264.6 16.5 %collective-permute-start.57 = (bf16[4,96,768]{2,1,0:T(8,128)(2,1)}, bf16[4,96,768]{2,1,0:T(8,128)(2,1)S(1)}, u32[]{:S(2)}, u32[]{:S(2)}) collective-permute-start(bf16[4,96,768]{2,1,0:T(8,128)(2,1)} %add_convert_fusion.5), channel_id=1, source_target_pairs={{0,4},{4,0},{1,5},{5,1},{2,6},{6,2},{3,7},{7,3},{8,12},{12,8},{9,1... | collective-permute-start | bytes 1769480 | tf_op jit(solution)/shard_map/ppermute | solution.py:89
  268.9 15.4 %collective-permute-start.63 = (bf16[4,96,768]{2,1,0:T(8,128)(2,1)}, bf16[4,96,768]{2,1,0:T(8,128)(2,1)}, u32[]{:S(2)}, u32[]{:S(2)}) collective-permute-start(bf16[4,96,768]{2,1,0:T(8,128)(2,1)} %add_convert_fusion.4), channel_id=1, source_target_pairs={{0,8},{8,0},{1,9},{9,1},{2,10},{10,2},{3,11},{11,3},{4,12},{12,4},... | collective-permute-start | bytes 1769480 | tf_op jit(solution)/shard_map/ppermute | solution.py:89
  272.8 16.6 %collective-permute-start.69 = (bf16[4,96,768]{2,1,0:T(8,128)(2,1)}, bf16[4,96,768]{2,1,0:T(8,128)(2,1)}, u32[]{:S(2)}, u32[]{:S(2)}) collective-permute-start(bf16[4,96,768]{2,1,0:T(8,128)(2,1)} %add_convert_fusion.3), channel_id=1, source_target_pairs={{0,1},{1,0},{2,3},{3,2},{4,5},{5,4},{6,7},{7,6},{8,9},{9,8},{10,11... | collective-permute-start | bytes 1769480 | tf_op jit(solution)/shard_map/ppermute | solution.py:89
  282.3 11.8 %collective-permute-start.58 = (bf16[2,96,768]{2,1,0:T(8,128)(2,1)S(1)}, bf16[2,96,768]{2,1,0:T(8,128)(2,1)S(1)}, u32[]{:S(2)}, u32[]{:S(2)}) collective-permute-start(bf16[2,96,768]{2,1,0:T(8,128)(2,1)S(1)} %add_convert_fusion.8), channel_id=1, source_target_pairs={{0,1},{1,0},{2,3},{3,2},{4,5},{5,4},{6,7},{7,6},{8,9},{9,8},{10,11... | collective-permute-start | bytes 884744 | tf_op jit(solution)/shard_map/ppermute | solution.py:89
  285.7 12.8 %collective-permute-start.64 = (bf16[2,96,768]{2,1,0:T(8,128)(2,1)S(1)}, bf16[2,96,768]{2,1,0:T(8,128)(2,1)S(1)}, u32[]{:S(2)}, u32[]{:S(2)}) collective-permute-start(bf16[2,96,768]{2,1,0:T(8,128)(2,1)S(1)} %add_convert_fusion.7), channel_id=1, source_target_pairs={{0,4},{4,0},{1,5},{5,1},{2,6},{6,2},{3,7},{7,3},{8,12},{12,8},{9,1... | collective-permute-start | bytes 884744 | tf_op jit(solution)/shard_map/ppermute | solution.py:89
  290.8 10.2 %collective-permute-start.70 = (bf16[2,96,768]{2,1,0:T(8,128)(2,1)S(1)}, bf16[2,96,768]{2,1,0:T(8,128)(2,1)S(1)}, u32[]{:S(2)}, u32[]{:S(2)}) collective-permute-start(bf16[2,96,768]{2,1,0:T(8,128)(2,1)S(1)} %add_convert_fusion.6), channel_id=1, source_target_pairs={{0,8},{8,0},{1,9},{9,1},{2,10},{10,2},{3,11},{11,3},{4,12},{12,4},... | collective-permute-start | bytes 884744 | tf_op jit(solution)/shard_map/ppermute | solution.py:89
  296.1 21.3 %collective-permute-start.59 = (bf16[1,96,768]{2,1,0:T(8,128)(2,1)}, bf16[1,96,768]{2,1,0:T(8,128)(2,1)}, u32[]{:S(2)}, u32[]{:S(2)}) collective-permute-start(bf16[1,96,768]{2,1,0:T(8,128)(2,1)} %add_convert_fusion.14), channel_id=1, source_target_pairs={{0,16},{16,0},{1,17},{17,1},{2,18},{18,2},{3,19},{19,3},{4,20},{20... | collective-permute-start | bytes 442376 | tf_op jit(solution)/shard_map/ppermute | solution.py:89
  300.5 18.2 %collective-permute-start.65 = (bf16[1,96,768]{2,1,0:T(8,128)(2,1)}, bf16[1,96,768]{2,1,0:T(8,128)(2,1)}, u32[]{:S(2)}, u32[]{:S(2)}) collective-permute-start(bf16[1,96,768]{2,1,0:T(8,128)(2,1)} %add_convert_fusion.13), channel_id=1, source_target_pairs={{0,16},{16,0},{1,17},{17,1},{2,18},{18,2},{3,19},{19,3},{4,20},{20... | collective-permute-start | bytes 442376 | tf_op jit(solution)/shard_map/ppermute | solution.py:89
  303.6 16.5 %collective-permute-start.71 = (bf16[1,96,768]{2,1,0:T(8,128)(2,1)}, bf16[1,96,768]{2,1,0:T(8,128)(2,1)}, u32[]{:S(2)}, u32[]{:S(2)}) collective-permute-start(bf16[1,96,768]{2,1,0:T(8,128)(2,1)} %add_convert_fusion.12), channel_id=1, source_target_pairs={{0,16},{16,0},{1,17},{17,1},{2,18},{18,2},{3,19},{19,3},{4,20},{20... | collective-permute-start | bytes 442376 | tf_op jit(solution)/shard_map/ppermute | solution.py:89
  (52 other events, 389.2 us)
